TPU v7x, 128 devices: a whole 4x4x4 slice. The times are simulated.
128 devices in a mesh: xy: 32 (over x, z, core), gz: 4 (over y).
Axes of the slice: x: 4, y: 4, z: 4, core: 2. Of those that a mesh axis runs over, the one named last changes fastest.
Arguments:
- concentration: float32 [2048, 32, 2048], P('xy', 'gz'), may hold values from -1 to 1
- psi_level: int32 [2048, 32, 2048], P('xy', 'gz'), may hold values from 0 to 4095
- tile_mask: int32 [16, 16], replicated, may hold values 0 or 1
Outputs:
- chem_potential: float32 [2048, 32, 2048], P('xy', 'gz')
- increment: float32 [2048, 32, 2048], P('xy', 'gz')
All inputs are finite; a program needn't handle non-finite values.
Results may differ from a plain program's by a relative error of at most 0.0012.
Values sent between devices are 32-bit elements; how exact they have to be, the bound alone decides.
No kernel may reach another device: no remote copies, remote signals or barrier semaphores. Data moves between devices by JAX's collectives and lax.ppermute only.
A program may use at most 128 MiB of HBM per device.

v0:
```python
import jax
import jax.numpy as jnp
from jax import lax
from jax.sharding import PartitionSpec as P

TILE = 128
LEVELS = 4096
STIFF = 4096


GRADIENT_COEF = 0.5
TIME_STEP = 32.0
PSI_FLOOR = 0.25


def extended(block, sides, width):
    for axis, dim in sides:
        count = lax.axis_size(axis)
        forward = [(i, i + 1) for i in range(count - 1)]
        backward = [(target, source) for source, target in forward]
        low = lax.ppermute(
            lax.slice_in_dim(block, block.shape[dim] - width, None, axis=dim), axis, forward
        )
        high = lax.ppermute(lax.slice_in_dim(block, 0, width, axis=dim), axis, backward)
        block = jnp.concatenate([low, block, high], axis=dim)
    return block


def neighbours(padded):
    return [
        padded[:-2, 1:-1, 1:-1],
        padded[2:, 1:-1, 1:-1],
        padded[1:-1, :-2, 1:-1],
        padded[1:-1, 2:, 1:-1],
        padded[1:-1, 1:-1, :-2],
        padded[1:-1, 1:-1, 2:],
    ]


def divergence(values, weights):
    centre_value = values[1:-1, 1:-1, 1:-1]
    centre_psi = weights[1:-1, 1:-1, 1:-1]
    total = jnp.zeros_like(centre_value)
    for near_value, near_psi in zip(neighbours(values), neighbours(weights)):
        both = centre_psi + near_psi
        weight = 2.0 * centre_psi * near_psi / jnp.where(both > 0.0, both, 1.0)
        total = total + weight * (near_value - centre_value)
    return total / jnp.where(centre_psi > 0.0, centre_psi, 1.0)


def pad_lines(field, width):
    return jnp.pad(field, ((0, 0), (0, 0), (width, width)))


def cosine_table(length):
    freq = jnp.arange(length, dtype=jnp.int32)[:, None]
    cells = jnp.arange(length, dtype=jnp.int32)[None, :]
    phase = (2 * cells + 1) * freq % (4 * length)
    table = jnp.cos(phase.astype(jnp.float32) * (jnp.pi / (2.0 * length))) * jnp.sqrt(2.0 / length)
    first = jnp.where(freq == 0, 1.0 / jnp.sqrt(2.0), 1.0)
    factor = 1.0 / (
        1.0
        + STIFF * (2.0 - 2.0 * jnp.cos(jnp.arange(length, dtype=jnp.float32) * (jnp.pi / length)))
    )
    return (table * first, factor)


def solve_columns(matrix):
    table, factor = cosine_table(matrix.shape[0])
    spectrum = jnp.dot(
        table, matrix, precision=lax.Precision.HIGHEST, preferred_element_type=jnp.float32
    )
    spectrum = spectrum * factor[:, None]
    return jnp.dot(
        table.T, spectrum, precision=lax.Precision.HIGHEST, preferred_element_type=jnp.float32
    )


def solve_rows(matrix):
    table, factor = cosine_table(matrix.shape[1])
    spectrum = jnp.dot(
        matrix, table.T, precision=lax.Precision.HIGHEST, preferred_element_type=jnp.float32
    )
    spectrum = spectrum * factor[None, :]
    return jnp.dot(
        spectrum, table, precision=lax.Precision.HIGHEST, preferred_element_type=jnp.float32
    )


def solve_y(field):
    brick_x, planes, width_y = field.shape
    return solve_rows(field.reshape(brick_x * planes, width_y)).reshape(brick_x, planes, width_y)


def solve_x_block(block):
    length_x, planes, line_rows = block.shape
    solved = solve_columns(block.reshape(length_x, planes * line_rows)).reshape(
        length_x, planes, line_rows
    )
    return lax.all_to_all(solved, "xy", split_axis=0, concat_axis=2, tiled=True)


def solve_x(field):
    return solve_x_block(lax.all_to_all(field, "xy", split_axis=2, concat_axis=0, tiled=True))


def per_device(concentration, psi_level, tile_mask):
    brick_x, planes, width_y = concentration.shape
    psi = PSI_FLOOR + (1.0 - PSI_FLOOR) * psi_level.astype(jnp.float32) / (LEVELS - 1)
    conc_ext, psi_ext = (
        extended(concentration, (("xy", 0), ("gz", 1)), 1),
        extended(psi, (("xy", 0), ("gz", 1)), 1),
    )
    conc_pad = pad_lines(conc_ext, 1)
    psi_pad = pad_lines(psi_ext, 1)
    potential = (
        concentration * concentration * concentration
        - concentration
        - GRADIENT_COEF * divergence(conc_pad, psi_pad)
    )
    pot_ext = extended(potential, (("xy", 0), ("gz", 1)), 1)
    pot_pad = pad_lines(pot_ext, 1)
    tiles_x = tile_mask.shape[0]
    global_x = lax.axis_index("xy") * brick_x + jnp.arange(brick_x, dtype=jnp.int32)
    selector = (global_x[:, None] // TILE == jnp.arange(tiles_x, dtype=jnp.int32)[None, :]).astype(
        jnp.float32
    )
    mask_rows = jnp.dot(selector, tile_mask.astype(jnp.float32), preferred_element_type=jnp.float32)
    active = jnp.broadcast_to(mask_rows[:, :, None], (brick_x, mask_rows.shape[1], TILE)).reshape(
        brick_x, width_y
    )
    right_side = active[:, None, :] * (TIME_STEP * divergence(pot_pad, psi_pad))
    increment = solve_x(solve_y(right_side))
    return (potential, increment)


def solution(mesh):
    placed = (P("xy", "gz", None), P("xy", "gz", None), P())
    return jax.shard_map(
        per_device,
        mesh=mesh,
        in_specs=placed,
        out_specs=(P("xy", "gz", None), P("xy", "gz", None)),
        check_vma=False,
    )
```

profile of v0, /device:TPU:25, one launch (start us, length us, event | category | flops | bytes accessed | tf_op | source)
XLA Modules:
  0.0 772.0 jit_solution(2414627250806028875)
XLA Ops:
  0.6 0.9 fusion.121
  1.5 4.1 collective-permute-start.1
  5.6 2.2 collective-permute-start.3
  7.8 2.7 multiply_add_fusion
  10.6 0.3 constant_dynamic-update-slice_fusion.1
  10.9 0.6 collective-permute-done.3
  11.5 1.1 copy-done.9
  12.6 0.7 fusion.118
  13.3 0.2 copy.61
  13.5 1.3 collective-permute-start.5
  14.8 0.2 copy.65
  15.0 4.0 collective-permute-start.7
  19.0 3.5 collective-permute-start
  22.5 1.9 collective-permute-start.2
  24.5 3.6 collective-permute-done.2
  28.1 4.0 pad_maximum_fusion.29
  32.3 1.3 collective-permute-start.4
  33.8 4.3 collective-permute-start.6
  38.1 0.6 copy.62
  38.7 0.6 copy.66
  39.3 8.7 %select_maximum_fusion.4 = f32[66,10,2050]{2,1,0:T(8,128)} fusion(f32[66,1,2048]{2,1,0:T(1,128)S(1)} %copy.66, f32[66,8,2048]{2,1,0:T(8,128)S(1)} %bitcast.38, f32[66,1,2048]{2,1,0:T(1,128)S(1)} %copy.62), kind=kLoop, calls=%fused_computation.24 | loop fusion | flops 10824000 | bytes 10818720 | tf_op jit(solution)/shard_map/concatenate | solution.py:25
  48.0 0.6 copy.60
  48.6 0.6 collective-permute-done.6
  49.2 0.6 copy.64
  49.8 10.1 %select_maximum_fusion.6 = f32[66,10,2050]{2,1,0:T(8,128)S(1)} fusion(f32[66,1,2048]{2,1,0:T(1,128)S(1)} %copy.64, f32[66,1,2048]{2,1,0:T(1,128)S(1)} %copy.60, f32[1,8,2048]{2,1,0:T(8,128)S(1)} %collective-permute-done.2, f32[64,8,2048]{2,1,0:T(8,128)S(1)} %copy-done.1, f32[1,8,2048]{2,1,0:T(8,128)S(1)} %collective-permute-done), kind=kLoop, calls=%fused_computation.26 | loop fusion | flops 16236000 | bytes 10818720 | tf_op jit(solution)/shard_map/concatenate | solution.py:25
  59.9 25.3 %fusion.17 = f32[64,8,2048]{2,1,0:T(8,128)} fusion(f32[64,8,2048]{2,1,0:T(8,128)} %param.3, f32[66,10,2050]{2,1,0:T(8,128)} %select_maximum_fusion.4, f32[66,1,2048]{2,1,0:T(1,128)} %copy-done.8, f32[66,8,2048]{2,1,0:T(8,128)} %copy-done.5, f32[66,1,2048]{2,1,0:T(1,128)} %copy-done.7, f32[1,8,2048]{2,1,0:T(8,128)} %copy-done.9, ...), kind=kLoop, calls=%fused_computation.36 | loop fusion | flops 71303168 | bytes 36110336 | tf_op jit(solution)/shard_map/sub | solution.py:117
  85.2 0.9 fusion.119
  86.1 3.6 collective-permute-start.8
  89.6 2.5 collective-permute-start.9
  92.2 3.0 collective-permute-done.9
  95.2 4.0 pad_maximum_fusion.26
  99.2 0.2 copy.71
  99.4 1.3 collective-permute-start.10
  100.7 1.0 copy.73
  101.7 5.6 collective-permute-start.11
  107.3 0.2 convolution_multiply_fusion
  107.6 0.2 broadcast_in_dim.44
  108.0 6.9 collective-permute-done.10
  115.0 1.6 copy.72
  116.6 1.3 collective-permute-done.11
  117.9 1.6 copy.74
  119.6 13.4 %select_maximum_fusion = f32[66,10,2050]{2,1,0:T(8,128)} fusion(f32[66,1,2048]{2,1,0:T(1,128)S(1)} %copy.74, f32[66,1,2048]{2,1,0:T(1,128)S(1)} %copy.72, f32[1,8,2048]{2,1,0:T(8,128)S(1)} %collective-permute-done.9, f32[64,8,2048]{2,1,0:T(8,128)} %fusion.17, f32[1,8,2048]{2,1,0:T(8,128)S(1)} %collective-permute-done.8), kind=kLoop, calls=%fused_computation.20 | loop fusion | flops 16236000 | bytes 10818720 | tf_op jit(solution)/shard_map/concatenate | solution.py:25
  133.0 21.5 %fusion.146 = f32[512,2048]{1,0:T(8,128)} fusion(f32[64,8,2048]{2,1,0:T(8,128)S(1)} %copy-done.4, f32[66,10,2050]{2,1,0:T(8,128)} %select_maximum_fusion, f32[66,1,2048]{2,1,0:T(1,128)S(1)} %copy.74, f32[1,8,2048]{2,1,0:T(8,128)S(1)} %collective-permute-done.9, f32[1,8,2048]{2,1,0:T(8,128)S(1)} %collective-permute-done.8, ...), kind=kLoop, calls=%fused_computation.48.clone.clone.2 | loop fusion | flops 71303168 | bytes 32309248 | tf_op jit(solution)/shard_map/dot_general | solution.py:81
  154.5 92.2 %fusion.15 = f32[512,2048]{1,0:T(8,128)S(1)} fusion(f32[2048]{0:T(1024)S(1)} %select_multiply_fusion, s32[2048]{0:T(1024)S(1)} %multiply_add_fusion.1, f32[512,2048]{1,0:T(8,128)} %fusion.146), kind=kOutput, calls=%fused_computation.34 | convolution fusion | flops 25832718336 | bytes 8404992 | tf_op jit(solution)/shard_map/dot_general | solution.py:81
  246.7 0.7 fusion.148
  247.4 88.9 %fusion.79 = f32[64,8,2048]{2,1,0:T(8,128)} fusion(f32[2048]{0:T(1024)S(1)} %select_multiply_fusion, s32[2048]{0:T(1024)S(1)} %multiply_add_fusion.1, f32[512,2048]{1,0:T(8,128)S(1)} %fusion.148), kind=kOutput, calls=%fused_computation.117 | convolution fusion | flops 25832718336 | bytes 8404992 | tf_op jit(solution)/shard_map/dot_general | solution.py:85
  336.3 7.7 copy.78
  344.0 9.8 %reshape.96 = f32[32,1,32768]{2,1,0:T(1,128)} reshape(f32[2048,8,64]{2,1,0:T(8,128)} %bitcast.34) | data formatting | bytes 8388608
  353.8 60.0 %all_to_all.33 = f32[32,1,32768]{2,1,0:T(1,128)} all-to-all(f32[32,1,32768]{2,1,0:T(1,128)} %reshape.96), channel_id=1, replica_groups=mesh['xy'=32,'gz'=4] {'xy'}, dimensions={0} | all-to-all | bytes 8388608 | tf_op jit(solution)/shard_map/all_to_all | solution.py:104
  413.8 0.6 broadcast.317
  414.4 13.8 %reduce = f32[32,32768]{1,0:T(8,128)} reduce(f32[32,1,32768]{2,1,0:T(1,128)} %all_to_all.33, f32[]{:T(128)} %broadcast.317), dimensions={1}, to_apply=%all_to_all.24.reduce_sub_computation | reduce | bytes 8388612 | tf_op jit(solution)/shard_map/all_to_all | solution.py:104
  428.2 7.4 reshape.97
  435.6 9.5 %copy.80 = f32[32,64,8,64]{3,2,1,0:T(8,128)} copy(f32[32,64,8,64]{1,2,3,0:T(8,128)} %bitcast.35) | data formatting | bytes 8388608 | tf_op jit(solution)/shard_map/all_to_all | solution.py:104
  445.1 7.5 reshape.94
  452.6 93.5 %fusion.11 = f32[2048,512]{1,0:T(8,128)S(1)} fusion(f32[2048,512]{1,0:T(8,128)} %reshape.94, f32[2048]{0:T(1024)S(1)} %select_multiply_fusion, s32[2048]{0:T(1024)S(1)} %multiply_add_fusion.1), kind=kOutput, calls=%fused_computation.32 | convolution fusion | flops 25832718336 | bytes 8404992 | tf_op jit(solution)/shard_map/dot_general | solution.py:70
  546.0 0.3 fusion.144
  546.4 112.8 %fusion.9 = f32[2048,512]{0,1:T(8,128)} fusion(f32[2048]{0:T(1024)S(1)} %select_multiply_fusion, s32[2048]{0:T(1024)S(1)} %multiply_add_fusion.1, f32[2048,512]{1,0:T(8,128)S(1)} %fusion.144), kind=kOutput, calls=%fused_computation.31 | convolution fusion | flops 25832718336 | bytes 8404992 | tf_op jit(solution)/shard_map/dot_general | solution.py:74
  659.2 7.0 copy.81
  666.2 9.8 %reshape.98 = f32[32,1,32768]{2,1,0:T(1,128)} reshape(f32[2048,8,64]{2,1,0:T(8,128)} %copy.81) | data formatting | bytes 8388608
  676.0 55.3 %all_to_all.34 = f32[32,1,32768]{2,1,0:T(1,128)} all-to-all(f32[32,1,32768]{2,1,0:T(1,128)} %reshape.98), channel_id=1, replica_groups=mesh['xy'=32,'gz'=4] {'xy'}, dimensions={0} | all-to-all | bytes 8388608 | tf_op jit(solution)/shard_map/all_to_all | solution.py:100
  731.3 13.8 %reduce.1 = f32[32,32768]{1,0:T(8,128)} reduce(f32[32,1,32768]{2,1,0:T(1,128)} %all_to_all.34, f32[]{:T(128)} %broadcast.317), dimensions={1}, to_apply=%all_to_all.27.reduce_sub_computation | reduce | bytes 8388612 | tf_op jit(solution)/shard_map/all_to_all | solution.py:100
  745.1 7.4 reshape.99
  752.5 11.5 %copy.82 = f32[64,8,32,64]{3,2,1,0:T(8,128)} copy(f32[64,8,32,64]{3,1,0,2:T(8,128)} %bitcast.36) | data formatting | bytes 8388608 | tf_op jit(solution)/shard_map/all_to_all | solution.py:100
  764.0 7.8 %all_to_all.30 = f32[64,8,2048]{2,1,0:T(8,128)} reshape(f32[64,8,32,64]{3,2,1,0:T(8,128)} %copy.82) | data formatting | bytes 8388608 | tf_op jit(solution)/shard_map/all_to_all | solution.py:100
  (43 shorter events, 0.8 us)
Async XLA Ops:
  1.5 9.1 %collective-permute-start.1 = (f32[1,8,2048]{2,1,0:T(8,128)S(1)}, f32[1,8,2048]{2,1,0:T(8,128)S(1)}, u32[]{:S(2)}, u32[]{:S(2)}) collective-permute-start(f32[1,8,2048]{2,1,0:T(8,128)S(1)} %get-tuple-element.15), channel_id=1, source_target_pairs={{0,4},{4,8},{8,12},{12,16},{16,20},{20,24},{24,28},{28,32},{32,36}... | collective-permute-start | bytes 196616 | tf_op jit(solution)/shard_map/ppermute | solution.py:21
  5.6 5.0 copy-start.6
  5.6 5.8 collective-permute-start.3
  10.6 8.4 %copy-start = (f32[64,8,2048]{2,1,0:T(8,128)}, f32[64,8,2048]{2,1,0:T(8,128)S(1)}, u32[]{:S(2)}) copy-start(f32[64,8,2048]{2,1,0:T(8,128)S(1)} %multiply_add_fusion) | copy-start | bytes 12582916
  11.5 1.1 copy-start.9
  12.6 6.5 copy-start.5
  13.5 24.6 %collective-permute-start.5 = (f32[66,1,2048]{2,0,1:T(8,128)S(1)}, f32[66,1,2048]{2,0,1:T(8,128)S(1)}, u32[]{:S(2)}, u32[]{:S(2)}) collective-permute-start(f32[66,1,2048]{2,0,1:T(8,128)S(1)} %copy.61), channel_id=1, source_target_pairs={{0,1},{1,2},{2,3},{4,5},{5,6},{6,7},{8,9},{9,10},{10,11},{12,13},{... | collective-permute-start | bytes 1622024 | tf_op jit(solution)/shard_map/ppermute | solution.py:21
  15.0 23.7 %collective-permute-start.7 = (f32[66,1,2048]{2,0,1:T(8,128)S(1)}, f32[66,1,2048]{2,0,1:T(8,128)S(1)}, u32[]{:S(2)}, u32[]{:S(2)}) collective-permute-start(f32[66,1,2048]{2,0,1:T(8,128)S(1)} %copy.65), channel_id=1, source_target_pairs={{1,0},{2,1},{3,2},{5,4},{6,5},{7,6},{9,8},{10,9},{11,10},{13,12},{... | collective-permute-start | bytes 1622024 | tf_op jit(solution)/shard_map/ppermute | solution.py:24
  19.0 5.4 collective-permute-start
  22.5 5.6 collective-permute-start.2
  24.5 14.8 %slice-start = ((s8[4325376]{0:T(1024)(128)(4,1)}), s8[131072]{0:T(1024)(128)(4,1)S(1)}, s32[]{:S(2)}) async-start(s8[4325376]{0:T(1024)(128)(4,1)} %bitcast.37), calls=%async_computation.2 | async-start | bytes 262144
  24.5 14.8 %slice-start.1 = ((s8[4325376]{0:T(1024)(128)(4,1)}), s8[4194304]{0:T(1024)(128)(4,1)S(1)}, s32[]{:S(2)}) async-start(s8[4325376]{0:T(1024)(128)(4,1)} %bitcast.37), calls=%async_computation.3 | async-start | bytes 8388608
  32.3 15.7 %collective-permute-start.4 = (f32[66,1,2048]{2,0,1:T(8,128)S(1)}, f32[66,1,2048]{2,0,1:T(8,128)S(1)}, u32[]{:S(2)}, u32[]{:S(2)}) collective-permute-start(f32[66,1,2048]{2,0,1:T(8,128)S(1)} %copy.59), channel_id=1, source_target_pairs={{0,1},{1,2},{2,3},{4,5},{5,6},{6,7},{8,9},{9,10},{10,11},{12,13},{... | collective-permute-start | bytes 1622024 | tf_op jit(solution)/shard_map/ppermute | solution.py:21
  33.8 15.4 %collective-permute-start.6 = (f32[66,1,2048]{2,0,1:T(8,128)S(1)}, f32[66,1,2048]{2,0,1:T(8,128)S(1)}, u32[]{:S(2)}, u32[]{:S(2)}) collective-permute-start(f32[66,1,2048]{2,0,1:T(8,128)S(1)} %copy.63), channel_id=1, source_target_pairs={{1,0},{2,1},{3,2},{5,4},{6,5},{7,6},{9,8},{10,9},{11,10},{13,12},{... | collective-permute-start | bytes 1622024 | tf_op jit(solution)/shard_map/ppermute | solution.py:24
  38.7 9.4 %copy-start.7 = (f32[66,1,2048]{2,1,0:T(1,128)}, f32[66,1,2048]{2,1,0:T(1,128)S(1)}, u32[]{:S(2)}) copy-start(f32[66,1,2048]{2,1,0:T(1,128)S(1)} %copy.62) | copy-start | bytes 1622020
  39.3 8.7 %copy-start.8 = (f32[66,1,2048]{2,1,0:T(1,128)}, f32[66,1,2048]{2,1,0:T(1,128)S(1)}, u32[]{:S(2)}) copy-start(f32[66,1,2048]{2,1,0:T(1,128)S(1)} %copy.66) | copy-start | bytes 1622020
  39.3 10.5 %copy-start.1 = (f32[64,8,2048]{2,1,0:T(8,128)S(1)}, f32[64,8,2048]{2,1,0:T(8,128)}, u32[]{:S(2)}) copy-start(f32[64,8,2048]{2,1,0:T(8,128)} %copy-done) | copy-start | bytes 12582916
  59.9 25.3 %copy-start.3 = (f32[66,10,2050]{2,1,0:T(8,128)}, f32[66,10,2050]{2,1,0:T(8,128)S(1)}, u32[]{:S(2)}) copy-start(f32[66,10,2050]{2,1,0:T(8,128)S(1)} %select_maximum_fusion.6) | copy-start | bytes 16236004
  85.2 22.1 %copy-start.10 = (s32[16,16]{1,0:T(8,128)S(1)}, s32[16,16]{1,0:T(8,128)}, u32[]{:S(2)}) copy-start(s32[16,16]{1,0:T(8,128)} %param.5) | copy-start | bytes 3076
  86.1 6.1 collective-permute-start.8
  89.6 5.6 collective-permute-start.9
  99.4 15.6 %collective-permute-start.10 = (f32[66,1,2048]{2,0,1:T(8,128)S(1)}, f32[66,1,2048]{2,0,1:T(8,128)}, u32[]{:S(2)}, u32[]{:S(2)}) collective-permute-start(f32[66,1,2048]{2,0,1:T(8,128)S(1)} %copy.71), channel_id=1, source_target_pairs={{0,1},{1,2},{2,3},{4,5},{5,6},{6,7},{8,9},{9,10},{10,11},{12,13},{... | collective-permute-start | bytes 1622024 | tf_op jit(solution)/shard_map/ppermute | solution.py:21
  101.7 16.2 %collective-permute-start.11 = (f32[66,1,2048]{2,0,1:T(8,128)}, f32[66,1,2048]{2,0,1:T(8,128)}, u32[]{:S(2)}, u32[]{:S(2)}) collective-permute-start(f32[66,1,2048]{2,0,1:T(8,128)} %copy.73), channel_id=1, source_target_pairs={{1,0},{2,1},{3,2},{5,4},{6,5},{7,6},{9,8},{10,9},{11,10},{13,12},{... | collective-permute-start | bytes 1622024 | tf_op jit(solution)/shard_map/ppermute | solution.py:24
  119.5 13.4 %copy-start.2 = (f32[64,8,2048]{2,1,0:T(8,128)S(1)}, f32[64,8,2048]{2,1,0:T(8,128)}, u32[]{:S(2)}) copy-start(f32[64,8,2048]{2,1,0:T(8,128)} %copy-done) | copy-start | bytes 12582916
  119.5 13.4 %copy-start.4 = (f32[64,8,2048]{2,1,0:T(8,128)S(1)}, f32[64,8,2048]{2,1,0:T(8,128)}, u32[]{:S(2)}) copy-start(f32[64,8,2048]{2,1,0:T(8,128)} %fusion.17) | copy-start | bytes 12582916
where the time goes:
time: 782 us; the launch traced here: 772 us
  matrix products  388 us (50%)
  other arithmetic  118 us (15%)
  blocking collectives  115 us (15%)
  local copies, waits for them, and re-layouts  97.7 us (12%)
  starting transfers between devices  35.5 us (5%)
  waiting for transfers between devices  16.1 us (2%)
    dot_general x1, matrix products, solve_columns(): jnp.dot(table.T, spectrum, precision=lax.Precision.HIGHEST, preferred_ele...  113 us
    dot_general x1, matrix products, solve_columns(): jnp.dot(table, matrix, precision=lax.Precision.HIGHEST, preferred_element...  93.5 us
    dot_general x1, matrix products, solve_rows(): jnp.dot(matrix, table.T, precision=lax.Precision.HIGHEST, preferred_eleme...  92.2 us
    dot_general x1, matrix products, solve_rows(): jnp.dot(spectrum, table, precision=lax.Precision.HIGHEST, preferred_eleme...  88.9 us
    all_to_all x1, blocking collectives, solve_x(): lax.all_to_all(field, 'xy', split_axis=2, concat_axis=0, tiled=True)  60 us
    all_to_all x1, blocking collectives, solve_x_block(): return lax.all_to_all(solved, 'xy', split_axis=0, concat_axis=2, tiled=True)  55.3 us
    unnamed x33, local copies, waits for them, and re-layouts  36 us
    concatenate x3, other arithmetic, extended(): block = jnp.concatenate([low, block, high], axis=dim)  32.2 us
  transfers between devices with their start and end apart: 12, of which 6 were waited for; matrix products, arithmetic and copies ran while one was open for 3% of the time, Pallas kernels for 0%

commit v1 on v0

v1 whole, which is shorter than its diff:
```python
import functools
import math

import jax
import jax.numpy as jnp
import numpy as np
from jax import lax
from jax.experimental import pallas as pl
from jax.experimental.pallas import tpu as pltpu
from jax.sharding import PartitionSpec as P

TILE = 128
LEVELS = 4096
STIFF = 4096
GRADIENT_COEF = 0.5
TIME_STEP = 32.0
PSI_FLOOR = 0.25

X = 64
Z = 8
Y = 2048
YT = 16
LANES = 128
ROW = YT * Z
ROWS = X * ROW
FACE = X * YT
LINE = 2048
NB = 256
F32 = jnp.float32
BF16 = jnp.bfloat16

_half = 1.0 + 0.5 / STIFF
THETA = math.log(_half + math.sqrt(_half * _half - 1.0))
RHO = math.exp(-THETA)
GAIN = (RHO / STIFF) / (1.0 - RHO * RHO)


def rho(power):
    return math.exp(-THETA * power)


def vmem(limit_mib):
    return pltpu.CompilerParams(vmem_limit_bytes=limit_mib * 2**20)


def half_over_psi(level):
    return 0.5 / (PSI_FLOOR + level.astype(F32) * ((1.0 - PSI_FLOOR) / (LEVELS - 1)))


def recip(value):
    return 1.0 / value


def lane_iota(shape):
    return lax.broadcasted_iota(jnp.int32, shape, len(shape) - 1)


def sub_iota(shape):
    return lax.broadcasted_iota(jnp.int32, shape, len(shape) - 2)


def next_y(v):
    axis = v.ndim - 1
    turned = pltpu.roll(v, LANES - 1, axis)
    if TILES_LEAD[v.shape[-2]]:
        following = jnp.concatenate([turned[1:], turned[:1]], axis=0)
    else:
        following = pltpu.roll(turned, YT - 1, axis - 1)
    return jnp.where(lane_iota(v.shape) == LANES - 1, following, turned)


def prev_y(v):
    axis = v.ndim - 1
    turned = pltpu.roll(v, 1, axis)
    if TILES_LEAD[v.shape[-2]]:
        previous = jnp.concatenate([turned[-1:], turned[:-1]], axis=0)
    else:
        previous = pltpu.roll(turned, 1, axis - 1)
    return jnp.where(lane_iota(v.shape) == 0, previous, turned)


TILES_LEAD = {Z: True, YT: False}


def next_z(v):
    return pltpu.roll(v, Z - 1, 1)


def prev_z(v):
    return pltpu.roll(v, 1, 1)


PRE_X = 16


def faces_kernel(c_ref, l_ref, zlo_ref, zhi_ref, in_ref, xlo_ref, xhi_ref):
    step = pl.program_id(0)

    def plane(ref, z):
        return ref[pl.ds(z, PRE_X * YT, stride=Z), :]

    for out, edge, inner, spot in ((zlo_ref, 0, 1, 0), (zhi_ref, 7, 6, 1)):
        c_edge, c_inner = plane(c_ref, edge), plane(c_ref, inner)
        h_edge = half_over_psi(plane(l_ref, edge))
        h_inner = half_over_psi(plane(l_ref, inner))
        out[0] = c_edge
        out[1] = h_edge
        out[2] = recip(h_edge + h_inner) * (c_inner - c_edge)
        in_ref[spot] = h_inner

    @pl.when(step == 0)
    def _():
        xlo_ref[0] = c_ref[0:2 * ROW, :]
        xlo_ref[1] = half_over_psi(l_ref[0:2 * ROW, :])

    @pl.when(step == X // PRE_X - 1)
    def _():
        last = (PRE_X - 2) * ROW
        xhi_ref[0] = c_ref[last:last + 2 * ROW, :]
        xhi_ref[1] = half_over_psi(l_ref[last:last + 2 * ROW, :])


def make_faces(c, level):
    block = pl.BlockSpec((PRE_X * ROW, LANES), lambda i: (i, 0))
    face = pl.BlockSpec((3, PRE_X * YT, LANES), lambda i: (0, i, 0))
    inner = pl.BlockSpec((2, PRE_X * YT, LANES), lambda i: (0, i, 0))
    whole = pl.BlockSpec((2, 2 * ROW, LANES), lambda i: (0, 0, 0))
    return pl.pallas_call(
        faces_kernel,
        grid=(X // PRE_X,),
        in_specs=[block, block],
        out_specs=[face, face, inner, whole, whole],
        out_shape=[
            jax.ShapeDtypeStruct((3, FACE, LANES), F32),
            jax.ShapeDtypeStruct((3, FACE, LANES), F32),
            jax.ShapeDtypeStruct((2, FACE, LANES), F32),
            jax.ShapeDtypeStruct((2, 2 * ROW, LANES), F32),
            jax.ShapeDtypeStruct((2, 2 * ROW, LANES), F32),
        ],
        compiler_params=vmem(40),
        cost_estimate=pl.CostEstimate(flops=10**6, bytes_accessed=13 * 2**20, transcendentals=0),
        name="faces",
    )(c, level)


def y_tables():
    idx = np.arange(NB)
    table = GAIN * np.exp(-THETA * np.abs(idx[:, None] - idx[None, :]))
    high = table.astype(jnp.bfloat16)
    low = (table - high.astype(np.float64)).astype(jnp.bfloat16)
    fwd = np.exp(-THETA * (idx + 1.0))
    bwd = np.exp(-THETA * (NB - idx.astype(np.float64)))
    edge = np.zeros((8, LANES), np.float32)
    edge[0], edge[1] = fwd[:LANES], fwd[LANES:]
    edge[2], edge[3] = bwd[:LANES], bwd[LANES:]
    return high, low, edge


def split(v):
    high = v.astype(BF16)
    return high, (v - high.astype(F32)).astype(BF16)


def dot3(a, b):
    (a_high, a_low), (b_high, b_low) = a, b
    mm = functools.partial(jnp.dot, preferred_element_type=F32)
    return mm(a_high, b_high) + (mm(a_low, b_high) + mm(a_high, b_low))


def ends(first, last, length):
    scale = 1.0 / (1.0 - rho(2 * length))
    tail = rho(length)
    return (first + tail * last) * scale, (last + tail * first) * scale


def y_carry(tiles, edge):
    count = YT // 2
    heads = [tiles[2 * b][:, 0:1] for b in range(count)]
    tails = [tiles[2 * b + 1][:, LANES - 1:LANES] for b in range(count)]
    hop = rho(NB)
    right = [jnp.zeros_like(heads[0])]
    for b in range(count - 1):
        right.append(hop * right[-1] + tails[b])
    left = [jnp.zeros_like(heads[0])]
    for b in range(count - 1, 0, -1):
        left.append(hop * left[-1] + heads[b])
    left = left[::-1]
    from_low, from_high = ends(heads[0] + hop * left[0], tails[-1] + hop * right[-1], Y)
    out = []
    for b in range(count):
        carry_r = right[b] + rho(NB * b) * from_low
        carry_l = left[b] + rho(NB * (count - 1 - b)) * from_high
        for k in range(2):
            out.append(tiles[2 * b + k] + carry_r * edge[k:k + 1, :] + carry_l * edge[2 + k:3 + k, :])
    return out


CHUNK = 8
NCHUNK = X // CHUNK
MROWS = 16


def block_kernel(flag_ref, c_hbm, l_hbm, xlo_ref, xhi_ref, act_ref, thigh_ref, tlow_ref, edge_ref,
                 pot_hbm, v_hbm, mom_ref, edgepot_ref,
                 c_s, l_s, pot_s, f_s, u_s, st, in_sem, pot_sem, v_sem):
    def copies_in(i):
        at = pl.ds(i * CHUNK, CHUNK)
        return (pltpu.make_async_copy(c_hbm.at[at], c_s.at[at], in_sem.at[0, i]),
                pltpu.make_async_copy(l_hbm.at[at], l_s.at[at], in_sem.at[1, i]))

    for i in range(NCHUNK):
        for copy in copies_in(i):
            copy.start()

    shape = (YT, Z, LANES)
    open_z = lax.broadcasted_iota(jnp.int32, shape, 1) < Z - 1
    open_y = jnp.logical_or(
        lax.broadcasted_iota(jnp.int32, shape, 2) < LANES - 1,
        lax.broadcasted_iota(jnp.int32, shape, 0) < YT - 1,
    )
    C1, H1, A1, FX2, WZ1, WY1, WX2, POT2, H2, B2, GX3, PF = range(12)

    def advance(c, h, open_x, emit):
        h1, c1 = st[H1], st[C1]
        wx1 = recip(h1 + h) * open_x
        fx1 = wx1 * (c - c1)
        wz = jnp.where(open_z, recip(h + next_z(h)), 0.0)
        wy = jnp.where(open_y, recip(h + next_y(h)), 0.0)
        fz = wz * (next_z(c) - c)
        fy = wy * (next_y(c) - c)
        across = (fz - prev_z(fz)) + (fy - prev_y(fy))
        pot1 = c1 * (c1 * c1 - 1.0) - h1 * (st[A1] + fx1 - st[FX2])
        gx2 = st[WX2] * (pot1 - st[POT2])
        gz = st[WZ1] * (next_z(pot1) - pot1)
        gy = st[WY1] * (next_y(pot1) - pot1)
        across2 = (gz - prev_z(gz)) + (gy - prev_y(gy))
        if emit is not None:
            rhs = act_ref[...] * (st[H2] * (st[B2] + gx2 - st[GX3]))
            forward = RHO * st[PF] + rhs
            st[PF] = forward
            f_s[emit] = rhs
            u_s[emit] = forward
            pot_s[prow(emit), :] = st[POT2].reshape(ROW, LANES)
        st[A1] = across
        st[FX2] = fx1
        st[WZ1] = wz
        st[WY1] = wy
        st[WX2] = wx1
        st[POT2] = pot1
        st[H2] = h1
        st[B2] = across2
        st[GX3] = gx2
        st[C1] = c
        st[H1] = h

    def prow(x):
        return pl.ds(pl.multiple_of(x * ROW, ROW), ROW)

    for k in range(12):
        st[k] = jnp.zeros(shape, F32)
    open_lo, open_hi = flag_ref[0], flag_ref[1]
    ones = jnp.ones(shape, F32)
    st[H1] = ones
    advance(xlo_ref[0, 0], jnp.where(open_lo > 0.0, xlo_ref[1, 0], ones), 0.0, None)
    advance(xlo_ref[0, 1], jnp.where(open_lo > 0.0, xlo_ref[1, 1], ones), open_lo, None)

    def main(x, emit):
        advance(c_s[x], half_over_psi(l_s[x]), jnp.where(x == 0, open_lo, 1.0), emit)

    for copy in copies_in(0):
        copy.wait()
    main(0, None)
    main(1, None)

    def rows_loop(first, last):
        def body(x, _):
            main(x, x - 2)
            return 0
        lax.fori_loop(first, last, body, 0)

    def pot_copy(i):
        at = pl.ds(i * CHUNK * ROW, CHUNK * ROW)
        return pltpu.make_async_copy(pot_s.at[at], pot_hbm.at[at], pot_sem.at[i])

    rows_loop(2, CHUNK)
    for i in range(1, NCHUNK):
        for copy in copies_in(i):
            copy.wait()
        rows_loop(i * CHUNK, (i + 1) * CHUNK)
        pot_copy(i - 1).start()
    advance(xhi_ref[0, 0], jnp.where(open_hi > 0.0, xhi_ref[1, 0], ones), open_hi, X - 2)
    advance(xhi_ref[0, 1], jnp.where(open_hi > 0.0, xhi_ref[1, 1], ones), open_hi, X - 1)
    pot_copy(NCHUNK - 1).start()

    def back(k, carry):
        x = X - 1 - k
        f = f_s[x]
        u_s[x] = GAIN * (u_s[x] + carry)
        return RHO * (carry + f)

    lax.fori_loop(0, X, back, jnp.zeros(shape, F32))
    mom_ref[0] = u_s[X - 1]
    mom_ref[1] = u_s[0]
    for side, z in ((0, 0), (1, 7)):
        edgepot_ref[side] = pot_s[pl.ds(z, FACE, stride=Z), :]

    def blocks(i, _):
        xs = pl.ds(i * MROWS, MROWS)
        table = (thigh_ref[...], tlow_ref[...])
        for b in range(YT // 2):
            pair = [u_s[xs, 2 * b + k].reshape(MROWS * Z, LANES) for k in range(2)]
            solved = dot3(split(jnp.concatenate(pair, axis=1)), table)
            for k in range(2):
                f_s[xs, 2 * b + k] = solved[:, k * LANES:(k + 1) * LANES].reshape(MROWS, Z, LANES)
        return 0

    lax.fori_loop(0, X // MROWS, blocks, 0)
    edge = edge_ref[...]

    def v_copy(i):
        at = pl.ds(i * CHUNK, CHUNK)
        return pltpu.make_async_copy(u_s.at[at], v_hbm.at[at], v_sem.at[i])

    for i in range(NCHUNK):
        def body(x, _):
            for t, part in enumerate(y_carry([f_s[x, t] for t in range(YT)], edge)):
                u_s[x, t] = part
            return 0
        lax.fori_loop(i * CHUNK, (i + 1) * CHUNK, body, 0)
        v_copy(i).start()
    for i in range(NCHUNK):
        pot_copy(i).wait()
        v_copy(i).wait()


def solve_block(flags, c, level, xlo, xhi, act, tables):
    any_spec = pl.BlockSpec(memory_space=pl.ANY)
    vm = pl.BlockSpec(memory_space=pltpu.VMEM)
    block = (X, YT, Z, LANES)
    return pl.pallas_call(
        block_kernel,
        in_specs=[pl.BlockSpec(memory_space=pltpu.SMEM), any_spec, any_spec] + [vm] * 6,
        out_specs=[any_spec, any_spec, vm, vm],
        out_shape=[
            jax.ShapeDtypeStruct((ROWS, LANES), F32),
            jax.ShapeDtypeStruct(block, F32),
            jax.ShapeDtypeStruct((2, YT, Z, LANES), F32),
            jax.ShapeDtypeStruct((2, FACE, LANES), F32),
        ],
        scratch_shapes=[
            pltpu.VMEM(block, F32),
            pltpu.VMEM(block, jnp.int32),
            pltpu.VMEM((ROWS, LANES), F32),
            pltpu.VMEM(block, F32),
            pltpu.VMEM(block, F32),
            pltpu.VMEM((12, YT, Z, LANES), F32),
            pltpu.SemaphoreType.DMA((2, NCHUNK)),
            pltpu.SemaphoreType.DMA((NCHUNK,)),
            pltpu.SemaphoreType.DMA((NCHUNK,)),
        ],
        compiler_params=vmem(44),
        cost_estimate=pl.CostEstimate(flops=4 * 10**9, bytes_accessed=60 * 2**20, transcendentals=0),
        name="block",
    )(flags, c.reshape(block), level.reshape(block), xlo, xhi, act, *tables)


EXT = X + 2
GROUP = 8


def seam_kernel(flag_ref, pow_ref, own_lo_ref, own_hi_ref, inner_ref, got_lo_ref, got_hi_ref, xlo_ref, xhi_ref,
                corner_lo_ref, corner_hi_ref, edgepot_ref, mom_ref, act_ref,
                df_ref, dpot_ref, send_ref, c0_s, h0_s, cm_s, hm_s, fl_s, dp_s, acc_s):
    open_x = (flag_ref[0], flag_ref[1])
    act = act_ref[:, 0, :]
    shape = (GROUP, YT, LANES)
    open_y = jnp.logical_or(
        lax.broadcasted_iota(jnp.int32, shape, 2) < LANES - 1,
        lax.broadcasted_iota(jnp.int32, shape, 1) < YT - 1,
    )
    row = lax.broadcasted_iota(jnp.int32, shape, 0)
    acc_s[...] = jnp.zeros_like(acc_s)

    for side, (own, got, corner, z) in enumerate(
        ((own_lo_ref, got_lo_ref, corner_lo_ref, 0), (own_hi_ref, got_hi_ref, corner_hi_ref, 7))
    ):
        open_z = flag_ref[2 + side]
        main = slice(1, 1 + X)
        c0_s[main] = own[0]
        h0_s[main] = own[1]
        cm_s[main] = got[0]
        hm_s[main] = jnp.where(open_z > 0.0, got[1], 1.0)
        for spot, ref, r, k in ((0, xlo_ref, 1, 0), (EXT - 1, xhi_ref, 0, 1)):
            inside = open_x[k] > 0.0
            both = open_x[k] * open_z > 0.0
            c0_s[spot] = ref[0, r, :, z, :]
            h0_s[spot] = jnp.where(inside, ref[1, r, :, z, :], 1.0)
            cm_s[spot] = corner[2 * k]
            hm_s[spot] = jnp.where(both, corner[2 * k + 1], 1.0)

        def first(i, _):
            at = pl.ds(i * 6, 6)
            h0 = h0_s[at]
            flux = recip(h0 + hm_s[at]) * open_z * (cm_s[at] - c0_s[at])
            fl_s[at] = flux
            dp_s[at] = -h0 * flux
            return 0

        lax.fori_loop(0, EXT // 6, first, 0)

        def second(i, _):
            at = pl.ds(i * GROUP, GROUP)
            ext = pl.ds(i * GROUP + 1, GROUP)
            after = pl.ds(i * GROUP + 2, GROUP)
            lo_gate = jnp.where(row == 0, jnp.where(i == 0, open_x[0], 1.0), 1.0)
            hi_gate = jnp.where(row == GROUP - 1, jnp.where(i == X // GROUP - 1, open_x[1], 1.0), 1.0)

            def plane(h_ref, v_ref):
                h, v = h_ref[ext], v_ref[ext]
                wy = jnp.where(open_y, recip(h + next_y(h)), 0.0)
                fy = wy * (next_y(v) - v)
                total = recip(h + h_ref[at]) * lo_gate * (v_ref[at] - v)
                total = total + recip(h + h_ref[after]) * hi_gate * (v_ref[after] - v)
                return h, v, total + (fy - prev_y(fy))

            hm, cm, across_m = plane(hm_s, cm_s)
            h0, dp, across_0 = plane(h0_s, dp_s)
            flux = fl_s[ext]
            potm = cm * (cm * cm - 1.0) - hm * (across_m + got[2, at] - flux)
            pot0 = edgepot_ref[side, at] + dp
            h1 = inner_ref[side, at]
            toward = recip(h0 + h1) * dp
            join = recip(h0 + hm) * open_z * (potm - pot0)
            df0 = act * (h0 * (across_0 - toward + join))
            df1 = act * (h1 * toward)
            outer, inner = (0, 1) if side == 0 else (3, 2)
            df_ref[outer, at] = df0
            df_ref[inner, at] = df1
            dpot_ref[side, at] = dp
            for spot, value in ((outer, df0), (inner, df1)):
                last, start = acc_s[spot], acc_s[4 + spot]
                for r in range(GROUP):
                    x = i * GROUP + r
                    last = last + pow_ref[1, X - 1 - x] * value[r]
                    start = start + pow_ref[1, x] * value[r]
                acc_s[spot] = last
                acc_s[4 + spot] = start
            return 0

        lax.fori_loop(0, X // GROUP, second, 0)

    sub = sub_iota((Z, LANES))
    half = sub < 4
    for t in range(YT):
        totals = []
        for which in range(2):
            total = mom_ref[which, t]
            for k, z in enumerate((0, 1, 6, 7)):
                line = jnp.broadcast_to(acc_s[4 * which + k, t:t + 1, :], (Z, LANES))
                total = total + jnp.where(sub == z, line, 0.0)
            totals.append(total)
        last, start = totals
        send_ref[2 * t] = jnp.where(half, last, pltpu.roll(start, 4, 0))
        send_ref[2 * t + 1] = jnp.where(half, pltpu.roll(last, 4, 0), start)


def add_seams(flags, powers, own_lo, own_hi, inner, got_lo, got_hi, xlo, xhi, corner_lo, corner_hi, edgepot, mom, act):
    vm = pl.BlockSpec(memory_space=pltpu.VMEM)
    sm = pl.BlockSpec(memory_space=pltpu.SMEM)
    lines = [a.reshape(a.shape[0], X, YT, LANES) for a in (own_lo, own_hi, inner, got_lo, got_hi)]
    return pl.pallas_call(
        seam_kernel,
        in_specs=[sm, sm] + [vm] * 12,
        out_specs=[vm, vm, vm],
        out_shape=[
            jax.ShapeDtypeStruct((4, X, YT, LANES), F32),
            jax.ShapeDtypeStruct((2, X, YT, LANES), F32),
            jax.ShapeDtypeStruct((32, Z, LANES), F32),
        ],
        scratch_shapes=[pltpu.VMEM((EXT, YT, LANES), F32)] * 6 + [pltpu.VMEM((8, YT, LANES), F32)],
        compiler_params=vmem(40),
        cost_estimate=pl.CostEstimate(flops=10**7, bytes_accessed=12 * 2**20, transcendentals=0),
        name="seams",
    )(flags, powers, *lines, xlo, xhi, corner_lo, corner_hi, edgepot.reshape(2, X, YT, LANES), mom, act)


def planes_kernel(df_ref, thigh_ref, tlow_ref, edge_ref, out_ref, p_s, u_s, w_s):
    shape = (4, YT, LANES)

    def forth(x, carry):
        carry = RHO * carry + df_ref[:, x]
        p_s[:, x] = carry
        return carry

    lax.fori_loop(0, X, forth, jnp.zeros(shape, F32), unroll=4)

    def back(k, carry):
        x = X - 1 - k
        solved = GAIN * (p_s[:, x] + carry)
        at = pl.ds(pl.multiple_of(x * YT, YT), YT)
        for z in range(4):
            u_s[z, at, :] = solved[z]
        return RHO * (carry + df_ref[:, x])

    lax.fori_loop(0, X, back, jnp.zeros(shape, F32), unroll=4)

    table = (thigh_ref[...], tlow_ref[...])
    edge = edge_ref[...]
    for z in range(4):
        for b in range(YT // 2):
            pair = [u_s[z, pl.ds(2 * b + k, X, stride=YT), :] for k in range(2)]
            solved = dot3(split(jnp.concatenate(pair, axis=1)), table)
            for k in range(2):
                w_s[z, 2 * b + k] = solved[:, k * LANES:(k + 1) * LANES]

    for z in range(4):
        def body(i, _):
            at = pl.ds(pl.multiple_of(i * 8, 8), 8)
            parts = y_carry([w_s[z, t, at, :] for t in range(YT)], edge)
            for t, part in enumerate(parts):
                out_ref[z, pl.ds(i * 8 * YT + t, 8, stride=YT), :] = part
            return 0
        lax.fori_loop(0, X // 8, body, 0)


def solve_planes(df, tables):
    vm = pl.BlockSpec(memory_space=pltpu.VMEM)
    return pl.pallas_call(
        planes_kernel,
        in_specs=[vm] * 4,
        out_specs=vm,
        out_shape=jax.ShapeDtypeStruct((4, FACE, LANES), F32),
        scratch_shapes=[
            pltpu.VMEM((4, X, YT, LANES), F32),
            pltpu.VMEM((4, FACE, LANES), F32),
            pltpu.VMEM((4, YT, X, LANES), F32),
        ],
        compiler_params=vmem(40),
        cost_estimate=pl.CostEstimate(flops=2 * 10**9, bytes_accessed=10 * 2**20, transcendentals=0),
        name="planes",
    )(df, *tables)


def mend_kernel(pot_ref, dpot_ref, out_ref):
    out_ref[...] = pot_ref[...]
    for side, z in ((0, 0), (1, 7)):
        at = pl.ds(z, PRE_X * YT, stride=Z)
        out_ref[at, :] = pot_ref[at, :] + dpot_ref[side]


def mend_potential(pot, dpot):
    block = pl.BlockSpec((PRE_X * ROW, LANES), lambda i: (i, 0))
    return pl.pallas_call(
        mend_kernel,
        grid=(X // PRE_X,),
        in_specs=[block, pl.BlockSpec((2, PRE_X * YT, LANES), lambda i: (0, i, 0))],
        out_specs=block,
        out_shape=jax.ShapeDtypeStruct((ROWS, LANES), F32),
        compiler_params=vmem(40),
        cost_estimate=pl.CostEstimate(flops=10**6, bytes_accessed=9 * 2**20, transcendentals=0),
        name="mend",
    )(pot, dpot.reshape(2, FACE, LANES))


def carries_kernel(count, in_ref, out_ref):
    got = [in_ref[d] for d in range(count)]
    half = sub_iota((8, TILE)) < 4
    hop = rho(X)
    right = [jnp.zeros((8, TILE), F32)]
    for d in range(count - 1):
        right.append(hop * right[-1] + got[d])
    starts = [pltpu.roll(g, 4, 0) for g in got]
    left = [jnp.zeros((8, TILE), F32)]
    for d in range(count - 1, 0, -1):
        left.append(hop * left[-1] + starts[d])
    left = left[::-1]
    from_low, from_high = ends(starts[0] + hop * left[0], got[-1] + hop * right[-1], X * count)
    for d in range(count):
        carry_r = right[d] + rho(X * d) * from_low
        carry_l = left[d] + rho(X * (count - 1 - d)) * from_high
        out_ref[d] = jnp.where(half, carry_r, pltpu.roll(carry_l, 4, 0))


def scan_carries(got):
    vm = pl.BlockSpec(memory_space=pltpu.VMEM)
    return pl.pallas_call(
        functools.partial(carries_kernel, got.shape[0]),
        in_specs=[vm],
        out_specs=vm,
        out_shape=jax.ShapeDtypeStruct(got.shape, F32),
        cost_estimate=pl.CostEstimate(flops=10**6, bytes_accessed=2**18, transcendentals=0),
        name="carries",
    )(got)


FIN = 8


def final_kernel(pow_ref, got_ref, thigh_ref, tlow_ref, edge_ref, v_ref, dv_ref, out_ref, lr_s):
    step = pl.program_id(0)

    @pl.when(step == 0)
    def _():
        half = sub_iota((Z, LANES)) < 4
        edge = edge_ref[...]
        raw = []
        for t in range(YT):
            even, odd = got_ref[2 * t], got_ref[2 * t + 1]
            raw.append(jnp.concatenate([
                jnp.where(half, even, pltpu.roll(odd, 4, 0)),
                jnp.where(half, pltpu.roll(even, 4, 0), odd),
            ], axis=0))
        local = []
        for b in range(YT // 2):
            solved = dot3(split(jnp.concatenate(raw[2 * b:2 * b + 2], axis=1)), (thigh_ref[...], tlow_ref[...]))
            local += [solved[:, :LANES], solved[:, LANES:]]
        for side in range(2):
            tiles = [part[8 * side:8 * side + 8, :] for part in local]
            for t, part in enumerate(y_carry(tiles, edge)):
                lr_s[side, t * Z:(t + 1) * Z, :] = part

    for r in range(FIN):
        at = slice(r * ROW, (r + 1) * ROW)
        x = step * FIN + r
        out_ref[at, :] = v_ref[at, :] + pow_ref[0, x] * lr_s[0] + pow_ref[0, X - 1 - x] * lr_s[1]
    for k, z in enumerate((0, 1, 6, 7)):
        at = pl.ds(z, FIN * YT, stride=Z)
        out_ref[at, :] = out_ref[at, :] + dv_ref[k]


def finish(powers, got, tables, v, dv):
    def whole(a):
        return pl.BlockSpec(a.shape, lambda i: (0,) * a.ndim)

    block = pl.BlockSpec((FIN * ROW, LANES), lambda i: (i, 0))
    return pl.pallas_call(
        final_kernel,
        grid=(X // FIN,),
        in_specs=[pl.BlockSpec(memory_space=pltpu.SMEM), whole(got)] + [whole(t) for t in tables]
        + [block, pl.BlockSpec((4, FIN * YT, LANES), lambda i: (0, i, 0))],
        out_specs=block,
        out_shape=jax.ShapeDtypeStruct((ROWS, LANES), F32),
        scratch_shapes=[pltpu.VMEM((2, ROW, LANES), F32)],
        compiler_params=vmem(40),
        cost_estimate=pl.CostEstimate(flops=10**7, bytes_accessed=10 * 2**20, transcendentals=0),
        name="finish",
    )(powers, got, *tables, v, dv)


def shift(value, axis, forward):
    count = lax.axis_size(axis)
    pairs = [(i, i + 1) for i in range(count - 1)]
    if not forward:
        pairs = [(b, a) for a, b in pairs]
    return lax.ppermute(value, axis, pairs)


def to_tiles(block):
    return block.reshape(X, Z, YT, LANES).transpose(0, 2, 1, 3).reshape(ROWS, LANES)


def from_tiles(rows):
    return rows.reshape(X, YT, Z, LANES).transpose(0, 2, 1, 3).reshape(X, Z, Y)


def per_device(concentration, psi_level, tile_mask):
    c, level = to_tiles(concentration), to_tiles(psi_level)
    xy, gz = lax.axis_index("xy"), lax.axis_index("gz")
    n_xy, n_gz = lax.axis_size("xy"), lax.axis_size("gz")
    flags = jnp.stack([xy > 0, xy < n_xy - 1, gz > 0, gz < n_gz - 1]).astype(F32)
    mask_row = lax.dynamic_index_in_dim(tile_mask, xy * X // TILE, 0, keepdims=False)
    act = jnp.broadcast_to((mask_row.astype(F32) * (2.0 * TIME_STEP))[:, None, None], (YT, Z, LANES))
    tables = tuple(jnp.asarray(t) for t in y_tables())
    steps = np.exp(-THETA * np.arange(X + 1))
    powers = jnp.asarray(np.stack([steps[1:], GAIN * steps[:-1]]).astype(np.float32))

    zlo, zhi, inner, xlo, xhi = make_faces(c, level)
    pair = (2, 2, YT, Z, LANES)
    got_xlo = shift(xhi, "xy", True).reshape(pair)
    got_xhi = shift(xlo, "xy", False).reshape(pair)
    got_zlo = shift(zhi, "gz", True)
    got_zhi = shift(zlo, "gz", False)

    def corners(z):
        return jnp.stack([got_xlo[0, 1, :, z], got_xlo[1, 1, :, z], got_xhi[0, 0, :, z], got_xhi[1, 0, :, z]])

    corner_lo = shift(corners(7), "gz", True)
    corner_hi = shift(corners(0), "gz", False)

    pot, v, mom, edgepot = solve_block(flags, c, level, got_xlo, got_xhi, act, tables)
    df, dpot, send = add_seams(
        flags, powers, zlo, zhi, inner, got_zlo, got_zhi, got_xlo, got_xhi, corner_lo, corner_hi, edgepot, mom, act,
    )
    got = lax.all_to_all(send, "xy", split_axis=0, concat_axis=0, tiled=True)
    dv = solve_planes(df, tables)
    potential = mend_potential(pot, dpot)
    back = lax.all_to_all(scan_carries(got), "xy", split_axis=0, concat_axis=0, tiled=True)
    increment = finish(powers, back, tables, v.reshape(ROWS, LANES), dv)
    return from_tiles(potential), from_tiles(increment)


def solution(mesh):
    placed = (P("xy", "gz", None), P("xy", "gz", None), P())
    return jax.shard_map(
        per_device,
        mesh=mesh,
        in_specs=placed,
        out_specs=(P("xy", "gz", None), P("xy", "gz", None)),
        check_vma=False,
    )
```

time: 782 us -> 129 us (0.16); the launches traced: 772 us -> 127 us
  matrix products: 388 us -> 0 us
  other arithmetic: 118 us -> 0.79 us
  blocking collectives: 115 us -> 0 us
  local copies, waits for them, and re-layouts: 97.7 us -> 19.5 us
  Pallas kernels: 0 us -> 67.8 us
  waiting for transfers between devices: 16.1 us -> 7.18 us
    dot_general x5 -> x0, matrix products: 388 us -> none  [the longest x1 113 us: solve_columns(): jnp.dot(table.T, spectrum, precision=lax.Precision.HIGHEST, preferred_ele...]
    all_to_all x2 -> x0, blocking collectives: 115 us -> none  [the longest x1 60 us: solve_x(): lax.all_to_all(field, 'xy', split_axis=2, concat_axis=0, tiled=True)]
    pallas_call x0 -> x7, Pallas kernels: none -> 67.8 us  [the longest x1 37.2 us: solve_block(): pl.pallas_call(block_kernel, in_specs=[pl.BlockSpec(memory_space=pltpu.SM...]
    concatenate x3 -> x0, other arithmetic: 32.2 us -> none  [extended(): block = jnp.concatenate([low, block, high], axis=dim)]
    all_to_all x4 -> x0, local copies, waits for them, and re-layouts: 29.3 us -> none  [the longest x2 19.3 us: solve_x_block(): return lax.all_to_all(solved, 'xy', split_axis=0, concat_axis=2, tiled=True)]
    all_to_all x2 -> x0, other arithmetic: 27.6 us -> none  [the longest x1 13.8 us: solve_x_block(): return lax.all_to_all(solved, 'xy', split_axis=0, concat_axis=2, tiled=True)]
    sub x1 -> x0, other arithmetic: 25.3 us -> none  [per_device(): concentration * concentration * concentration - concentration]
    dot_general x3 -> x0, other arithmetic: 22.6 us -> none  [the longest x1 21.5 us: solve_rows(): jnp.dot(matrix, table.T, precision=lax.Precision.HIGHEST, preferred_eleme...]
  transfers between devices with their start and end apart: 12 -> 8, of which waited for: 6 -> 3; matrix products, arithmetic and copies ran while one was open for 3% -> 1% of each run, Pallas kernels for 0% -> 40%
where the time goes in v1:
time: 129 us; the launch traced here: 127 us
  Pallas kernels  67.8 us (53%)
  starting transfers between devices  30.8 us (24%)
  local copies, waits for them, and re-layouts  19.5 us (15%)
  waiting for transfers between devices  7.18 us (6%)
    pallas_call x1, Pallas kernels, solve_block(): pl.pallas_call(block_kernel, in_specs=[pl.BlockSpec(memory_space=pltpu.SM...  37.2 us
    unnamed x34, local copies, waits for them, and re-layouts  18.4 us
    ppermute x6, starting transfers between devices, shift(): return lax.ppermute(value, axis, pairs)  17.3 us
    pallas_call x1, Pallas kernels, solve_planes(): pl.pallas_call(planes_kernel, in_specs=[vm] * 4, out_specs=vm, out_shape=...  11 us
    all_to_all x1, starting transfers between devices, per_device(): got = lax.all_to_all(send, 'xy', split_axis=0, concat_axis=0, tiled=True)  7.78 us
    pallas_call x1, Pallas kernels, add_seams(): pl.pallas_call(seam_kernel, in_specs=[sm, sm] + [vm] * 12, out_specs=[vm,...  7.55 us
    all_to_all x1, starting transfers between devices, per_device(): lax.all_to_all(scan_carries(got), 'xy', split_axis=0, concat_axis=0, tile...  5.76 us
    ppermute x6, waiting for transfers between devices, shift(): return lax.ppermute(value, axis, pairs)  5.55 us
  transfers between devices with their start and end apart: 8, of which 3 were waited for; matrix products, arithmetic and copies ran while one was open for 1% of the time, Pallas kernels for 40%

profile of v1, /device:TPU:25, one launch (start us, length us, event | category | flops | bytes accessed | tf_op | source)
XLA Modules:
  0.0 127.0 jit_solution(3430922487359120729)
XLA Ops:
  0.6 0.0 copy-start
  0.6 2.2 %copy-done = f32[64,8,2048]{2,1,0:T(8,128)S(1)} copy-done((f32[64,8,2048]{2,1,0:T(8,128)S(1)}, f32[64,8,2048]{2,1,0:T(8,128)}, u32[]{:S(2)}) %copy-start) | copy-done | bytes 4194328
  2.8 0.0 copy-start.1
  2.8 2.2 %copy-done.1 = s32[64,8,2048]{2,1,0:T(8,128)S(1)} copy-done((s32[64,8,2048]{2,1,0:T(8,128)S(1)}, s32[64,8,2048]{2,1,0:T(8,128)}, u32[]{:S(2)}) %copy-start.1) | copy-done | bytes 4194328
  5.0 0.0 copy-start.9
  5.0 0.0 copy-start.12
  5.0 2.3 %faces.1 = (f32[3,1024,128]{2,1,0:T(8,128)S(1)}, f32[3,1024,128]{2,1,0:T(8,128)S(1)}, f32[2,1024,128]{2,1,0:T(8,128)S(1)}, f32[2,256,128]{2,1,0:T(8,128)}, f32[2,256,128]{2,1,0:T(8,128)}) custom-call(f32[8192,128]{1,0:T(8,128)S(1)} %bitcast.61, s32[8192,128]{1,0:T(8,128)S(1)} %bitcast.63), custom_call_target="tpu_custom_call" | custom-call | flops 1000000 | bytes 13631488 | tf_op jit(solution)/shard_map/faces/pallas_call | solution.py:128
  7.3 0.0 copy-start.5
  7.3 1.0 copy-done.5
  8.2 3.5 %collective-permute-start.3 = (f32[3,1024,128]{2,1,0:T(8,128)S(1)}, f32[3,1024,128]{2,1,0:T(8,128)}, u32[]{:S(2)}, u32[]{:S(2)}) collective-permute-start(f32[3,1024,128]{2,1,0:T(8,128)S(1)} %get-tuple-element.17), channel_id=1, source_target_pairs={{1,0},{2,1},{3,2},{5,4},{6,5},{7,6},{9,8},{10,9},{11,10},{13,12},{... | collective-permute-start | bytes 4718600 | tf_op jit(solution)/shard_map/ppermute | solution.py:655
  11.8 1.3 %collective-permute-start.2 = (f32[3,1024,128]{2,1,0:T(8,128)S(1)}, f32[3,1024,128]{2,1,0:T(8,128)}, u32[]{:S(2)}, u32[]{:S(2)}) collective-permute-start(f32[3,1024,128]{2,1,0:T(8,128)S(1)} %get-tuple-element.18), channel_id=1, source_target_pairs={{0,1},{1,2},{2,3},{4,5},{5,6},{6,7},{8,9},{9,10},{10,11},{12,13},{... | collective-permute-start | bytes 4718600 | tf_op jit(solution)/shard_map/ppermute | solution.py:655
  13.0 4.4 %collective-permute-start = (f32[2,256,128]{2,1,0:T(8,128)}, f32[2,256,128]{2,1,0:T(8,128)S(1)}, u32[]{:S(2)}, u32[]{:S(2)}) collective-permute-start(f32[2,256,128]{2,1,0:T(8,128)} %get-tuple-element.14), channel_id=1, source_target_pairs={{0,4},{4,8},{8,12},{12,16},{16,20},{20,24},{24,28},{28,32},{32,36}... | collective-permute-start | bytes 786440 | tf_op jit(solution)/shard_map/ppermute | solution.py:655
  17.4 1.9 %collective-permute-start.1 = (f32[2,256,128]{2,1,0:T(8,128)}, f32[2,256,128]{2,1,0:T(8,128)}, u32[]{:S(2)}, u32[]{:S(2)}) collective-permute-start(f32[2,256,128]{2,1,0:T(8,128)} %get-tuple-element.15), channel_id=1, source_target_pairs={{4,0},{8,4},{12,8},{16,12},{20,16},{24,20},{28,24},{32,28},{36,32}... | collective-permute-start | bytes 786440 | tf_op jit(solution)/shard_map/ppermute | solution.py:655
  19.4 0.7 multiply_bitcast_fusion
  20.1 0.1 add_convert_fusion.flag_ref
  20.2 0.9 collective-permute-done
  21.1 4.7 %collective-permute-done.1 = f32[2,256,128]{2,1,0:T(8,128)} collective-permute-done((f32[2,256,128]{2,1,0:T(8,128)}, f32[2,256,128]{2,1,0:T(8,128)}, u32[]{:S(2)}, u32[]{:S(2)}) %collective-permute-start.1) | collective-permute-done | bytes 262176 | tf_op jit(solution)/shard_map/ppermute | solution.py:655
  25.7 1.0 fusion.1
  26.7 1.3 %collective-permute-start.4 = (f32[4,16,128]{2,1,0:T(8,128)S(1)}, f32[4,16,128]{2,1,0:T(8,128)S(1)}, u32[]{:S(2)}, u32[]{:S(2)}) collective-permute-start(f32[4,16,128]{2,1,0:T(8,128)S(1)} %pad_maximum_fusion), channel_id=1, source_target_pairs={{0,1},{1,2},{2,3},{4,5},{5,6},{6,7},{8,9},{9,10},{10,11},{12,13},{... | collective-permute-start | bytes 98312 | tf_op jit(solution)/shard_map/ppermute | solution.py:655
  28.0 4.9 %collective-permute-start.5 = (f32[4,16,128]{2,1,0:T(8,128)S(1)}, f32[4,16,128]{2,1,0:T(8,128)S(1)}, u32[]{:S(2)}, u32[]{:S(2)}) collective-permute-start(f32[4,16,128]{2,1,0:T(8,128)S(1)} %pad_maximum_fusion.1), channel_id=1, source_target_pairs={{1,0},{2,1},{3,2},{5,4},{6,5},{7,6},{9,8},{10,9},{11,10},{13,12},{... | collective-permute-start | bytes 98312 | tf_op jit(solution)/shard_map/ppermute | solution.py:655
  32.9 0.1 broadcast_in_dim.2.act_ref
  33.0 0.0 copy-done.9
  33.0 0.0 copy-done.12
  33.0 0.0 copy-start.10
  33.0 0.9 copy-done.10
  33.9 0.0 copy-start.6
  33.9 0.0 copy-start.13
  33.9 37.2 %block.1 = (f32[8192,128]{1,0:T(8,128)S(1)}, f32[64,16,8,128]{3,2,1,0:T(8,128)}, f32[2,16,8,128]{3,2,1,0:T(8,128)S(1)}, f32[2,1024,128]{2,1,0:T(8,128)S(1)}) custom-call(f32[4]{0:T(128)S(1)} %add_convert_fusion.flag_ref, f32[64,16,8,128]{3,2,1,0:T(8,128)} %bitcast.60, s32[64,16,8,128]{3,2,1,0:T(8,128)} %bitcast.62, f32[2,2,16,8,128]{4,3,2,1,0:T(8,128)S(1)} %bitcast.71, ...), custom_call_target="tpu_custom_call" | custom-call | flops 4000000000 | bytes 62914560 | tf_op jit(solution)/shard_map/block/pallas_call | solution.py:340
  71.2 0.0 copy-start.3
  71.2 2.0 %copy-done.3 = f32[8192,128]{1,0:T(8,128)} copy-done((f32[8192,128]{1,0:T(8,128)}, f32[8192,128]{1,0:T(8,128)S(1)}, u32[]{:S(2)}) %copy-start.3) | copy-done | bytes 4194328
  73.2 0.0 collective-permute-done.4.corner_lo_ref
  73.2 0.0 collective-permute-done.5.corner_hi_ref
  73.2 0.0 collective-permute-done.3
  73.2 0.0 collective-permute-done.2
  73.2 0.0 copy-done.6
  73.2 0.0 copy-done.13
  73.2 7.6 %seams.1 = (f32[4,64,16,128]{3,2,1,0:T(8,128)S(1)}, f32[2,64,16,128]{3,2,1,0:T(8,128)S(1)}, f32[32,8,128]{2,1,0:T(8,128)}) custom-call(f32[4]{0:T(128)S(1)} %add_convert_fusion.flag_ref, f32[2,64]{1,0:T(2,128)S(1)} %copy-done.13, f32[3,64,16,128]{3,2,1,0:T(8,128)S(1)} %bitcast.65, f32[3,64,16,128]{3,2,1,0:T(8,128)S(1)} %bitcast.66, ...), custom_call_target="tpu_custom_call" | custom-call | flops 10000000 | bytes 12582912 | tf_op jit(solution)/shard_map/seams/pallas_call | solution.py:471
  80.8 0.0 copy-start.7
  80.8 1.0 copy-done.7
  81.8 0.0 copy-start.14
  81.8 1.3 %copy-done.14 = f32[4,64,16,128]{3,2,1,0:T(8,128)} copy-done((f32[4,64,16,128]{3,2,1,0:T(8,128)}, f32[4,64,16,128]{3,2,1,0:T(8,128)S(1)}, u32[]{:S(2)}) %copy-start.14) | copy-done | bytes 2097176
  83.1 7.8 %all-to-all-start = ((f32[32,8,128]{2,1,0:T(8,128)}), f32[32,8,128]{2,1,0:T(8,128)S(1)}, u32[]{:S(2)}, u32[]{:S(2)}) async-start(f32[32,8,128]{2,1,0:T(8,128)} %get-tuple-element.23), calls=%async_computation | async-start | bytes 262144 | tf_op jit(solution)/shard_map/all_to_all | solution.py:694
  90.9 0.0 copy-start.4
  90.9 2.2 %copy-done.4 = f32[8192,128]{1,0:T(8,128)S(1)} copy-done((f32[8192,128]{1,0:T(8,128)S(1)}, f32[8192,128]{1,0:T(8,128)}, u32[]{:S(2)}) %copy-start.4) | copy-done | bytes 4194328
  93.1 0.0 copy-start.8
  93.1 1.2 copy-done.8
  94.3 0.0 copy-start.11
  94.3 2.7 %mend.1 = f32[8192,128]{1,0:T(8,128)} custom-call(f32[8192,128]{1,0:T(8,128)S(1)} %copy-done.4, f32[2,1024,128]{2,1,0:T(8,128)S(1)} %bitcast.69), custom_call_target="tpu_custom_call" | custom-call | flops 1000000 | bytes 9437184 | tf_op jit(solution)/shard_map/mend/pallas_call | solution.py:553
  97.0 1.6 %all-to-all-done.in_ref = f32[32,8,128]{2,1,0:T(8,128)S(1)} async-done(((f32[32,8,128]{2,1,0:T(8,128)}), f32[32,8,128]{2,1,0:T(8,128)S(1)}, u32[]{:S(2)}, u32[]{:S(2)}) %all-to-all-start) | async-done | bytes 131104 | tf_op jit(solution)/shard_map/all_to_all | solution.py:694
  98.6 0.0 copy-start.16
  98.6 0.7 copy-done.16
  99.3 1.6 %carries.1 = f32[32,8,128]{2,1,0:T(8,128)} custom-call(f32[32,8,128]{2,1,0:T(8,128)} %copy-done.16), custom_call_target="tpu_custom_call" | custom-call | flops 1000000 | bytes 262144 | tf_op jit(solution)/shard_map/carries/pallas_call | solution.py:586
  100.9 5.8 %all-to-all-start.1 = ((f32[32,8,128]{2,1,0:T(8,128)}), f32[32,8,128]{2,1,0:T(8,128)S(1)}, u32[]{:S(2)}, u32[]{:S(2)}) async-start(f32[32,8,128]{2,1,0:T(8,128)} %carries.1), calls=%async_computation.1 | async-start | bytes 262144 | tf_op jit(solution)/shard_map/all_to_all | solution.py:697
  106.7 0.0 copy-done.11
  106.7 0.0 copy-start.15
  106.7 1.6 %copy-done.15 = f32[4,64,16,128]{3,2,1,0:T(8,128)S(1)} copy-done((f32[4,64,16,128]{3,2,1,0:T(8,128)S(1)}, f32[4,64,16,128]{3,2,1,0:T(8,128)}, u32[]{:S(2)}) %copy-start.15) | copy-done | bytes 2097176
  108.3 11.0 %planes.1.dv_ref = f32[4,1024,128]{2,1,0:T(8,128)S(1)} custom-call(f32[4,64,16,128]{3,2,1,0:T(8,128)S(1)} %copy-done.15, bf16[256,256]{1,0:T(8,128)(2,1)S(1)} %copy-done.11, bf16[256,256]{1,0:T(8,128)(2,1)S(1)} %copy-done.9, f32[8,128]{1,0:T(8,128)S(1)} %copy-done.12), custom_call_target="tpu_custom_call" | custom-call | flops 2000000000 | bytes 10485760 | tf_op jit(solution)/shard_map/planes/pallas_call | solution.py:528
  119.3 0.0 all-to-all-done.1.got_ref
  119.3 0.0 copy-start.2
  119.3 2.2 %copy-done.2 = f32[64,16,8,128]{3,2,1,0:T(8,128)S(1)} copy-done((f32[64,16,8,128]{3,2,1,0:T(8,128)S(1)}, f32[64,16,8,128]{3,2,1,0:T(8,128)}, u32[]{:S(2)}) %copy-start.2) | copy-done | bytes 4194328
  121.5 5.5 %finish.1 = f32[8192,128]{1,0:T(8,128)} custom-call(f32[2,64]{1,0:T(2,128)S(1)} %copy-done.13, f32[32,8,128]{2,1,0:T(8,128)S(1)} %all-to-all-done.1.got_ref, bf16[256,256]{1,0:T(8,128)(2,1)S(1)} %copy-done.11, bf16[256,256]{1,0:T(8,128)(2,1)S(1)} %copy-done.9, f32[8,128]{1,0:T(8,128)S(1)} %copy-done.12, f32[8192,128]{1,0:T(8,128)S(1)} %bitcast.64, ...), custom_call_target="tpu_custom_call" | custom-call | flops 10000000 | bytes 10485760 | tf_op jit(solution)/shard_map/finish/pallas_call | solution.py:636
  (3 shorter events, 0.0 us)
Async XLA Ops:
  0.6 2.2 %copy-start = (f32[64,8,2048]{2,1,0:T(8,128)S(1)}, f32[64,8,2048]{2,1,0:T(8,128)}, u32[]{:S(2)}) copy-start(f32[64,8,2048]{2,1,0:T(8,128)} %param.7) | copy-start | bytes 12582916
  2.8 2.2 %copy-start.1 = (s32[64,8,2048]{2,1,0:T(8,128)S(1)}, s32[64,8,2048]{2,1,0:T(8,128)}, u32[]{:S(2)}) copy-start(s32[64,8,2048]{2,1,0:T(8,128)} %param.8) | copy-start | bytes 12582916
  5.0 28.0 %copy-start.9 = (bf16[256,256]{1,0:T(8,128)(2,1)S(1)}, bf16[256,256]{1,0:T(8,128)(2,1)}, u32[]{:S(2)}) copy-start(bf16[256,256]{1,0:T(8,128)(2,1)} %constant.48.clone.tlow_ref) | copy-start | bytes 393220
  5.0 28.0 %copy-start.12 = (f32[8,128]{1,0:T(8,128)S(1)}, f32[8,128]{1,0:T(8,128)}, u32[]{:S(2)}) copy-start(f32[8,128]{1,0:T(8,128)} %constant.49.clone.edge_ref) | copy-start | bytes 12292
  7.3 1.0 copy-start.5
  8.2 64.9 %collective-permute-start.3 = (f32[3,1024,128]{2,1,0:T(8,128)S(1)}, f32[3,1024,128]{2,1,0:T(8,128)}, u32[]{:S(2)}, u32[]{:S(2)}) collective-permute-start(f32[3,1024,128]{2,1,0:T(8,128)S(1)} %get-tuple-element.17), channel_id=1, source_target_pairs={{1,0},{2,1},{3,2},{5,4},{6,5},{7,6},{9,8},{10,9},{11,10},{13,12},{... | collective-permute-start | bytes 4718600 | tf_op jit(solution)/shard_map/ppermute | solution.py:655
  11.8 61.4 %collective-permute-start.2 = (f32[3,1024,128]{2,1,0:T(8,128)S(1)}, f32[3,1024,128]{2,1,0:T(8,128)}, u32[]{:S(2)}, u32[]{:S(2)}) collective-permute-start(f32[3,1024,128]{2,1,0:T(8,128)S(1)} %get-tuple-element.18), channel_id=1, source_target_pairs={{0,1},{1,2},{2,3},{4,5},{5,6},{6,7},{8,9},{9,10},{10,11},{12,13},{... | collective-permute-start | bytes 4718600 | tf_op jit(solution)/shard_map/ppermute | solution.py:655
  13.0 8.0 %collective-permute-start = (f32[2,256,128]{2,1,0:T(8,128)}, f32[2,256,128]{2,1,0:T(8,128)S(1)}, u32[]{:S(2)}, u32[]{:S(2)}) collective-permute-start(f32[2,256,128]{2,1,0:T(8,128)} %get-tuple-element.14), channel_id=1, source_target_pairs={{0,4},{4,8},{8,12},{12,16},{16,20},{20,24},{24,28},{28,32},{32,36}... | collective-permute-start | bytes 786440 | tf_op jit(solution)/shard_map/ppermute | solution.py:655
  17.4 8.3 %collective-permute-start.1 = (f32[2,256,128]{2,1,0:T(8,128)}, f32[2,256,128]{2,1,0:T(8,128)}, u32[]{:S(2)}, u32[]{:S(2)}) collective-permute-start(f32[2,256,128]{2,1,0:T(8,128)} %get-tuple-element.15), channel_id=1, source_target_pairs={{4,0},{8,4},{12,8},{16,12},{20,16},{24,20},{28,24},{32,28},{36,32}... | collective-permute-start | bytes 786440 | tf_op jit(solution)/shard_map/ppermute | solution.py:655
  26.7 46.5 %collective-permute-start.4 = (f32[4,16,128]{2,1,0:T(8,128)S(1)}, f32[4,16,128]{2,1,0:T(8,128)S(1)}, u32[]{:S(2)}, u32[]{:S(2)}) collective-permute-start(f32[4,16,128]{2,1,0:T(8,128)S(1)} %pad_maximum_fusion), channel_id=1, source_target_pairs={{0,1},{1,2},{2,3},{4,5},{5,6},{6,7},{8,9},{9,10},{10,11},{12,13},{... | collective-permute-start | bytes 98312 | tf_op jit(solution)/shard_map/ppermute | solution.py:655
  28.0 45.2 %collective-permute-start.5 = (f32[4,16,128]{2,1,0:T(8,128)S(1)}, f32[4,16,128]{2,1,0:T(8,128)S(1)}, u32[]{:S(2)}, u32[]{:S(2)}) collective-permute-start(f32[4,16,128]{2,1,0:T(8,128)S(1)} %pad_maximum_fusion.1), channel_id=1, source_target_pairs={{1,0},{2,1},{3,2},{5,4},{6,5},{7,6},{9,8},{10,9},{11,10},{13,12},{... | collective-permute-start | bytes 98312 | tf_op jit(solution)/shard_map/ppermute | solution.py:655
  33.0 0.9 copy-start.10
  33.9 39.3 %copy-start.6 = (f32[2,1024,128]{2,1,0:T(8,128)S(1)}, f32[2,1024,128]{2,1,0:T(8,128)}, u32[]{:S(2)}) copy-start(f32[2,1024,128]{2,1,0:T(8,128)} %copy-done.5) | copy-start | bytes 3145732
  33.9 39.3 %copy-start.13 = (f32[2,64]{1,0:T(2,128)S(1)}, f32[2,64]{1,0:T(2,128)}, u32[]{:S(2)}) copy-start(f32[2,64]{1,0:T(2,128)} %constant.50.clone.pow_ref) | copy-start | bytes 1540
  71.2 2.0 %copy-start.3 = (f32[8192,128]{1,0:T(8,128)}, f32[8192,128]{1,0:T(8,128)S(1)}, u32[]{:S(2)}) copy-start(f32[8192,128]{1,0:T(8,128)S(1)} %get-tuple-element.16.pot_ref) | copy-start | bytes 12582916
  80.8 1.0 copy-start.7
  81.8 1.3 %copy-start.14 = (f32[4,64,16,128]{3,2,1,0:T(8,128)}, f32[4,64,16,128]{3,2,1,0:T(8,128)S(1)}, u32[]{:S(2)}) copy-start(f32[4,64,16,128]{3,2,1,0:T(8,128)S(1)} %get-tuple-element.25.df_ref) | copy-start | bytes 6291460
  83.1 15.5 %all-to-all-start = ((f32[32,8,128]{2,1,0:T(8,128)}), f32[32,8,128]{2,1,0:T(8,128)S(1)}, u32[]{:S(2)}, u32[]{:S(2)}) async-start(f32[32,8,128]{2,1,0:T(8,128)} %get-tuple-element.23), calls=%async_computation | async-start | bytes 262144 | tf_op jit(solution)/shard_map/all_to_all | solution.py:694
  90.9 2.2 %copy-start.4 = (f32[8192,128]{1,0:T(8,128)S(1)}, f32[8192,128]{1,0:T(8,128)}, u32[]{:S(2)}) copy-start(f32[8192,128]{1,0:T(8,128)} %copy-done.3) | copy-start | bytes 12582916
  93.1 1.2 copy-start.8
  94.3 12.3 %copy-start.11 = (bf16[256,256]{1,0:T(8,128)(2,1)S(1)}, bf16[256,256]{1,0:T(8,128)(2,1)}, u32[]{:S(2)}) copy-start(bf16[256,256]{1,0:T(8,128)(2,1)} %constant.47.clone.thigh_ref) | copy-start | bytes 393220
  98.6 0.7 copy-start.16
  100.9 18.4 %all-to-all-start.1 = ((f32[32,8,128]{2,1,0:T(8,128)}), f32[32,8,128]{2,1,0:T(8,128)S(1)}, u32[]{:S(2)}, u32[]{:S(2)}) async-start(f32[32,8,128]{2,1,0:T(8,128)} %carries.1), calls=%async_computation.1 | async-start | bytes 262144 | tf_op jit(solution)/shard_map/all_to_all | solution.py:697
  106.7 1.6 %copy-start.15 = (f32[4,64,16,128]{3,2,1,0:T(8,128)S(1)}, f32[4,64,16,128]{3,2,1,0:T(8,128)}, u32[]{:S(2)}) copy-start(f32[4,64,16,128]{3,2,1,0:T(8,128)} %copy-done.14) | copy-start | bytes 6291460
  119.3 2.2 %copy-start.2 = (f32[64,16,8,128]{3,2,1,0:T(8,128)S(1)}, f32[64,16,8,128]{3,2,1,0:T(8,128)}, u32[]{:S(2)}) copy-start(f32[64,16,8,128]{3,2,1,0:T(8,128)} %get-tuple-element.24) | copy-start | bytes 12582916

commit v2 on v1

v2 whole, which is shorter than its diff:
```python
import functools
import math

import jax
import jax.numpy as jnp
import numpy as np
from jax import lax
from jax.experimental import pallas as pl
from jax.experimental.pallas import tpu as pltpu
from jax.sharding import PartitionSpec as P

TILE = 128
LEVELS = 4096
STIFF = 4096
GRADIENT_COEF = 0.5
TIME_STEP = 32.0
PSI_FLOOR = 0.25

X = 64
Z = 8
Y = 2048
YT = 16
LANES = 128
ROW = YT * Z
ROWS = X * ROW
FACE = X * YT
LINE = 2048
NB = 256
F32 = jnp.float32
BF16 = jnp.bfloat16

_half = 1.0 + 0.5 / STIFF
THETA = math.log(_half + math.sqrt(_half * _half - 1.0))
RHO = math.exp(-THETA)
GAIN = (RHO / STIFF) / (1.0 - RHO * RHO)


def rho(power):
    return math.exp(-THETA * power)


def vmem(limit_mib):
    return pltpu.CompilerParams(vmem_limit_bytes=limit_mib * 2**20)


def half_over_psi(level):
    return recip(2.0 * PSI_FLOOR + level.astype(F32) * (2.0 * (1.0 - PSI_FLOOR) / (LEVELS - 1)))


def recip(value):
    return pl.reciprocal(value, approx=True)


def lane_iota(shape):
    return lax.broadcasted_iota(jnp.int32, shape, len(shape) - 1)


def sub_iota(shape):
    return lax.broadcasted_iota(jnp.int32, shape, len(shape) - 2)


def next_y(v):
    axis = v.ndim - 1
    turned = pltpu.roll(v, LANES - 1, axis)
    if TILES_LEAD[v.shape[-2]]:
        following = jnp.concatenate([turned[1:], turned[:1]], axis=0)
    else:
        following = pltpu.roll(turned, YT - 1, axis - 1)
    return jnp.where(lane_iota(v.shape) == LANES - 1, following, turned)


def prev_y(v):
    axis = v.ndim - 1
    turned = pltpu.roll(v, 1, axis)
    if TILES_LEAD[v.shape[-2]]:
        previous = jnp.concatenate([turned[-1:], turned[:-1]], axis=0)
    else:
        previous = pltpu.roll(turned, 1, axis - 1)
    return jnp.where(lane_iota(v.shape) == 0, previous, turned)


TILES_LEAD = {Z: True, YT: False}


def next_z(v):
    return pltpu.roll(v, Z - 1, 1)


def prev_z(v):
    return pltpu.roll(v, 1, 1)


CHUNK = 8
NCHUNK = X // CHUNK
PART = CHUNK * YT


def faces_kernel(c_hbm, l_hbm, zlo_hbm, zhi_hbm, in_hbm, xlo_ref, xhi_ref, c_s, l_s, z_s, i_s, in_sem, out_sem):
    def arrivals(i):
        at = pl.ds(i * CHUNK * ROW, CHUNK * ROW)
        return (pltpu.make_async_copy(c_hbm.at[at], c_s.at[at], in_sem.at[0, i]),
                pltpu.make_async_copy(l_hbm.at[at], l_s.at[at], in_sem.at[1, i]))

    def departures(i):
        at = pl.ds(i * PART, PART)
        pairs = ((z_s.at[0, :, at], zlo_hbm.at[:, at]), (z_s.at[1, :, at], zhi_hbm.at[:, at]),
                 (i_s.at[:, at], in_hbm.at[:, at]))
        return [pltpu.make_async_copy(near, far, out_sem.at[k, i]) for k, (near, far) in enumerate(pairs)]

    for i in range(NCHUNK):
        for copy in arrivals(i):
            copy.start()

    def chunk(i, _):
        for copy in arrivals(i):
            copy.wait()
        out = pl.ds(i * PART, PART)

        def plane(ref, z):
            return ref[pl.ds(i * CHUNK * ROW + z, PART, stride=Z), :]

        for side, edge, inner in ((0, 0, 1), (1, 7, 6)):
            c_edge, c_inner = plane(c_s, edge), plane(c_s, inner)
            h_edge = half_over_psi(plane(l_s, edge))
            h_inner = half_over_psi(plane(l_s, inner))
            z_s[side, 0, out] = c_edge
            z_s[side, 1, out] = h_edge
            z_s[side, 2, out] = recip(h_edge + h_inner) * (c_inner - c_edge)
            i_s[side, out] = h_inner
        for copy in departures(i):
            copy.start()
        return 0

    lax.fori_loop(0, NCHUNK, chunk, 0)
    last = (X - 2) * ROW
    for ref, at in ((xlo_ref, 0), (xhi_ref, last)):
        ref[0] = c_s[at:at + 2 * ROW, :]
        ref[1] = l_s[at:at + 2 * ROW, :].astype(F32)
    for i in range(NCHUNK):
        for copy in departures(i):
            copy.wait()


def make_faces(c, level):
    hbm = pl.BlockSpec(memory_space=pltpu.HBM)
    vm = pl.BlockSpec(memory_space=pltpu.VMEM)
    return pl.pallas_call(
        faces_kernel,
        in_specs=[hbm, hbm],
        out_specs=[hbm, hbm, hbm, vm, vm],
        out_shape=[
            jax.ShapeDtypeStruct((3, FACE, LANES), F32),
            jax.ShapeDtypeStruct((3, FACE, LANES), F32),
            jax.ShapeDtypeStruct((2, FACE, LANES), F32),
            jax.ShapeDtypeStruct((2, 2 * ROW, LANES), F32),
            jax.ShapeDtypeStruct((2, 2 * ROW, LANES), F32),
        ],
        scratch_shapes=[
            pltpu.VMEM((ROWS, LANES), F32),
            pltpu.VMEM((ROWS, LANES), jnp.int32),
            pltpu.VMEM((2, 3, FACE, LANES), F32),
            pltpu.VMEM((2, FACE, LANES), F32),
            pltpu.SemaphoreType.DMA((2, NCHUNK)),
            pltpu.SemaphoreType.DMA((3, NCHUNK)),
        ],
        compiler_params=vmem(60),
        cost_estimate=pl.CostEstimate(flops=10**6, bytes_accessed=13 * 2**20, transcendentals=0),
        name="faces",
    )(c, level)


def y_tables():
    idx = np.arange(NB)
    table = GAIN * np.exp(-THETA * np.abs(idx[:, None] - idx[None, :]))
    high = table.astype(jnp.bfloat16)
    low = (table - high.astype(np.float64)).astype(jnp.bfloat16)
    fwd = np.exp(-THETA * (idx + 1.0))
    bwd = np.exp(-THETA * (NB - idx.astype(np.float64)))
    edge = np.zeros((8, LANES), np.float32)
    edge[0], edge[1] = fwd[:LANES], fwd[LANES:]
    edge[2], edge[3] = bwd[:LANES], bwd[LANES:]
    return high, low, edge


def split(v):
    high = v.astype(BF16)
    return high, (v - high.astype(F32)).astype(BF16)


def dot3(a, b):
    (a_high, a_low), (b_high, b_low) = a, b
    mm = functools.partial(jnp.dot, preferred_element_type=F32)
    return mm(a_high, b_high) + (mm(a_low, b_high) + mm(a_high, b_low))


def ends(first, last, length):
    scale = 1.0 / (1.0 - rho(2 * length))
    tail = rho(length)
    return (first + tail * last) * scale, (last + tail * first) * scale


def y_carry(tiles, edge):
    count = YT // 2
    heads = [jnp.broadcast_to(tiles[2 * b][:, 0:1], (8, LANES)) for b in range(count)]
    tails = [jnp.broadcast_to(tiles[2 * b + 1][:, LANES - 1:LANES], (8, LANES)) for b in range(count)]
    hop = rho(NB)
    right = [jnp.zeros_like(heads[0])]
    for b in range(count - 1):
        right.append(hop * right[-1] + tails[b])
    left = [jnp.zeros_like(heads[0])]
    for b in range(count - 1, 0, -1):
        left.append(hop * left[-1] + heads[b])
    left = left[::-1]
    from_low, from_high = ends(heads[0] + hop * left[0], tails[-1] + hop * right[-1], Y)
    out = []
    for b in range(count):
        carry_r = right[b] + rho(NB * b) * from_low
        carry_l = left[b] + rho(NB * (count - 1 - b)) * from_high
        for k in range(2):
            out.append(tiles[2 * b + k] + carry_r * edge[k:k + 1, :] + carry_l * edge[2 + k:3 + k, :])
    return out


MROWS = 16


def block_kernel(flag_ref, act_ref, c_hbm, l_hbm, xlo_ref, xhi_ref,
                 pot_hbm, u_hbm, mom_ref, edgepot_ref,
                 c_s, l_s, pot_s, u_s, st, hr, in_sem, pot_sem, u_sem):
    def copies_in(i):
        at = pl.ds(i * CHUNK, CHUNK)
        return (pltpu.make_async_copy(c_hbm.at[at], c_s.at[pl.ds(i * CHUNK + 3, CHUNK)], in_sem.at[0, i]),
                pltpu.make_async_copy(l_hbm.at[at], l_s.at[pl.ds(i * CHUNK + 3, CHUNK)], in_sem.at[1, i]))

    for i in range(NCHUNK):
        for copy in copies_in(i):
            copy.start()

    tile = (Z, LANES)
    sub, lane = sub_iota(tile), lane_iota(tile)
    top, first, last = sub == Z - 1, lane == 0, lane == LANES - 1
    WZ, WY, WX, BASE, REST, POT, SWEEP = range(7)

    def up_z(v):
        return pltpu.roll(v, Z - 1, 0)

    def down_z(v):
        return pltpu.roll(v, 1, 0)

    def up_y(v):
        return pltpu.roll(v, LANES - 1, 1)

    def down_y(v):
        return pltpu.roll(v, 1, 1)

    def ptile(e, t):
        return pl.ds(pl.multiple_of(e * ROW + t * Z, Z), Z)

    def advance(e, parity, open_x, inside):
        h = half_over_psi(l_s[e, 0])
        up_h, up_c = up_y(h), up_y(c_s[e, 0])
        below = below2 = jnp.zeros(tile, F32)
        held = None

        def second(t, pot1, up_pot, up_next, gx2, wz, wy, below2):
            gz = wz * (up_z(pot1) - pot1)
            gy = wy * (jnp.where(last, up_next, up_pot) - pot1)
            turned = down_y(gy)
            st[REST, t] = (gz - down_z(gz)) + (gy - jnp.where(first, below2, turned)) - gx2
            return turned

        for t in range(YT):
            c = c_s[e, t]
            if t + 1 < YT:
                h_next = half_over_psi(l_s[e, t + 1])
                up_h_next, up_c_next = up_y(h_next), up_y(c_s[e, t + 1])
            else:
                h_next, up_h_next, up_c_next = h, up_h, up_c
            h1 = hr[1 - parity, t]
            wx = recip(h1 + h) * open_x
            fx = wx * (c - c_s[e - 1, t])
            pot1 = st[BASE, t] - h1 * fx
            gx2 = st[WX, t] * (pot1 - st[POT, t])
            rhs = (act_ref[t] * inside) * (hr[parity, t] * (st[REST, t] + gx2))
            swept = RHO * st[SWEEP, t] + rhs
            u_s[e, t] = swept
            st[SWEEP, t] = swept
            st[POT, t] = pot1
            pot_s[ptile(e, t), :] = pot1
            wz_old, wy_old = st[WZ, t], st[WY, t]
            wz = jnp.where(top, 0.0, recip(h + up_z(h)))
            wy = recip(h + jnp.where(last, up_h_next, up_h))
            if t == YT - 1:
                wy = jnp.where(last, 0.0, wy)
            fz = wz * (up_z(c) - c)
            fy = wy * (jnp.where(last, up_c_next, up_c) - c)
            turned = down_y(fy)
            total = (fz - down_z(fz)) + (fy - jnp.where(first, below, turned)) - fx
            below = turned
            st[BASE, t] = c * (c * c - 1.0) - h * total
            st[WZ, t], st[WY, t], st[WX, t] = wz, wy, wx
            hr[parity, t] = h
            up_pot = up_y(pot1)
            if held is not None:
                t0, p0, u0, g0, z0, y0 = held
                below2 = second(t0, p0, u0, up_pot, g0, z0, y0, below2)
            held = (t, pot1, up_pot, gx2, wz_old, wy_old)
            h, up_h, up_c = h_next, up_h_next, up_c_next
        t0, p0, u0, g0, z0, y0 = held
        second(t0, p0, u0, u0, g0, z0, y0, below2)

    open_lo, open_hi = flag_ref[0], flag_ref[1]
    st[...] = jnp.zeros_like(st)
    hr[...] = jnp.ones_like(hr)
    c_s[0] = jnp.zeros((YT, Z, LANES), F32)
    for at, ref in ((1, xlo_ref), (X + 3, xhi_ref)):
        c_s[at:at + 2] = ref[0]
        l_s[at:at + 2] = ref[1].astype(jnp.int32)

    def pot_copy(i):
        src = pl.ds((i * CHUNK + 4) * ROW, CHUNK * ROW)
        return pltpu.make_async_copy(pot_s.at[src], pot_hbm.at[pl.ds(i * CHUNK * ROW, CHUNK * ROW)], pot_sem.at[i])

    pairs = CHUNK // 2

    def rows(j, _):
        turn = lax.rem(j, pairs) == 1

        @pl.when(jnp.logical_and(turn, j < X // 2))
        def _():
            for copy in copies_in((j - 1) // pairs):
                copy.wait()

        for parity in range(2):
            e = 2 * j + 1 + parity
            open_x = jnp.where(e <= 3, open_lo, jnp.where(e >= X + 3, open_hi, 1.0))
            advance(e, parity, open_x, jnp.where(e >= 5, 1.0, 0.0))

        @pl.when(jnp.logical_and(turn, j > pairs))
        def _():
            pot_copy((j - 1) // pairs - 1).start()
        return 0

    lax.fori_loop(0, X // 2 + 2, rows, 0)

    def u_copy(i):
        src = pl.ds(i * CHUNK + 5, CHUNK)
        return pltpu.make_async_copy(u_s.at[src], u_hbm.at[pl.ds(i * CHUNK, CHUNK)], u_sem.at[i])

    def back(k, carry):
        x = X - 1 - k
        mine, after = carry
        before = u_s[x + 4]
        u_s[x + 5] = GAIN * (mine + after)

        @pl.when(lax.rem(x, CHUNK) == 0)
        def _():
            u_copy(x // CHUNK).start()
        return before, RHO * (after + (mine - RHO * before))

    lax.fori_loop(0, X, back, (u_s[X + 4], jnp.zeros((YT, Z, LANES), F32)))
    mom_ref[0] = u_s[X + 4]
    mom_ref[1] = u_s[5]
    for side, z in ((0, 0), (1, 7)):
        edgepot_ref[side] = pot_s[pl.ds(4 * ROW + z, FACE, stride=Z), :]

    for i in range(NCHUNK):
        pot_copy(i).wait()
        u_copy(i).wait()


def solve_block(flags, act, c, level, xlo, xhi):
    any_spec = pl.BlockSpec(memory_space=pltpu.HBM)
    vm = pl.BlockSpec(memory_space=pltpu.VMEM)
    sm = pl.BlockSpec(memory_space=pltpu.SMEM)
    block = (X, YT, Z, LANES)
    return pl.pallas_call(
        block_kernel,
        in_specs=[sm, sm, any_spec, any_spec, vm, vm],
        out_specs=[any_spec, any_spec, vm, vm],
        out_shape=[
            jax.ShapeDtypeStruct((ROWS, LANES), F32),
            jax.ShapeDtypeStruct(block, F32),
            jax.ShapeDtypeStruct((2, YT, Z, LANES), F32),
            jax.ShapeDtypeStruct((2, FACE, LANES), F32),
        ],
        scratch_shapes=[
            pltpu.VMEM((X + 5, YT, Z, LANES), F32),
            pltpu.VMEM((X + 5, YT, Z, LANES), jnp.int32),
            pltpu.VMEM(((X + 5) * ROW, LANES), F32),
            pltpu.VMEM((X + 5, YT, Z, LANES), F32),
            pltpu.VMEM((7, YT, Z, LANES), F32),
            pltpu.VMEM((2, YT, Z, LANES), F32),
            pltpu.SemaphoreType.DMA((2, NCHUNK)),
            pltpu.SemaphoreType.DMA((NCHUNK,)),
            pltpu.SemaphoreType.DMA((NCHUNK,)),
        ],
        compiler_params=vmem(60),
        cost_estimate=pl.CostEstimate(flops=4 * 10**9, bytes_accessed=60 * 2**20, transcendentals=0),
        name="block",
    )(flags, act, c.reshape(block), level.reshape(block), xlo, xhi)


EXT = X + 2
GROUP = 8


def seam_kernel(flag_ref, pow_ref, own_lo, own_hi, inner_hbm, got_lo, got_hi, xlo_ref, xhi_ref,
                corner_lo_ref, corner_hi_ref, edgepot_hbm, mom_ref, act_ref,
                df_hbm, dpot_hbm, send_ref, ext_s, in_s, df_s, dpot_s, fl_s, acc_s, in_sem, out_sem):
    open_x = (flag_ref[0], flag_ref[1])
    tile_row = lax.broadcasted_iota(jnp.int32, (YT, LANES), 0)
    act = jnp.zeros((YT, LANES), F32)
    for t in range(YT):
        act = jnp.where(tile_row == t, act_ref[t], act)
    shape = (GROUP, YT, LANES)
    open_y = jnp.logical_or(
        lax.broadcasted_iota(jnp.int32, shape, 2) < LANES - 1,
        lax.broadcasted_iota(jnp.int32, shape, 1) < YT - 1,
    )
    row = lax.broadcasted_iota(jnp.int32, shape, 0)
    acc_s[...] = jnp.zeros_like(acc_s)
    main = pl.ds(1, X)

    def arrivals(side):
        own, got = ((own_lo, got_lo), (own_hi, got_hi))[side]
        pairs = [(own.at[0], ext_s.at[side, 0, main]), (own.at[1], ext_s.at[side, 1, main]),
                 (got.at[0], ext_s.at[side, 2, main]), (got.at[1], ext_s.at[side, 3, main]),
                 (got.at[2], in_s.at[side, 0]), (inner_hbm.at[side], in_s.at[side, 1]),
                 (edgepot_hbm.at[side], in_s.at[side, 2])]
        return [pltpu.make_async_copy(far, near, in_sem.at[side, k]) for k, (far, near) in enumerate(pairs)]

    def departures(side):
        at = pl.ds(2 * side, 2)
        return [pltpu.make_async_copy(df_s.at[at], df_hbm.at[at], out_sem.at[side, 0]),
                pltpu.make_async_copy(dpot_s.at[side], dpot_hbm.at[side], out_sem.at[side, 1])]

    for side in range(2):
        for copy in arrivals(side):
            copy.start()

    for side, (corner, z) in enumerate(((corner_lo_ref, 0), (corner_hi_ref, 7))):
        for spot, ref, r, k in ((0, xlo_ref, 1, 0), (EXT - 1, xhi_ref, 0, 1)):
            ext_s[side, 0, spot] = ref[0, r, :, z, :]
            ext_s[side, 1, spot] = half_over_psi(ref[1, r, :, z, :])
            ext_s[side, 2, spot] = corner[2 * k]
            ext_s[side, 3, spot] = half_over_psi(corner[2 * k + 1])

    def one_side(side, _):
        for k in range(2):
            @pl.when(side == k)
            def _():
                for copy in arrivals(k):
                    copy.wait()
        open_z = flag_ref[2 + side]
        bias = 1.0 - open_z
        c0_s, h0_s, cm_s, hm_s, dp_s = (ext_s.at[side, k] for k in range(5))
        got2_s, inner_s, pot_s = (in_s.at[side, k] for k in range(3))

        def first(i, _):
            at = pl.ds(i * 6, 6)
            h0 = h0_s[at]
            flux = recip(h0 + hm_s[at]) * open_z * (cm_s[at] - c0_s[at])
            fl_s[at] = flux
            dp_s[at] = -h0 * flux
            return 0

        lax.fori_loop(0, EXT // 6, first, 0)

        def second(i, _):
            at = pl.ds(i * GROUP, GROUP)
            ext = pl.ds(i * GROUP + 1, GROUP)
            after = pl.ds(i * GROUP + 2, GROUP)
            lo_gate = jnp.where(row == 0, jnp.where(i == 0, open_x[0], 1.0), 1.0)
            hi_gate = jnp.where(row == GROUP - 1, jnp.where(i == X // GROUP - 1, open_x[1], 1.0), 1.0)

            def plane(h_ref, v_ref, extra):
                h, v = h_ref[ext] + extra, v_ref[ext]
                wy = jnp.where(open_y, recip(h + next_y(h)), 0.0)
                fy = wy * (next_y(v) - v)
                total = recip(h + h_ref[at]) * lo_gate * (v_ref[at] - v)
                total = total + recip(h + h_ref[after]) * hi_gate * (v_ref[after] - v)
                return h, v, total + (fy - prev_y(fy))

            hm, cm, across_m = plane(hm_s, cm_s, bias)
            h0, dp, across_0 = plane(h0_s, dp_s, 0.0)
            flux = fl_s[ext]
            potm = cm * (cm * cm - 1.0) - hm * (across_m + got2_s[at] - flux)
            pot0 = pot_s[at] + dp
            h1 = inner_s[at]
            toward = recip(h0 + h1) * dp
            join = recip(h0 + hm) * open_z * (potm - pot0)
            df0 = act * (h0 * (across_0 - toward + join))
            df1 = act * (h1 * toward)
            outer, inner = 3 * side, 1 + side
            df_s[outer, at] = df0
            df_s[inner, at] = df1
            dpot_s[side, at] = dp
            for spot, value in ((outer, df0), (inner, df1)):
                last, start = acc_s[spot], acc_s[4 + spot]
                for r in range(GROUP):
                    x = i * GROUP + r
                    last = last + pow_ref[1, X - 1 - x] * value[r]
                    start = start + pow_ref[1, x] * value[r]
                acc_s[spot] = last
                acc_s[4 + spot] = start
            return 0

        lax.fori_loop(0, X // GROUP, second, 0)
        for copy in departures(side):
            copy.start()
        return 0

    lax.fori_loop(0, 2, one_side, 0)

    sub = sub_iota((Z, LANES))
    half = sub < 4
    for t in range(YT):
        totals = []
        for which in range(2):
            total = mom_ref[which, t]
            for k, z in enumerate((0, 1, 6, 7)):
                line = jnp.broadcast_to(acc_s[4 * which + k, t:t + 1, :], (Z, LANES))
                total = total + jnp.where(sub == z, line, 0.0)
            totals.append(total)
        last, start = totals
        send_ref[2 * t] = jnp.where(half, last, pltpu.roll(start, 4, 0))
        send_ref[2 * t + 1] = jnp.where(half, pltpu.roll(last, 4, 0), start)
    for side in range(2):
        for copy in departures(side):
            copy.wait()


def add_seams(flags, powers, own_lo, own_hi, inner, got_lo, got_hi, xlo, xhi, corner_lo, corner_hi, edgepot, mom, act):
    vm = pl.BlockSpec(memory_space=pltpu.VMEM)
    sm = pl.BlockSpec(memory_space=pltpu.SMEM)
    hbm = pl.BlockSpec(memory_space=pltpu.HBM)
    lines = [a.reshape(a.shape[0], X, YT, LANES) for a in (own_lo, own_hi, inner, got_lo, got_hi)]
    return pl.pallas_call(
        seam_kernel,
        in_specs=[sm, sm] + [hbm] * 5 + [vm] * 4 + [hbm, vm, sm],
        out_specs=[hbm, hbm, vm],
        out_shape=[
            jax.ShapeDtypeStruct((4, X, YT, LANES), F32),
            jax.ShapeDtypeStruct((2, X, YT, LANES), F32),
            jax.ShapeDtypeStruct((32, Z, LANES), F32),
        ],
        scratch_shapes=[
            pltpu.VMEM((2, 5, EXT, YT, LANES), F32),
            pltpu.VMEM((2, 3, X, YT, LANES), F32),
            pltpu.VMEM((4, X, YT, LANES), F32),
            pltpu.VMEM((2, X, YT, LANES), F32),
            pltpu.VMEM((EXT, YT, LANES), F32),
            pltpu.VMEM((8, YT, LANES), F32),
            pltpu.SemaphoreType.DMA((2, 7)),
            pltpu.SemaphoreType.DMA((2, 2)),
        ],
        compiler_params=vmem(60),
        cost_estimate=pl.CostEstimate(flops=10**7, bytes_accessed=12 * 2**20, transcendentals=0),
        name="seams",
    )(flags, powers, *lines, xlo, xhi, corner_lo, corner_hi, edgepot.reshape(2, X, YT, LANES), mom, act)


def settle_kernel(pot_hbm, u_hbm, dpot_ref, df_ref, pot_out, u_out, pot_s, u_s, p_s, in_sem, out_sem):
    def moves(i):
        at = pl.ds(i * CHUNK * ROW, CHUNK * ROW)
        return [
            (pltpu.make_async_copy(far.at[at], near.at[at], in_sem.at[k, i]),
             pltpu.make_async_copy(near.at[at], out.at[at], out_sem.at[k, i]))
            for k, (far, near, out) in enumerate(((pot_hbm, pot_s, pot_out), (u_hbm, u_s, u_out)))
        ]

    for i in reversed(range(NCHUNK)):
        for start, _ in moves(i):
            start.start()

    shape = (4, YT, LANES)

    def forth(x, carry):
        carry = RHO * carry + df_ref[:, x]
        p_s[:, x] = carry
        return carry

    lax.fori_loop(0, X, forth, jnp.zeros(shape, F32), unroll=8)

    def back(k, carry):
        x = X - 1 - k
        solved = GAIN * (p_s[:, x] + carry)
        for n, z in enumerate((0, 1, 6, 7)):
            at = pl.ds(x * ROW + z, YT, stride=Z)
            u_s[at, :] = u_s[at, :] + solved[n]
        return RHO * (carry + df_ref[:, x])

    def chunk(done, carry):
        i = NCHUNK - 1 - done
        (pot_in, pot_back), (u_in, u_back) = moves(i)
        pot_in.wait()
        for side, z in ((0, 0), (1, 7)):
            at = pl.ds(i * CHUNK * ROW + z, PART, stride=Z)
            pot_s[at, :] = pot_s[at, :] + dpot_ref[side, pl.ds(i * PART, PART), :]
        pot_back.start()
        u_in.wait()
        carry = lax.fori_loop(0, CHUNK, lambda k, c: back(done * CHUNK + k, c), carry, unroll=4)
        u_back.start()
        return carry

    lax.fori_loop(0, NCHUNK, chunk, jnp.zeros(shape, F32))
    for i in range(NCHUNK):
        for _, back_copy in moves(i):
            back_copy.wait()


def settle(pot, u, dpot, df):
    vm = pl.BlockSpec(memory_space=pltpu.VMEM)
    any_spec = pl.BlockSpec(memory_space=pltpu.HBM)
    rows = jax.ShapeDtypeStruct((ROWS, LANES), F32)
    return pl.pallas_call(
        settle_kernel,
        in_specs=[any_spec, any_spec, vm, vm],
        out_specs=[any_spec, any_spec],
        out_shape=[rows, rows],
        scratch_shapes=[
            pltpu.VMEM((ROWS, LANES), F32),
            pltpu.VMEM((ROWS, LANES), F32),
            pltpu.VMEM((4, X, YT, LANES), F32),
            pltpu.SemaphoreType.DMA((2, NCHUNK)),
            pltpu.SemaphoreType.DMA((2, NCHUNK)),
        ],
        compiler_params=vmem(60),
        cost_estimate=pl.CostEstimate(flops=10**7, bytes_accessed=10 * 2**20, transcendentals=0),
        name="settle",
    )(pot, u.reshape(ROWS, LANES), dpot.reshape(2, FACE, LANES), df)


def lines_kernel(u_hbm, thigh_ref, tlow_ref, edge_ref, out_hbm, u_s, w_s, in_sem, out_sem):
    groups = X // MROWS

    def moves(i):
        at = pl.ds(i * MROWS, MROWS)
        return (pltpu.make_async_copy(u_hbm.at[at], u_s.at[at], in_sem.at[i]),
                pltpu.make_async_copy(u_s.at[at], out_hbm.at[at], out_sem.at[i]))

    for i in range(groups):
        moves(i)[0].start()
    edge = edge_ref[...]

    def group(i, _):
        come, leave = moves(i)
        come.wait()
        xs = pl.ds(i * MROWS, MROWS)
        table = (thigh_ref[...], tlow_ref[...])
        for b in range(YT // 2):
            pair = [u_s[xs, 2 * b + k].reshape(MROWS * Z, LANES) for k in range(2)]
            solved = dot3(split(jnp.concatenate(pair, axis=1)), table)
            for k in range(2):
                w_s[:, 2 * b + k] = solved[:, k * LANES:(k + 1) * LANES].reshape(MROWS, Z, LANES)

        def body(x, _):
            for t, part in enumerate(y_carry([w_s[x, t] for t in range(YT)], edge)):
                u_s[i * MROWS + x, t] = part
            return 0

        lax.fori_loop(0, MROWS, body, 0, unroll=UNROLL)
        leave.start()
        return 0

    lax.fori_loop(0, groups, group, 0)
    for i in range(groups):
        moves(i)[1].wait()


UNROLL = 4


def solve_lines(u, tables):
    vm = pl.BlockSpec(memory_space=pltpu.VMEM)
    hbm = pl.BlockSpec(memory_space=pltpu.HBM)
    return pl.pallas_call(
        lines_kernel,
        in_specs=[hbm] + [vm] * 3,
        out_specs=hbm,
        out_shape=jax.ShapeDtypeStruct((X, YT, Z, LANES), F32),
        scratch_shapes=[
            pltpu.VMEM((X, YT, Z, LANES), F32),
            pltpu.VMEM((MROWS, YT, Z, LANES), F32),
            pltpu.SemaphoreType.DMA((X // MROWS,)),
            pltpu.SemaphoreType.DMA((X // MROWS,)),
        ],
        compiler_params=vmem(60),
        cost_estimate=pl.CostEstimate(flops=2 * 10**9, bytes_accessed=10 * 2**20, transcendentals=0),
        name="lines",
    )(u, *tables)


def carries_kernel(count, in_ref, out_ref):
    got = [in_ref[d] for d in range(count)]
    half = sub_iota((8, TILE)) < 4
    hop = rho(X)
    right = [jnp.zeros((8, TILE), F32)]
    for d in range(count - 1):
        right.append(hop * right[-1] + got[d])
    starts = [pltpu.roll(g, 4, 0) for g in got]
    left = [jnp.zeros((8, TILE), F32)]
    for d in range(count - 1, 0, -1):
        left.append(hop * left[-1] + starts[d])
    left = left[::-1]
    from_low, from_high = ends(starts[0] + hop * left[0], got[-1] + hop * right[-1], X * count)
    for d in range(count):
        carry_r = right[d] + rho(X * d) * from_low
        carry_l = left[d] + rho(X * (count - 1 - d)) * from_high
        out_ref[d] = jnp.where(half, carry_r, pltpu.roll(carry_l, 4, 0))


def scan_carries(got):
    vm = pl.BlockSpec(memory_space=pltpu.VMEM)
    return pl.pallas_call(
        functools.partial(carries_kernel, got.shape[0]),
        in_specs=[vm],
        out_specs=vm,
        out_shape=jax.ShapeDtypeStruct(got.shape, F32),
        cost_estimate=pl.CostEstimate(flops=10**6, bytes_accessed=2**18, transcendentals=0),
        name="carries",
    )(got)


FIN = 8


def final_kernel(pow_ref, got_ref, thigh_ref, tlow_ref, edge_ref, v_hbm, out_hbm, v_s, lr_s, in_sem, out_sem):
    def moves(i):
        at = pl.ds(i * FIN * ROW, FIN * ROW)
        return (pltpu.make_async_copy(v_hbm.at[at], v_s.at[at], in_sem.at[i]),
                pltpu.make_async_copy(v_s.at[at], out_hbm.at[at], out_sem.at[i]))

    for i in range(X // FIN):
        moves(i)[0].start()
    half = sub_iota((Z, LANES)) < 4
    edge = edge_ref[...]

    def solve(b, _):
        pair = []
        for k in range(2):
            even, odd = got_ref[4 * b + 2 * k], got_ref[4 * b + 2 * k + 1]
            pair.append(jnp.concatenate([
                jnp.where(half, even, pltpu.roll(odd, 4, 0)),
                jnp.where(half, pltpu.roll(even, 4, 0), odd),
            ], axis=0))
        solved = dot3(split(jnp.concatenate(pair, axis=1)), (thigh_ref[...], tlow_ref[...]))
        for side in range(2):
            for k in range(2):
                lr_s[side, 2 * b + k] = solved[8 * side:8 * side + 8, k * LANES:(k + 1) * LANES]
        return 0

    lax.fori_loop(0, YT // 2, solve, 0)

    def carry(side, _):
        for t, part in enumerate(y_carry([lr_s[side, t] for t in range(YT)], edge)):
            lr_s[side, t] = part
        return 0

    lax.fori_loop(0, 2, carry, 0)

    def chunk(i, _):
        come, leave = moves(i)
        come.wait()

        def row(r, _):
            x = i * FIN + r
            at = pl.ds(pl.multiple_of(x * ROW, ROW), ROW)
            low, high = (lr_s[side].reshape(ROW, LANES) for side in range(2))
            v_s[at, :] = v_s[at, :] + pow_ref[0, x] * low + pow_ref[0, X - 1 - x] * high
            return 0

        lax.fori_loop(0, FIN, row, 0, unroll=2)
        leave.start()
        return 0

    lax.fori_loop(0, X // FIN, chunk, 0)
    for i in range(X // FIN):
        moves(i)[1].wait()


def finish(powers, got, tables, v):
    vm = pl.BlockSpec(memory_space=pltpu.VMEM)
    hbm = pl.BlockSpec(memory_space=pltpu.HBM)
    return pl.pallas_call(
        final_kernel,
        in_specs=[pl.BlockSpec(memory_space=pltpu.SMEM)] + [vm] * 4 + [hbm],
        out_specs=hbm,
        out_shape=jax.ShapeDtypeStruct((ROWS, LANES), F32),
        scratch_shapes=[
            pltpu.VMEM((ROWS, LANES), F32),
            pltpu.VMEM((2, YT, Z, LANES), F32),
            pltpu.SemaphoreType.DMA((X // FIN,)),
            pltpu.SemaphoreType.DMA((X // FIN,)),
        ],
        compiler_params=vmem(60),
        cost_estimate=pl.CostEstimate(flops=10**7, bytes_accessed=10 * 2**20, transcendentals=0),
        name="finish",
    )(powers, got, *tables, v)


def shift(value, axis, forward):
    count = lax.axis_size(axis)
    pairs = [(i, i + 1) for i in range(count - 1)]
    if not forward:
        pairs = [(b, a) for a, b in pairs]
    return lax.ppermute(value, axis, pairs)


def to_tiles(block):
    return block.reshape(X, Z, YT, LANES).transpose(0, 2, 1, 3).reshape(ROWS, LANES)


def from_tiles(rows):
    return rows.reshape(X, YT, Z, LANES).transpose(0, 2, 1, 3).reshape(X, Z, Y)


def per_device(concentration, psi_level, tile_mask):
    c, level = to_tiles(concentration), to_tiles(psi_level)
    xy, gz = lax.axis_index("xy"), lax.axis_index("gz")
    n_xy, n_gz = lax.axis_size("xy"), lax.axis_size("gz")
    flags = jnp.stack([xy > 0, xy < n_xy - 1, gz > 0, gz < n_gz - 1]).astype(F32)
    mask_row = lax.dynamic_index_in_dim(tile_mask, xy * X // TILE, 0, keepdims=False)
    act = mask_row.astype(F32) * (2.0 * TIME_STEP)
    tables = tuple(jnp.asarray(t) for t in y_tables())
    steps = np.exp(-THETA * np.arange(X + 1))
    powers = jnp.asarray(np.stack([steps[1:], GAIN * steps[:-1]]).astype(np.float32))

    zlo, zhi, inner, xlo, xhi = make_faces(c, level)
    pair = (2, 2, YT, Z, LANES)
    got_xlo = shift(xhi, "xy", True).reshape(pair)
    got_xhi = shift(xlo, "xy", False).reshape(pair)
    got_zlo = shift(zhi, "gz", True)
    got_zhi = shift(zlo, "gz", False)

    def corners(z):
        return jnp.stack([got_xlo[0, 1, :, z], got_xlo[1, 1, :, z], got_xhi[0, 0, :, z], got_xhi[1, 0, :, z]])

    corner_lo = shift(corners(7), "gz", True)
    corner_hi = shift(corners(0), "gz", False)

    pot, u, mom, edgepot = solve_block(flags, act, c, level, got_xlo, got_xhi)
    df, dpot, send = add_seams(
        flags, powers, zlo, zhi, inner, got_zlo, got_zhi, got_xlo, got_xhi, corner_lo, corner_hi, edgepot, mom, act,
    )
    got = lax.all_to_all(send, "xy", split_axis=0, concat_axis=0, tiled=True)
    potential, u = settle(pot, u, dpot, df)
    got, u = lax.optimization_barrier((got, u))
    back = lax.all_to_all(scan_carries(got), "xy", split_axis=0, concat_axis=0, tiled=True)
    v = solve_lines(u.reshape(X, YT, Z, LANES), tables)
    increment = finish(powers, back, tables, v.reshape(ROWS, LANES))
    return from_tiles(potential), from_tiles(increment)


def solution(mesh):
    placed = (P("xy", "gz", None), P("xy", "gz", None), P())
    return jax.shard_map(
        per_device,
        mesh=mesh,
        in_specs=placed,
        out_specs=(P("xy", "gz", None), P("xy", "gz", None)),
        check_vma=False,
    )
```

time: 129 us -> 103 us (0.80)
  local copies, waits for them, and re-layouts: 19.5 us -> 3.94 us
  Pallas kernels: 67.8 us -> 58.1 us
  waiting for transfers between devices: 7.18 us -> 1.66 us
  starting transfers between devices: 30.8 us -> 35.6 us
    unnamed x34 -> x14, local copies, waits for them, and re-layouts: 18.4 us -> 2.96 us
    pallas_call x6, Pallas kernels: 66.2 us -> 56.5 us  [the longest x1 18.2 us: solve_block(): pl.pallas_call(block_kernel, in_specs=[sm, sm, any_spec, any_spec, vm, vm...]
    ppermute x6, waiting for transfers between devices: 5.55 us -> 1.66 us  [shift(): return lax.ppermute(value, axis, pairs)]
    all_to_all x1, starting transfers between devices: 7.78 us -> 11 us  [per_device(): got = lax.all_to_all(send, 'xy', split_axis=0, concat_axis=0, tiled=True)]
    all_to_all x1, waiting for transfers between devices: 1.63 us -> 0.01 us  [per_device(): got = lax.all_to_all(send, 'xy', split_axis=0, concat_axis=0, tiled=True)]
    all_to_all x1, starting transfers between devices: 5.76 us -> 7.38 us  [per_device(): lax.all_to_all(scan_carries(got), 'xy', split_axis=0, concat_axis=0, tile...]
  transfers between devices with their start and end apart: 8 -> 8, of which waited for: 3 -> 2; matrix products, arithmetic and copies ran while one was open for 1% -> 3% of each run, Pallas kernels for 40% -> 34%
where the time goes in v2:
time: 103 us; the launch traced here: 102 us
  Pallas kernels  58.1 us (56%)
  starting transfers between devices  35.6 us (35%)
  local copies, waits for them, and re-layouts  3.94 us (4%)
  other arithmetic  1.92 us (2%)
  waiting for transfers between devices  1.66 us (2%)
    pallas_call x1, Pallas kernels, solve_block(): pl.pallas_call(block_kernel, in_specs=[sm, sm, any_spec, any_spec, vm, vm...  18.2 us
    ppermute x6, starting transfers between devices, shift(): return lax.ppermute(value, axis, pairs)  17.2 us
    all_to_all x1, starting transfers between devices, per_device(): got = lax.all_to_all(send, 'xy', split_axis=0, concat_axis=0, tiled=True)  11 us
    pallas_call x1, Pallas kernels, add_seams(): pl.pallas_call(seam_kernel, in_specs=[sm, sm] + [hbm] * 5 + [vm] * 4 + [h...  9.92 us
    pallas_call x1, Pallas kernels, settle(): pl.pallas_call(settle_kernel, in_specs=[any_spec, any_spec, vm, vm], out_...  8.55 us
    pallas_call x1, Pallas kernels, solve_lines(): pl.pallas_call(lines_kernel, in_specs=[hbm] + [vm] * 3, out_specs=hbm, ou...  8.47 us
    all_to_all x1, starting transfers between devices, per_device(): lax.all_to_all(scan_carries(got), 'xy', split_axis=0, concat_axis=0, tile...  7.38 us
    pallas_call x1, Pallas kernels, make_faces(): pl.pallas_call(faces_kernel, in_specs=[hbm, hbm], out_specs=[hbm, hbm, hb...  6.37 us
  transfers between devices with their start and end apart: 8, of which 2 were waited for; matrix products, arithmetic and copies ran while one was open for 3% of the time, Pallas kernels for 34%

profile of v2, /device:TPU:25, one launch (start us, length us, event | category | flops | bytes accessed | tf_op | source)
XLA Modules:
  0.0 102.2 jit_solution(12380003736082869468)
XLA Ops:
  0.6 6.4 %faces.1 = (f32[3,1024,128]{2,1,0:T(8,128)}, f32[3,1024,128]{2,1,0:T(8,128)}, f32[2,1024,128]{2,1,0:T(8,128)}, f32[2,256,128]{2,1,0:T(8,128)}, f32[2,256,128]{2,1,0:T(8,128)}) custom-call(f32[8192,128]{1,0:T(8,128)} %bitcast.63, s32[8192,128]{1,0:T(8,128)} %bitcast.65), custom_call_target="tpu_custom_call" | custom-call | flops 1000000 | bytes 13631488 | tf_op jit(solution)/shard_map/faces/pallas_call | solution.py:147
  7.0 1.3 %collective-permute-start.2 = (f32[3,1024,128]{2,1,0:T(8,128)}, f32[3,1024,128]{2,1,0:T(8,128)S(1)}, u32[]{:S(2)}, u32[]{:S(2)}) collective-permute-start(f32[3,1024,128]{2,1,0:T(8,128)} %get-tuple-element.23), channel_id=1, source_target_pairs={{0,1},{1,2},{2,3},{4,5},{5,6},{6,7},{8,9},{9,10},{10,11},{12,13},{... | collective-permute-start | bytes 4718600 | tf_op jit(solution)/shard_map/ppermute | solution.py:808
  8.3 4.1 %collective-permute-start.3 = (f32[3,1024,128]{2,1,0:T(8,128)}, f32[3,1024,128]{2,1,0:T(8,128)S(1)}, u32[]{:S(2)}, u32[]{:S(2)}) collective-permute-start(f32[3,1024,128]{2,1,0:T(8,128)} %get-tuple-element.22), channel_id=1, source_target_pairs={{1,0},{2,1},{3,2},{5,4},{6,5},{7,6},{9,8},{10,9},{11,10},{13,12},{... | collective-permute-start | bytes 4718600 | tf_op jit(solution)/shard_map/ppermute | solution.py:808
  12.4 3.1 %collective-permute-start.1 = (f32[2,256,128]{2,1,0:T(8,128)}, f32[2,256,128]{2,1,0:T(8,128)S(1)}, u32[]{:S(2)}, u32[]{:S(2)}) collective-permute-start(f32[2,256,128]{2,1,0:T(8,128)} %get-tuple-element.19), channel_id=1, source_target_pairs={{4,0},{8,4},{12,8},{16,12},{20,16},{24,20},{28,24},{32,28},{36,32}... | collective-permute-start | bytes 786440 | tf_op jit(solution)/shard_map/ppermute | solution.py:808
  15.5 3.4 %collective-permute-start = (f32[2,256,128]{2,1,0:T(8,128)}, f32[2,256,128]{2,1,0:T(8,128)}, u32[]{:S(2)}, u32[]{:S(2)}) collective-permute-start(f32[2,256,128]{2,1,0:T(8,128)} %get-tuple-element.18), channel_id=1, source_target_pairs={{0,4},{4,8},{8,12},{12,16},{16,20},{20,24},{24,28},{28,32},{32,36}... | collective-permute-start | bytes 786440 | tf_op jit(solution)/shard_map/ppermute | solution.py:808
  19.0 1.2 %multiply_bitcast_fusion.act_ref = f32[16]{0:T(128)} fusion(s32[16,16]{1,0:T(8,128)} %param.9, s32[]{:T(128)S(6)} %select_n.10), kind=kLoop, calls=%fused_computation.3 | loop fusion | flops 32 | bytes 132 | tf_op jit(solution)/shard_map/mul | solution.py:825
  20.3 0.7 add_convert_fusion.flag_ref
  20.9 0.7 collective-permute-done.1
  21.6 0.0 copy-start.4
  21.6 1.0 collective-permute-done
  22.6 1.0 fusion
  23.6 1.3 %collective-permute-start.4 = (f32[4,16,128]{2,1,0:T(8,128)S(1)}, f32[4,16,128]{2,1,0:T(8,128)S(1)}, u32[]{:S(2)}, u32[]{:S(2)}) collective-permute-start(f32[4,16,128]{2,1,0:T(8,128)S(1)} %pad_maximum_fusion), channel_id=1, source_target_pairs={{0,1},{1,2},{2,3},{4,5},{5,6},{6,7},{8,9},{9,10},{10,11},{12,13},{... | collective-permute-start | bytes 98312 | tf_op jit(solution)/shard_map/ppermute | solution.py:808
  24.9 4.0 %collective-permute-start.5 = (f32[4,16,128]{2,1,0:T(8,128)S(1)}, f32[4,16,128]{2,1,0:T(8,128)S(1)}, u32[]{:S(2)}, u32[]{:S(2)}) collective-permute-start(f32[4,16,128]{2,1,0:T(8,128)S(1)} %pad_maximum_fusion.1), channel_id=1, source_target_pairs={{1,0},{2,1},{3,2},{5,4},{6,5},{7,6},{9,8},{10,9},{11,10},{13,12},{... | collective-permute-start | bytes 98312 | tf_op jit(solution)/shard_map/ppermute | solution.py:808
  28.9 0.0 copy-done.4
  28.9 18.2 %block.1 = (f32[8192,128]{1,0:T(8,128)}, f32[64,16,8,128]{3,2,1,0:T(8,128)}, f32[2,16,8,128]{3,2,1,0:T(8,128)}, f32[2,1024,128]{2,1,0:T(8,128)}) custom-call(f32[4]{0:T(128)} %add_convert_fusion.flag_ref, f32[16]{0:T(128)} %multiply_bitcast_fusion.act_ref, f32[64,16,8,128]{3,2,1,0:T(8,128)} %bitcast.64, s32[64,16,8,128]{3,2,1,0:T(8,128)} %bitcast.66, ...), custom_call_target="tpu_custom_call" | custom-call | flops 4000000000 | bytes 62914560 | tf_op jit(solution)/shard_map/block/pallas_call | solution.py:377
  47.1 0.0 collective-permute-done.4.corner_lo_ref
  47.1 0.0 copy-start.5
  47.1 0.0 collective-permute-done.5.corner_hi_ref
  47.1 0.0 copy-start.6
  47.2 0.0 collective-permute-done.2
  47.2 0.0 copy-start
  47.2 0.0 collective-permute-done.3
  47.2 0.0 copy-start.1
  47.2 0.5 copy-done.5
  47.7 0.0 copy-done.6
  47.8 0.6 copy-done
  48.3 0.5 copy-done.1
  48.8 9.9 %seams.1 = (f32[4,64,16,128]{3,2,1,0:T(8,128)}, f32[2,64,16,128]{3,2,1,0:T(8,128)}, f32[32,8,128]{2,1,0:T(8,128)}) custom-call(f32[4]{0:T(128)} %add_convert_fusion.flag_ref, f32[2,64]{1,0:T(2,128)} %constant.50.clone.pow_ref, f32[3,64,16,128]{3,2,1,0:T(8,128)} %bitcast.70, f32[3,64,16,128]{3,2,1,0:T(8,128)} %bitcast.71, f32[2,64,16,128]{3,2,1,0:T(8,128)} %bitcast.74, ...), custom_call_target="tpu_custom_call" | custom-call | flops 10000000 | bytes 12582912 | tf_op jit(solution)/shard_map/seams/pallas_call | solution.py:539
  58.8 11.0 %all-to-all-start = ((f32[32,8,128]{2,1,0:T(8,128)}), f32[32,8,128]{2,1,0:T(8,128)S(1)}, u32[]{:S(2)}, u32[]{:S(2)}) async-start(f32[32,8,128]{2,1,0:T(8,128)} %get-tuple-element.30), calls=%async_computation | async-start | bytes 262144 | tf_op jit(solution)/shard_map/all_to_all | solution.py:847
  69.8 8.5 %settle.1 = (f32[8192,128]{1,0:T(8,128)}, f32[8192,128]{1,0:T(8,128)}) custom-call(f32[8192,128]{1,0:T(8,128)} %get-tuple-element.20.pot_hbm, f32[8192,128]{1,0:T(8,128)} %bitcast.69, f32[2,1024,128]{2,1,0:T(8,128)} %bitcast.76, f32[4,64,16,128]{3,2,1,0:T(8,128)} %get-tuple-element.28.df_ref), custom_call_target="tpu_custom_call" | custom-call | flops 10000000 | bytes 10485760 | tf_op jit(solution)/shard_map/settle/pallas_call | solution.py:617
  78.3 0.0 all-to-all-done.in_ref
  78.3 0.0 copy-start.3
  78.3 0.6 copy-done.3
  79.0 1.6 %carries.1 = f32[32,8,128]{2,1,0:T(8,128)} custom-call(f32[32,8,128]{2,1,0:T(8,128)} %copy-done.3), custom_call_target="tpu_custom_call" | custom-call | flops 1000000 | bytes 262144 | tf_op jit(solution)/shard_map/carries/pallas_call | solution.py:716
  80.6 7.4 %all-to-all-start.1 = ((f32[32,8,128]{2,1,0:T(8,128)}), f32[32,8,128]{2,1,0:T(8,128)S(1)}, u32[]{:S(2)}, u32[]{:S(2)}) async-start(f32[32,8,128]{2,1,0:T(8,128)} %carries.1), calls=%async_computation.1 | async-start | bytes 262144 | tf_op jit(solution)/shard_map/all_to_all | solution.py:850
  88.0 8.5 %lines.1 = f32[64,16,8,128]{3,2,1,0:T(8,128)} custom-call(f32[64,16,8,128]{3,2,1,0:T(8,128)} %bitcast.68, bf16[256,256]{1,0:T(8,128)(2,1)} %constant.47.clone.thigh_ref, bf16[256,256]{1,0:T(8,128)(2,1)} %constant.48.clone.tlow_ref, f32[8,128]{1,0:T(8,128)} %constant.49.clone.edge_ref), custom_call_target="tpu_custom_call" | custom-call | flops 2000000000 | bytes 10485760 | tf_op jit(solution)/shard_map/lines/pallas_call | solution.py:678
  96.5 0.0 all-to-all-done.1.got_ref
  96.5 0.0 copy-start.2
  96.5 0.7 copy-done.2
  97.2 5.0 %finish.1 = f32[8192,128]{1,0:T(8,128)} custom-call(f32[2,64]{1,0:T(2,128)} %constant.50.clone.pow_ref, f32[32,8,128]{2,1,0:T(8,128)} %copy-done.2, bf16[256,256]{1,0:T(8,128)(2,1)} %constant.47.clone.thigh_ref, bf16[256,256]{1,0:T(8,128)(2,1)} %constant.48.clone.tlow_ref, f32[8,128]{1,0:T(8,128)} %constant.49.clone.edge_ref, f32[8192,128]{1,0:T(8,128)} %bitcast.62), custom_call_target="tpu_custom_call" | custom-call | flops 10000000 | bytes 10485760 | tf_op jit(solution)/shard_map/finish/pallas_call | solution.py:786
  (3 shorter events, 0.0 us)
Async XLA Ops:
  7.0 40.2 %collective-permute-start.2 = (f32[3,1024,128]{2,1,0:T(8,128)}, f32[3,1024,128]{2,1,0:T(8,128)S(1)}, u32[]{:S(2)}, u32[]{:S(2)}) collective-permute-start(f32[3,1024,128]{2,1,0:T(8,128)} %get-tuple-element.23), channel_id=1, source_target_pairs={{0,1},{1,2},{2,3},{4,5},{5,6},{6,7},{8,9},{9,10},{10,11},{12,13},{... | collective-permute-start | bytes 4718600 | tf_op jit(solution)/shard_map/ppermute | solution.py:808
  8.3 38.9 %collective-permute-start.3 = (f32[3,1024,128]{2,1,0:T(8,128)}, f32[3,1024,128]{2,1,0:T(8,128)S(1)}, u32[]{:S(2)}, u32[]{:S(2)}) collective-permute-start(f32[3,1024,128]{2,1,0:T(8,128)} %get-tuple-element.22), channel_id=1, source_target_pairs={{1,0},{2,1},{3,2},{5,4},{6,5},{7,6},{9,8},{10,9},{11,10},{13,12},{... | collective-permute-start | bytes 4718600 | tf_op jit(solution)/shard_map/ppermute | solution.py:808
  12.4 9.2 %collective-permute-start.1 = (f32[2,256,128]{2,1,0:T(8,128)}, f32[2,256,128]{2,1,0:T(8,128)S(1)}, u32[]{:S(2)}, u32[]{:S(2)}) collective-permute-start(f32[2,256,128]{2,1,0:T(8,128)} %get-tuple-element.19), channel_id=1, source_target_pairs={{4,0},{8,4},{12,8},{16,12},{20,16},{24,20},{28,24},{32,28},{36,32}... | collective-permute-start | bytes 786440 | tf_op jit(solution)/shard_map/ppermute | solution.py:808
  15.5 7.1 %collective-permute-start = (f32[2,256,128]{2,1,0:T(8,128)}, f32[2,256,128]{2,1,0:T(8,128)}, u32[]{:S(2)}, u32[]{:S(2)}) collective-permute-start(f32[2,256,128]{2,1,0:T(8,128)} %get-tuple-element.18), channel_id=1, source_target_pairs={{0,4},{4,8},{8,12},{12,16},{16,20},{20,24},{24,28},{28,32},{32,36}... | collective-permute-start | bytes 786440 | tf_op jit(solution)/shard_map/ppermute | solution.py:808
  21.6 7.3 %copy-start.4 = (f32[2,256,128]{2,1,0:T(8,128)}, f32[2,256,128]{2,1,0:T(8,128)S(1)}, u32[]{:S(2)}) copy-start(f32[2,256,128]{2,1,0:T(8,128)S(1)} %collective-permute-done.1) | copy-start | bytes 786436
  23.6 23.5 %collective-permute-start.4 = (f32[4,16,128]{2,1,0:T(8,128)S(1)}, f32[4,16,128]{2,1,0:T(8,128)S(1)}, u32[]{:S(2)}, u32[]{:S(2)}) collective-permute-start(f32[4,16,128]{2,1,0:T(8,128)S(1)} %pad_maximum_fusion), channel_id=1, source_target_pairs={{0,1},{1,2},{2,3},{4,5},{5,6},{6,7},{8,9},{9,10},{10,11},{12,13},{... | collective-permute-start | bytes 98312 | tf_op jit(solution)/shard_map/ppermute | solution.py:808
  24.9 22.2 %collective-permute-start.5 = (f32[4,16,128]{2,1,0:T(8,128)S(1)}, f32[4,16,128]{2,1,0:T(8,128)S(1)}, u32[]{:S(2)}, u32[]{:S(2)}) collective-permute-start(f32[4,16,128]{2,1,0:T(8,128)S(1)} %pad_maximum_fusion.1), channel_id=1, source_target_pairs={{1,0},{2,1},{3,2},{5,4},{6,5},{7,6},{9,8},{10,9},{11,10},{13,12},{... | collective-permute-start | bytes 98312 | tf_op jit(solution)/shard_map/ppermute | solution.py:808
  47.1 0.6 copy-start.5
  47.1 0.6 copy-start.6
  47.2 1.2 %copy-start = (f32[3,1024,128]{2,1,0:T(8,128)}, f32[3,1024,128]{2,1,0:T(8,128)S(1)}, u32[]{:S(2)}) copy-start(f32[3,1024,128]{2,1,0:T(8,128)S(1)} %collective-permute-done.2) | copy-start | bytes 4718596
  47.2 1.7 %copy-start.1 = (f32[3,1024,128]{2,1,0:T(8,128)}, f32[3,1024,128]{2,1,0:T(8,128)S(1)}, u32[]{:S(2)}) copy-start(f32[3,1024,128]{2,1,0:T(8,128)S(1)} %collective-permute-done.3) | copy-start | bytes 4718596
  58.8 19.6 %all-to-all-start = ((f32[32,8,128]{2,1,0:T(8,128)}), f32[32,8,128]{2,1,0:T(8,128)S(1)}, u32[]{:S(2)}, u32[]{:S(2)}) async-start(f32[32,8,128]{2,1,0:T(8,128)} %get-tuple-element.30), calls=%async_computation | async-start | bytes 262144 | tf_op jit(solution)/shard_map/all_to_all | solution.py:847
  78.3 0.7 copy-start.3
  80.6 15.9 %all-to-all-start.1 = ((f32[32,8,128]{2,1,0:T(8,128)}), f32[32,8,128]{2,1,0:T(8,128)S(1)}, u32[]{:S(2)}, u32[]{:S(2)}) async-start(f32[32,8,128]{2,1,0:T(8,128)} %carries.1), calls=%async_computation.1 | async-start | bytes 262144 | tf_op jit(solution)/shard_map/all_to_all | solution.py:850
  96.5 0.7 copy-start.2

commit v3 on v2

--- a/solution.py
+++ b/solution.py
@@ -163,7 +163,7 @@
             pltpu.SemaphoreType.DMA((2, NCHUNK)),
             pltpu.SemaphoreType.DMA((3, NCHUNK)),
         ],
-        compiler_params=vmem(60),
+        compiler_params=vmem(50),
         cost_estimate=pl.CostEstimate(flops=10**6, bytes_accessed=13 * 2**20, transcendentals=0),
         name="faces",
     )(c, level)
@@ -190,7 +190,9 @@
 def dot3(a, b):
     (a_high, a_low), (b_high, b_low) = a, b
     mm = functools.partial(jnp.dot, preferred_element_type=F32)
-    return mm(a_high, b_high) + (mm(a_low, b_high) + mm(a_high, b_low))
+    both = mm(jnp.concatenate([a_high, a_low], axis=0), b_high)
+    rows = a_high.shape[0]
+    return both[:rows] + (both[rows:] + mm(a_high, b_low))
 
 
 def ends(first, last, length):
@@ -395,7 +397,7 @@
             pltpu.SemaphoreType.DMA((NCHUNK,)),
             pltpu.SemaphoreType.DMA((NCHUNK,)),
         ],
-        compiler_params=vmem(60),
+        compiler_params=vmem(50),
         cost_estimate=pl.CostEstimate(flops=4 * 10**9, bytes_accessed=60 * 2**20, transcendentals=0),
         name="block",
     )(flags, act, c.reshape(block), level.reshape(block), xlo, xhi)
@@ -555,109 +557,66 @@
             pltpu.SemaphoreType.DMA((2, 7)),
             pltpu.SemaphoreType.DMA((2, 2)),
         ],
-        compiler_params=vmem(60),
+        compiler_params=vmem(50),
         cost_estimate=pl.CostEstimate(flops=10**7, bytes_accessed=12 * 2**20, transcendentals=0),
         name="seams",
     )(flags, powers, *lines, xlo, xhi, corner_lo, corner_hi, edgepot.reshape(2, X, YT, LANES), mom, act)
 
 
-def settle_kernel(pot_hbm, u_hbm, dpot_ref, df_ref, pot_out, u_out, pot_s, u_s, p_s, in_sem, out_sem):
+def lines_kernel(u_hbm, df_hbm, thigh_ref, tlow_ref, edge_ref, out_hbm, u_s, df_s, p_s, w_s, v_s, df_sem, in_sem, out_sem):
+    groups = X // MROWS
+    grow = MROWS * ROW
+
     def moves(i):
-        at = pl.ds(i * CHUNK * ROW, CHUNK * ROW)
-        return [
-            (pltpu.make_async_copy(far.at[at], near.at[at], in_sem.at[k, i]),
-             pltpu.make_async_copy(near.at[at], out.at[at], out_sem.at[k, i]))
-            for k, (far, near, out) in enumerate(((pot_hbm, pot_s, pot_out), (u_hbm, u_s, u_out)))
-        ]
-
-    for i in reversed(range(NCHUNK)):
-        for start, _ in moves(i):
-            start.start()
-
+        at = pl.ds(i * MROWS, MROWS)
+        return (pltpu.make_async_copy(u_hbm.at[pl.ds(i * grow, grow)], u_s.at[pl.ds(i * grow, grow)], in_sem.at[i]),
+                pltpu.make_async_copy(v_s.at[at], out_hbm.at[at], out_sem.at[i]))
+
+    bring = pltpu.make_async_copy(df_hbm, df_s, df_sem)
+    bring.start()
+    for i in range(groups):
+        moves(i)[0].start()
+    bring.wait()
     shape = (4, YT, LANES)
 
     def forth(x, carry):
-        carry = RHO * carry + df_ref[:, x]
+        carry = RHO * carry + df_s[:, x]
         p_s[:, x] = carry
         return carry
 
-    lax.fori_loop(0, X, forth, jnp.zeros(shape, F32), unroll=8)
+    lax.fori_loop(0, X, forth, jnp.zeros(shape, F32), unroll=4)
 
     def back(k, carry):
         x = X - 1 - k
-        solved = GAIN * (p_s[:, x] + carry)
-        for n, z in enumerate((0, 1, 6, 7)):
-            at = pl.ds(x * ROW + z, YT, stride=Z)
-            u_s[at, :] = u_s[at, :] + solved[n]
-        return RHO * (carry + df_ref[:, x])
-
-    def chunk(done, carry):
-        i = NCHUNK - 1 - done
-        (pot_in, pot_back), (u_in, u_back) = moves(i)
-        pot_in.wait()
-        for side, z in ((0, 0), (1, 7)):
-            at = pl.ds(i * CHUNK * ROW + z, PART, stride=Z)
-            pot_s[at, :] = pot_s[at, :] + dpot_ref[side, pl.ds(i * PART, PART), :]
-        pot_back.start()
-        u_in.wait()
-        carry = lax.fori_loop(0, CHUNK, lambda k, c: back(done * CHUNK + k, c), carry, unroll=4)
-        u_back.start()
-        return carry
-
-    lax.fori_loop(0, NCHUNK, chunk, jnp.zeros(shape, F32))
-    for i in range(NCHUNK):
-        for _, back_copy in moves(i):
-            back_copy.wait()
-
-
-def settle(pot, u, dpot, df):
-    vm = pl.BlockSpec(memory_space=pltpu.VMEM)
-    any_spec = pl.BlockSpec(memory_space=pltpu.HBM)
-    rows = jax.ShapeDtypeStruct((ROWS, LANES), F32)
-    return pl.pallas_call(
-        settle_kernel,
-        in_specs=[any_spec, any_spec, vm, vm],
-        out_specs=[any_spec, any_spec],
-        out_shape=[rows, rows],
-        scratch_shapes=[
-            pltpu.VMEM((ROWS, LANES), F32),
-            pltpu.VMEM((ROWS, LANES), F32),
-            pltpu.VMEM((4, X, YT, LANES), F32),
-            pltpu.SemaphoreType.DMA((2, NCHUNK)),
-            pltpu.SemaphoreType.DMA((2, NCHUNK)),
-        ],
-        compiler_params=vmem(60),
-        cost_estimate=pl.CostEstimate(flops=10**7, bytes_accessed=10 * 2**20, transcendentals=0),
-        name="settle",
-    )(pot, u.reshape(ROWS, LANES), dpot.reshape(2, FACE, LANES), df)
-
-
-def lines_kernel(u_hbm, thigh_ref, tlow_ref, edge_ref, out_hbm, u_s, w_s, in_sem, out_sem):
-    groups = X // MROWS
-
-    def moves(i):
-        at = pl.ds(i * MROWS, MROWS)
-        return (pltpu.make_async_copy(u_hbm.at[at], u_s.at[at], in_sem.at[i]),
-                pltpu.make_async_copy(u_s.at[at], out_hbm.at[at], out_sem.at[i]))
-
-    for i in range(groups):
-        moves(i)[0].start()
+        f = df_s[:, x]
+        df_s[:, x] = GAIN * (p_s[:, x] + carry)
+        return RHO * (carry + f)
+
+    lax.fori_loop(0, X, back, jnp.zeros(shape, F32), unroll=4)
     edge = edge_ref[...]
 
     def group(i, _):
         come, leave = moves(i)
         come.wait()
-        xs = pl.ds(i * MROWS, MROWS)
+        for n, z in enumerate((0, 1, 6, 7)):
+            at = pl.ds(i * grow + z, MROWS * YT, stride=Z)
+            added = df_s[n, pl.ds(i * MROWS, MROWS)].reshape(MROWS * YT, LANES)
+            u_s[at, :] = u_s[at, :] + added
         table = (thigh_ref[...], tlow_ref[...])
         for b in range(YT // 2):
-            pair = [u_s[xs, 2 * b + k].reshape(MROWS * Z, LANES) for k in range(2)]
+            pair = [
+                jnp.concatenate([
+                    u_s[pl.ds(pl.multiple_of(i * grow + x * ROW + (2 * b + k) * Z, Z), Z), :] for x in range(MROWS)
+                ], axis=0)
+                for k in range(2)
+            ]
             solved = dot3(split(jnp.concatenate(pair, axis=1)), table)
             for k in range(2):
                 w_s[:, 2 * b + k] = solved[:, k * LANES:(k + 1) * LANES].reshape(MROWS, Z, LANES)
 
         def body(x, _):
             for t, part in enumerate(y_carry([w_s[x, t] for t in range(YT)], edge)):
-                u_s[i * MROWS + x, t] = part
+                v_s[i * MROWS + x, t] = part
             return 0
 
         lax.fori_loop(0, MROWS, body, 0, unroll=UNROLL)
@@ -669,27 +628,77 @@
         moves(i)[1].wait()
 
 
-UNROLL = 4
-
-
-def solve_lines(u, tables):
+UNROLL = 16
+
+
+def solve_lines(u, df, tables):
     vm = pl.BlockSpec(memory_space=pltpu.VMEM)
     hbm = pl.BlockSpec(memory_space=pltpu.HBM)
+    block = (X, YT, Z, LANES)
     return pl.pallas_call(
         lines_kernel,
-        in_specs=[hbm] + [vm] * 3,
+        in_specs=[hbm, hbm] + [vm] * 3,
         out_specs=hbm,
-        out_shape=jax.ShapeDtypeStruct((X, YT, Z, LANES), F32),
+        out_shape=jax.ShapeDtypeStruct(block, F32),
         scratch_shapes=[
-            pltpu.VMEM((X, YT, Z, LANES), F32),
+            pltpu.VMEM((ROWS, LANES), F32),
+            pltpu.VMEM((4, X, YT, LANES), F32),
+            pltpu.VMEM((4, X, YT, LANES), F32),
             pltpu.VMEM((MROWS, YT, Z, LANES), F32),
+            pltpu.VMEM(block, F32),
+            pltpu.SemaphoreType.DMA,
             pltpu.SemaphoreType.DMA((X // MROWS,)),
             pltpu.SemaphoreType.DMA((X // MROWS,)),
         ],
-        compiler_params=vmem(60),
+        compiler_params=vmem(50),
         cost_estimate=pl.CostEstimate(flops=2 * 10**9, bytes_accessed=10 * 2**20, transcendentals=0),
         name="lines",
-    )(u, *tables)
+    )(u.reshape(ROWS, LANES), df, *tables)
+
+
+def mend_kernel(pot_hbm, dpot_hbm, out_hbm, pot_s, dpot_s, in_sem, out_sem):
+    def moves(i):
+        at, part = pl.ds(i * CHUNK * ROW, CHUNK * ROW), pl.ds(i * PART, PART)
+        return (pltpu.make_async_copy(pot_hbm.at[at], pot_s.at[at], in_sem.at[0, i]),
+                pltpu.make_async_copy(dpot_hbm.at[:, part], dpot_s.at[:, part], in_sem.at[1, i]),
+                pltpu.make_async_copy(pot_s.at[at], out_hbm.at[at], out_sem.at[i]))
+
+    for i in range(NCHUNK):
+        moves(i)[0].start()
+        moves(i)[1].start()
+
+    def chunk(i, _):
+        pot_in, dpot_in, leave = moves(i)
+        pot_in.wait()
+        dpot_in.wait()
+        for side, z in ((0, 0), (1, 7)):
+            at = pl.ds(i * CHUNK * ROW + z, PART, stride=Z)
+            pot_s[at, :] = pot_s[at, :] + dpot_s[side, pl.ds(i * PART, PART), :]
+        leave.start()
+        return 0
+
+    lax.fori_loop(0, NCHUNK, chunk, 0)
+    for i in range(NCHUNK):
+        moves(i)[2].wait()
+
+
+def mend_potential(pot, dpot):
+    hbm = pl.BlockSpec(memory_space=pltpu.HBM)
+    return pl.pallas_call(
+        mend_kernel,
+        in_specs=[hbm, hbm],
+        out_specs=hbm,
+        out_shape=jax.ShapeDtypeStruct((ROWS, LANES), F32),
+        scratch_shapes=[
+            pltpu.VMEM((ROWS, LANES), F32),
+            pltpu.VMEM((2, FACE, LANES), F32),
+            pltpu.SemaphoreType.DMA((2, NCHUNK)),
+            pltpu.SemaphoreType.DMA((NCHUNK,)),
+        ],
+        compiler_params=vmem(50),
+        cost_estimate=pl.CostEstimate(flops=10**7, bytes_accessed=10 * 2**20, transcendentals=0),
+        name="mend",
+    )(pot, dpot.reshape(2, FACE, LANES))
 
 
 def carries_kernel(count, in_ref, out_ref):
@@ -794,7 +803,7 @@
             pltpu.SemaphoreType.DMA((X // FIN,)),
             pltpu.SemaphoreType.DMA((X // FIN,)),
         ],
-        compiler_params=vmem(60),
+        compiler_params=vmem(50),
         cost_estimate=pl.CostEstimate(flops=10**7, bytes_accessed=10 * 2**20, transcendentals=0),
         name="finish",
     )(powers, got, *tables, v)
@@ -845,10 +854,11 @@
         flags, powers, zlo, zhi, inner, got_zlo, got_zhi, got_xlo, got_xhi, corner_lo, corner_hi, edgepot, mom, act,
     )
     got = lax.all_to_all(send, "xy", split_axis=0, concat_axis=0, tiled=True)
-    potential, u = settle(pot, u, dpot, df)
-    got, u = lax.optimization_barrier((got, u))
-    back = lax.all_to_all(scan_carries(got), "xy", split_axis=0, concat_axis=0, tiled=True)
-    v = solve_lines(u.reshape(X, YT, Z, LANES), tables)
+    v = solve_lines(u, df, tables)
+    got, v = lax.optimization_barrier((got, v))
+    carried, pot = lax.optimization_barrier((scan_carries(got), pot))
+    back = lax.all_to_all(carried, "xy", split_axis=0, concat_axis=0, tiled=True)
+    potential = mend_potential(pot, dpot)
     increment = finish(powers, back, tables, v.reshape(ROWS, LANES))
     return from_tiles(potential), from_tiles(increment)
 

time: 103 us -> 96.5 us (0.937)
  Pallas kernels: 58.1 us -> 47.2 us
  waiting for transfers between devices: 1.66 us -> 10.4 us
  local copies, waits for them, and re-layouts: 3.94 us -> 2.31 us
  starting transfers between devices: 35.6 us -> 34.4 us
  other arithmetic: 1.92 us -> 0.79 us
    pallas_call x2, Pallas kernels: 17 us -> 10 us  [the longest x1 6.29 us: solve_lines(): pl.pallas_call(lines_kernel, in_specs=[hbm, hbm] + [vm] * 3, out_specs=hb...]
    ppermute x6, waiting for transfers between devices: 1.66 us -> 6.4 us  [shift(): return lax.ppermute(value, axis, pairs)]
    all_to_all x1, waiting for transfers between devices: 0.01 us -> 3.96 us  [per_device(): lax.all_to_all(carried, 'xy', split_axis=0, concat_axis=0, tiled=True)]
    pallas_call x1, Pallas kernels: 18.2 us -> 16.7 us  [solve_block(): pl.pallas_call(block_kernel, in_specs=[sm, sm, any_spec, any_spec, vm, vm...]
    all_to_all x1, starting transfers between devices: 11 us -> 9.7 us  [per_device(): got = lax.all_to_all(send, 'xy', split_axis=0, concat_axis=0, tiled=True)]
  transfers between devices with their start and end apart: 8 -> 8, of which waited for: 2 -> 4; matrix products, arithmetic and copies ran while one was open for 3% -> 1% of each run, Pallas kernels for 34% -> 28%
where the time goes in v3:
time: 96.5 us; the launch traced here: 96 us
  Pallas kernels  47.2 us (49%)
  starting transfers between devices  34.4 us (36%)
  waiting for transfers between devices  10.4 us (11%)
  local copies, waits for them, and re-layouts  2.31 us (2%)
    ppermute x6, starting transfers between devices, shift(): return lax.ppermute(value, axis, pairs)  17.4 us
    pallas_call x1, Pallas kernels, solve_block(): pl.pallas_call(block_kernel, in_specs=[sm, sm, any_spec, any_spec, vm, vm...  16.7 us
    all_to_all x1, starting transfers between devices, per_device(): got = lax.all_to_all(send, 'xy', split_axis=0, concat_axis=0, tiled=True)  9.7 us
    pallas_call x1, Pallas kernels, add_seams(): pl.pallas_call(seam_kernel, in_specs=[sm, sm] + [hbm] * 5 + [vm] * 4 + [h...  8.9 us
    all_to_all x1, starting transfers between devices, per_device(): lax.all_to_all(carried, 'xy', split_axis=0, concat_axis=0, tiled=True)  7.39 us
    ppermute x6, waiting for transfers between devices, shift(): return lax.ppermute(value, axis, pairs)  6.4 us
    pallas_call x1, Pallas kernels, solve_lines(): pl.pallas_call(lines_kernel, in_specs=[hbm, hbm] + [vm] * 3, out_specs=hb...  6.29 us
    pallas_call x1, Pallas kernels, make_faces(): pl.pallas_call(faces_kernel, in_specs=[hbm, hbm], out_specs=[hbm, hbm, hb...  5.61 us
  transfers between devices with their start and end apart: 8, of which 4 were waited for; matrix products, arithmetic and copies ran while one was open for 1% of the time, Pallas kernels for 28%

profile of v3, /device:TPU:25, one launch (start us, length us, event | category | flops | bytes accessed | tf_op | source)
XLA Modules:
  0.0 96.0 jit_solution(14380018890811369328)
XLA Ops:
  0.6 5.6 %faces.1 = (f32[3,1024,128]{2,1,0:T(8,128)S(1)}, f32[3,1024,128]{2,1,0:T(8,128)}, f32[2,1024,128]{2,1,0:T(8,128)S(1)}, f32[2,256,128]{2,1,0:T(8,128)S(1)}, f32[2,256,128]{2,1,0:T(8,128)}) custom-call(f32[8192,128]{1,0:T(8,128)} %bitcast.73, s32[8192,128]{1,0:T(8,128)} %bitcast.75), custom_call_target="tpu_custom_call" | custom-call | flops 1000000 | bytes 13631488 | tf_op jit(solution)/shard_map/faces/pallas_call | solution.py:147
  6.2 0.0 copy-start.1
  6.3 3.6 %collective-permute-start.1 = (f32[3,1024,128]{2,1,0:T(8,128)S(1)}, f32[3,1024,128]{2,1,0:T(8,128)}, u32[]{:S(2)}, u32[]{:S(2)}) collective-permute-start(f32[3,1024,128]{2,1,0:T(8,128)S(1)} %get-tuple-element.18), channel_id=1, source_target_pairs={{1,0},{2,1},{3,2},{5,4},{6,5},{7,6},{9,8},{10,9},{11,10},{13,12},{... | collective-permute-start | bytes 4718600 | tf_op jit(solution)/shard_map/ppermute | solution.py:817
  9.8 1.3 %collective-permute-start = (f32[3,1024,128]{2,1,0:T(8,128)}, f32[3,1024,128]{2,1,0:T(8,128)}, u32[]{:S(2)}, u32[]{:S(2)}) collective-permute-start(f32[3,1024,128]{2,1,0:T(8,128)} %get-tuple-element.19), channel_id=1, source_target_pairs={{0,1},{1,2},{2,3},{4,5},{5,6},{6,7},{8,9},{9,10},{10,11},{12,13},{... | collective-permute-start | bytes 4718600 | tf_op jit(solution)/shard_map/ppermute | solution.py:817
  11.1 4.4 %collective-permute-start.2 = (f32[2,256,128]{2,1,0:T(8,128)}, f32[2,256,128]{2,1,0:T(8,128)S(1)}, u32[]{:S(2)}, u32[]{:S(2)}) collective-permute-start(f32[2,256,128]{2,1,0:T(8,128)} %get-tuple-element.21), channel_id=1, source_target_pairs={{0,4},{4,8},{8,12},{12,16},{16,20},{20,24},{24,28},{28,32},{32,36}... | collective-permute-start | bytes 786440 | tf_op jit(solution)/shard_map/ppermute | solution.py:817
  15.5 1.9 %collective-permute-start.3 = (f32[2,256,128]{2,1,0:T(8,128)S(1)}, f32[2,256,128]{2,1,0:T(8,128)S(1)}, u32[]{:S(2)}, u32[]{:S(2)}) collective-permute-start(f32[2,256,128]{2,1,0:T(8,128)S(1)} %get-tuple-element.22), channel_id=1, source_target_pairs={{4,0},{8,4},{12,8},{16,12},{20,16},{24,20},{28,24},{32,28},{36,32}... | collective-permute-start | bytes 786440 | tf_op jit(solution)/shard_map/ppermute | solution.py:817
  17.5 0.7 multiply_bitcast_fusion.act_ref
  18.2 0.1 add_convert_fusion.flag_ref
  18.3 0.9 collective-permute-done.2
  19.2 4.5 %collective-permute-done.3 = f32[2,256,128]{2,1,0:T(8,128)S(1)} collective-permute-done((f32[2,256,128]{2,1,0:T(8,128)S(1)}, f32[2,256,128]{2,1,0:T(8,128)S(1)}, u32[]{:S(2)}, u32[]{:S(2)}) %collective-permute-start.3) | collective-permute-done | bytes 262176 | tf_op jit(solution)/shard_map/ppermute | solution.py:817
  23.7 1.3 %collective-permute-start.4 = (f32[4,16,128]{2,1,0:T(8,128)S(1)}, f32[4,16,128]{2,1,0:T(8,128)S(1)}, u32[]{:S(2)}, u32[]{:S(2)}) collective-permute-start(f32[4,16,128]{2,1,0:T(8,128)S(1)} %pad_maximum_fusion), channel_id=1, source_target_pairs={{0,1},{1,2},{2,3},{4,5},{5,6},{6,7},{8,9},{9,10},{10,11},{12,13},{... | collective-permute-start | bytes 98312 | tf_op jit(solution)/shard_map/ppermute | solution.py:817
  25.0 4.9 %collective-permute-start.5 = (f32[4,16,128]{2,1,0:T(8,128)S(1)}, f32[4,16,128]{2,1,0:T(8,128)S(1)}, u32[]{:S(2)}, u32[]{:S(2)}) collective-permute-start(f32[4,16,128]{2,1,0:T(8,128)S(1)} %pad_maximum_fusion.1), channel_id=1, source_target_pairs={{1,0},{2,1},{3,2},{5,4},{6,5},{7,6},{9,8},{10,9},{11,10},{13,12},{... | collective-permute-start | bytes 98312 | tf_op jit(solution)/shard_map/ppermute | solution.py:817
  29.9 0.0 copy-start.5
  29.9 16.7 %block.1 = (f32[8192,128]{1,0:T(8,128)}, f32[64,16,8,128]{3,2,1,0:T(8,128)}, f32[2,16,8,128]{3,2,1,0:T(8,128)S(1)}, f32[2,1024,128]{2,1,0:T(8,128)S(1)}) custom-call(f32[4]{0:T(128)S(1)} %add_convert_fusion.flag_ref, f32[16]{0:T(128)S(1)} %multiply_bitcast_fusion.act_ref, f32[64,16,8,128]{3,2,1,0:T(8,128)} %bitcast.74, s32[64,16,8,128]{3,2,1,0:T(8,128)} %bitcast.76, ...), custom_call_target="tpu_custom_call" | custom-call | flops 4000000000 | bytes 62914560 | tf_op jit(solution)/shard_map/block/pallas_call | solution.py:379
  46.6 0.0 copy-done.1
  46.6 1.1 %collective-permute-done.4.corner_lo_ref = f32[4,16,128]{2,1,0:T(8,128)S(1)} collective-permute-done((f32[4,16,128]{2,1,0:T(8,128)S(1)}, f32[4,16,128]{2,1,0:T(8,128)S(1)}, u32[]{:S(2)}, u32[]{:S(2)}) %collective-permute-start.4) | collective-permute-done | bytes 32800 | tf_op jit(solution)/shard_map/ppermute | solution.py:817
  47.7 0.0 collective-permute-done.5.corner_hi_ref
  47.7 0.0 collective-permute-done.1
  47.7 0.0 collective-permute-done
  47.7 0.0 copy-done.5
  47.7 0.0 copy-start.2
  47.7 0.0 copy-start.3
  47.7 0.0 copy-start.4
  47.8 8.9 %seams.1 = (f32[4,64,16,128]{3,2,1,0:T(8,128)}, f32[2,64,16,128]{3,2,1,0:T(8,128)S(1)}, f32[32,8,128]{2,1,0:T(8,128)}) custom-call(f32[4]{0:T(128)S(1)} %add_convert_fusion.flag_ref, f32[2,64]{1,0:T(2,128)S(1)} %copy-done.5, f32[3,64,16,128]{3,2,1,0:T(8,128)} %bitcast.61, f32[3,64,16,128]{3,2,1,0:T(8,128)} %bitcast.79, f32[2,64,16,128]{3,2,1,0:T(8,128)S(1)} %bitcast.62, ...), custom_call_target="tpu_custom_call" | custom-call | flops 10000000 | bytes 12582912 | tf_op jit(solution)/shard_map/seams/pallas_call | solution.py:541
  56.7 9.7 %all-to-all-start = ((f32[32,8,128]{2,1,0:T(8,128)}), f32[32,8,128]{2,1,0:T(8,128)S(1)}, u32[]{:S(2)}, u32[]{:S(2)}) async-start(f32[32,8,128]{2,1,0:T(8,128)} %get-tuple-element.25), calls=%async_computation | async-start | bytes 262144 | tf_op jit(solution)/shard_map/all_to_all | solution.py:856
  66.4 0.0 copy-done.2
  66.4 0.0 copy-done.3
  66.4 0.0 copy-done.4
  66.4 0.0 copy-start
  66.4 1.6 %copy-done = f32[4,64,16,128]{3,2,1,0:T(8,128)S(1)} copy-done((f32[4,64,16,128]{3,2,1,0:T(8,128)S(1)}, f32[4,64,16,128]{3,2,1,0:T(8,128)}, u32[]{:S(2)}) %copy-start) | copy-done | bytes 2097176
  68.0 6.3 %lines.1 = f32[64,16,8,128]{3,2,1,0:T(8,128)} custom-call(f32[8192,128]{1,0:T(8,128)} %bitcast.72, f32[4,64,16,128]{3,2,1,0:T(8,128)S(1)} %copy-done, bf16[256,256]{1,0:T(8,128)(2,1)S(1)} %copy-done.3, bf16[256,256]{1,0:T(8,128)(2,1)S(1)} %copy-done.2, f32[8,128]{1,0:T(8,128)S(1)} %copy-done.4), custom_call_target="tpu_custom_call" | custom-call | flops 2000000000 | bytes 10485760 | tf_op jit(solution)/shard_map/lines/pallas_call | solution.py:638
  74.3 0.0 all-to-all-done.in_ref
  74.3 0.0 copy-start.6
  74.3 0.6 copy-done.6
  75.0 1.6 %carries.1 = f32[32,8,128]{2,1,0:T(8,128)} custom-call(f32[32,8,128]{2,1,0:T(8,128)} %copy-done.6), custom_call_target="tpu_custom_call" | custom-call | flops 1000000 | bytes 262144 | tf_op jit(solution)/shard_map/carries/pallas_call | solution.py:725
  76.6 7.4 %all-to-all-start.1 = ((f32[32,8,128]{2,1,0:T(8,128)}), f32[32,8,128]{2,1,0:T(8,128)S(1)}, u32[]{:S(2)}, u32[]{:S(2)}) async-start(f32[32,8,128]{2,1,0:T(8,128)} %carries.1), calls=%async_computation.1 | async-start | bytes 262144 | tf_op jit(solution)/shard_map/all_to_all | solution.py:860
  84.0 3.7 %mend.1 = f32[8192,128]{1,0:T(8,128)} custom-call(f32[8192,128]{1,0:T(8,128)} %get-tuple-element.30.pot_hbm, f32[2,1024,128]{2,1,0:T(8,128)S(1)} %bitcast.63), custom_call_target="tpu_custom_call" | custom-call | flops 10000000 | bytes 10485760 | tf_op jit(solution)/shard_map/mend/pallas_call | solution.py:687
  87.7 4.0 %all-to-all-done.1.got_ref = f32[32,8,128]{2,1,0:T(8,128)S(1)} async-done(((f32[32,8,128]{2,1,0:T(8,128)}), f32[32,8,128]{2,1,0:T(8,128)S(1)}, u32[]{:S(2)}, u32[]{:S(2)}) %all-to-all-start.1) | async-done | bytes 131104 | tf_op jit(solution)/shard_map/all_to_all | solution.py:860
  91.7 4.3 %finish.1 = f32[8192,128]{1,0:T(8,128)} custom-call(f32[2,64]{1,0:T(2,128)S(1)} %copy-done.5, f32[32,8,128]{2,1,0:T(8,128)S(1)} %all-to-all-done.1.got_ref, bf16[256,256]{1,0:T(8,128)(2,1)S(1)} %copy-done.3, bf16[256,256]{1,0:T(8,128)(2,1)S(1)} %copy-done.2, f32[8,128]{1,0:T(8,128)S(1)} %copy-done.4, f32[8192,128]{1,0:T(8,128)} %bitcast.71), custom_call_target="tpu_custom_call" | custom-call | flops 10000000 | bytes 10485760 | tf_op jit(solution)/shard_map/finish/pallas_call | solution.py:795
  (4 shorter events, 0.1 us)
Async XLA Ops:
  6.2 40.4 %copy-start.1 = (f32[3,1024,128]{2,1,0:T(8,128)}, f32[3,1024,128]{2,1,0:T(8,128)S(1)}, u32[]{:S(2)}) copy-start(f32[3,1024,128]{2,1,0:T(8,128)S(1)} %get-tuple-element.18) | copy-start | bytes 4718596
  6.3 41.4 %collective-permute-start.1 = (f32[3,1024,128]{2,1,0:T(8,128)S(1)}, f32[3,1024,128]{2,1,0:T(8,128)}, u32[]{:S(2)}, u32[]{:S(2)}) collective-permute-start(f32[3,1024,128]{2,1,0:T(8,128)S(1)} %get-tuple-element.18), channel_id=1, source_target_pairs={{1,0},{2,1},{3,2},{5,4},{6,5},{7,6},{9,8},{10,9},{11,10},{13,12},{... | collective-permute-start | bytes 4718600 | tf_op jit(solution)/shard_map/ppermute | solution.py:817
  9.8 37.9 %collective-permute-start = (f32[3,1024,128]{2,1,0:T(8,128)}, f32[3,1024,128]{2,1,0:T(8,128)}, u32[]{:S(2)}, u32[]{:S(2)}) collective-permute-start(f32[3,1024,128]{2,1,0:T(8,128)} %get-tuple-element.19), channel_id=1, source_target_pairs={{0,1},{1,2},{2,3},{4,5},{5,6},{6,7},{8,9},{9,10},{10,11},{12,13},{... | collective-permute-start | bytes 4718600 | tf_op jit(solution)/shard_map/ppermute | solution.py:817
  11.1 8.0 %collective-permute-start.2 = (f32[2,256,128]{2,1,0:T(8,128)}, f32[2,256,128]{2,1,0:T(8,128)S(1)}, u32[]{:S(2)}, u32[]{:S(2)}) collective-permute-start(f32[2,256,128]{2,1,0:T(8,128)} %get-tuple-element.21), channel_id=1, source_target_pairs={{0,4},{4,8},{8,12},{12,16},{16,20},{20,24},{24,28},{28,32},{32,36}... | collective-permute-start | bytes 786440 | tf_op jit(solution)/shard_map/ppermute | solution.py:817
  15.5 8.1 %collective-permute-start.3 = (f32[2,256,128]{2,1,0:T(8,128)S(1)}, f32[2,256,128]{2,1,0:T(8,128)S(1)}, u32[]{:S(2)}, u32[]{:S(2)}) collective-permute-start(f32[2,256,128]{2,1,0:T(8,128)S(1)} %get-tuple-element.22), channel_id=1, source_target_pairs={{4,0},{8,4},{12,8},{16,12},{20,16},{24,20},{28,24},{32,28},{36,32}... | collective-permute-start | bytes 786440 | tf_op jit(solution)/shard_map/ppermute | solution.py:817
  23.7 24.0 %collective-permute-start.4 = (f32[4,16,128]{2,1,0:T(8,128)S(1)}, f32[4,16,128]{2,1,0:T(8,128)S(1)}, u32[]{:S(2)}, u32[]{:S(2)}) collective-permute-start(f32[4,16,128]{2,1,0:T(8,128)S(1)} %pad_maximum_fusion), channel_id=1, source_target_pairs={{0,1},{1,2},{2,3},{4,5},{5,6},{6,7},{8,9},{9,10},{10,11},{12,13},{... | collective-permute-start | bytes 98312 | tf_op jit(solution)/shard_map/ppermute | solution.py:817
  25.0 22.7 %collective-permute-start.5 = (f32[4,16,128]{2,1,0:T(8,128)S(1)}, f32[4,16,128]{2,1,0:T(8,128)S(1)}, u32[]{:S(2)}, u32[]{:S(2)}) collective-permute-start(f32[4,16,128]{2,1,0:T(8,128)S(1)} %pad_maximum_fusion.1), channel_id=1, source_target_pairs={{1,0},{2,1},{3,2},{5,4},{6,5},{7,6},{9,8},{10,9},{11,10},{13,12},{... | collective-permute-start | bytes 98312 | tf_op jit(solution)/shard_map/ppermute | solution.py:817
  29.9 17.8 %copy-start.5 = (f32[2,64]{1,0:T(2,128)S(1)}, f32[2,64]{1,0:T(2,128)}, u32[]{:S(2)}) copy-start(f32[2,64]{1,0:T(2,128)} %constant.50.clone.pow_ref) | copy-start | bytes 1540
  47.7 18.7 %copy-start.2 = (bf16[256,256]{1,0:T(8,128)(2,1)S(1)}, bf16[256,256]{1,0:T(8,128)(2,1)}, u32[]{:S(2)}) copy-start(bf16[256,256]{1,0:T(8,128)(2,1)} %constant.48.clone.tlow_ref) | copy-start | bytes 393220
  47.7 18.6 %copy-start.3 = (bf16[256,256]{1,0:T(8,128)(2,1)S(1)}, bf16[256,256]{1,0:T(8,128)(2,1)}, u32[]{:S(2)}) copy-start(bf16[256,256]{1,0:T(8,128)(2,1)} %constant.47.clone.thigh_ref) | copy-start | bytes 393220
  47.7 18.6 %copy-start.4 = (f32[8,128]{1,0:T(8,128)S(1)}, f32[8,128]{1,0:T(8,128)}, u32[]{:S(2)}) copy-start(f32[8,128]{1,0:T(8,128)} %constant.49.clone.edge_ref) | copy-start | bytes 12292
  56.7 17.6 %all-to-all-start = ((f32[32,8,128]{2,1,0:T(8,128)}), f32[32,8,128]{2,1,0:T(8,128)S(1)}, u32[]{:S(2)}, u32[]{:S(2)}) async-start(f32[32,8,128]{2,1,0:T(8,128)} %get-tuple-element.25), calls=%async_computation | async-start | bytes 262144 | tf_op jit(solution)/shard_map/all_to_all | solution.py:856
  66.4 1.6 %copy-start = (f32[4,64,16,128]{3,2,1,0:T(8,128)S(1)}, f32[4,64,16,128]{3,2,1,0:T(8,128)}, u32[]{:S(2)}) copy-start(f32[4,64,16,128]{3,2,1,0:T(8,128)} %get-tuple-element.27.df_hbm) | copy-start | bytes 6291460
  74.3 0.7 copy-start.6
  76.6 15.1 %all-to-all-start.1 = ((f32[32,8,128]{2,1,0:T(8,128)}), f32[32,8,128]{2,1,0:T(8,128)S(1)}, u32[]{:S(2)}, u32[]{:S(2)}) async-start(f32[32,8,128]{2,1,0:T(8,128)} %carries.1), calls=%async_computation.1 | async-start | bytes 262144 | tf_op jit(solution)/shard_map/all_to_all | solution.py:860

commit v4 on v3

--- a/solution.py
+++ b/solution.py
@@ -172,27 +172,36 @@
 def y_tables():
     idx = np.arange(NB)
     table = GAIN * np.exp(-THETA * np.abs(idx[:, None] - idx[None, :]))
-    high = table.astype(jnp.bfloat16)
-    low = (table - high.astype(np.float64)).astype(jnp.bfloat16)
+    parts, rest = [], table
+    for _ in range(3):
+        parts.append(rest.astype(jnp.bfloat16))
+        rest = rest - parts[-1].astype(np.float64)
     fwd = np.exp(-THETA * (idx + 1.0))
     bwd = np.exp(-THETA * (NB - idx.astype(np.float64)))
     edge = np.zeros((8, LANES), np.float32)
     edge[0], edge[1] = fwd[:LANES], fwd[LANES:]
     edge[2], edge[3] = bwd[:LANES], bwd[LANES:]
-    return high, low, edge
+    return np.stack(parts), edge
 
 
 def split(v):
     high = v.astype(BF16)
-    return high, (v - high.astype(F32)).astype(BF16)
-
-
-def dot3(a, b):
-    (a_high, a_low), (b_high, b_low) = a, b
-    mm = functools.partial(jnp.dot, preferred_element_type=F32)
-    both = mm(jnp.concatenate([a_high, a_low], axis=0), b_high)
-    rows = a_high.shape[0]
-    return both[:rows] + (both[rows:] + mm(a_high, b_low))
+    rest = v - high.astype(F32)
+    middle = rest.astype(BF16)
+    return high, middle, (rest - middle.astype(F32)).astype(BF16)
+
+
+def dot6(value, table_ref):
+    terms = split(value)
+    rows = value.shape[0]
+    total = None
+    for k in (2, 1, 0):
+        left = jnp.concatenate(terms[:3 - k], axis=0) if k < 2 else terms[0]
+        product = jnp.dot(left, table_ref[k], preferred_element_type=F32)
+        for i in reversed(range(3 - k)):
+            piece = product[i * rows:(i + 1) * rows]
+            total = piece if total is None else total + piece
+    return total
 
 
 def ends(first, last, length):
@@ -228,7 +237,7 @@
 
 def block_kernel(flag_ref, act_ref, c_hbm, l_hbm, xlo_ref, xhi_ref,
                  pot_hbm, u_hbm, mom_ref, edgepot_ref,
-                 c_s, l_s, pot_s, u_s, st, hr, in_sem, pot_sem, u_sem):
+                 c_s, l_s, pot_s, u_s, st, in_sem, pot_sem, u_sem):
     def copies_in(i):
         at = pl.ds(i * CHUNK, CHUNK)
         return (pltpu.make_async_copy(c_hbm.at[at], c_s.at[pl.ds(i * CHUNK + 3, CHUNK)], in_sem.at[0, i]),
@@ -241,7 +250,7 @@
     tile = (Z, LANES)
     sub, lane = sub_iota(tile), lane_iota(tile)
     top, first, last = sub == Z - 1, lane == 0, lane == LANES - 1
-    WZ, WY, WX, BASE, REST, POT, SWEEP = range(7)
+    WZ, WY, WX, BASE, REST, POT, SWEEP, H1, H2 = range(9)
 
     def up_z(v):
         return pltpu.roll(v, Z - 1, 0)
@@ -258,17 +267,19 @@
     def ptile(e, t):
         return pl.ds(pl.multiple_of(e * ROW + t * Z, Z), Z)
 
-    def advance(e, parity, open_x, inside):
+    def advance(e, load, store):
+        open_x = jnp.where(e <= 3, open_lo, jnp.where(e >= X + 3, open_hi, 1.0))
+        inside = jnp.where(e >= 5, 1.0, 0.0)
         h = half_over_psi(l_s[e, 0])
         up_h, up_c = up_y(h), up_y(c_s[e, 0])
         below = below2 = jnp.zeros(tile, F32)
         held = None
 
-        def second(t, pot1, up_pot, up_next, gx2, wz, wy, below2):
+        def second(t, pot1, up_pot, gx2, wz, wy, up_next, below2):
             gz = wz * (up_z(pot1) - pot1)
             gy = wy * (jnp.where(last, up_next, up_pot) - pot1)
             turned = down_y(gy)
-            st[REST, t] = (gz - down_z(gz)) + (gy - jnp.where(first, below2, turned)) - gx2
+            store(REST, t, (gz - down_z(gz)) + (gy - jnp.where(first, below2, turned)) - gx2)
             return turned
 
         for t in range(YT):
@@ -278,18 +289,16 @@
                 up_h_next, up_c_next = up_y(h_next), up_y(c_s[e, t + 1])
             else:
                 h_next, up_h_next, up_c_next = h, up_h, up_c
-            h1 = hr[1 - parity, t]
+            h1 = load(H1, t)
             wx = recip(h1 + h) * open_x
             fx = wx * (c - c_s[e - 1, t])
-            pot1 = st[BASE, t] - h1 * fx
-            gx2 = st[WX, t] * (pot1 - st[POT, t])
-            rhs = (act_ref[t] * inside) * (hr[parity, t] * (st[REST, t] + gx2))
-            swept = RHO * st[SWEEP, t] + rhs
+            pot1 = load(BASE, t) - h1 * fx
+            gx2 = load(WX, t) * (pot1 - load(POT, t))
+            rhs = (act_ref[t] * inside) * (load(H2, t) * (load(REST, t) + gx2))
+            swept = RHO * load(SWEEP, t) + rhs
             u_s[e, t] = swept
-            st[SWEEP, t] = swept
-            st[POT, t] = pot1
             pot_s[ptile(e, t), :] = pot1
-            wz_old, wy_old = st[WZ, t], st[WY, t]
+            wz_old, wy_old = load(WZ, t), load(WY, t)
             wz = jnp.where(top, 0.0, recip(h + up_z(h)))
             wy = recip(h + jnp.where(last, up_h_next, up_h))
             if t == YT - 1:
@@ -299,21 +308,38 @@
             turned = down_y(fy)
             total = (fz - down_z(fz)) + (fy - jnp.where(first, below, turned)) - fx
             below = turned
-            st[BASE, t] = c * (c * c - 1.0) - h * total
-            st[WZ, t], st[WY, t], st[WX, t] = wz, wy, wx
-            hr[parity, t] = h
+            for kind, value in ((SWEEP, swept), (POT, pot1), (BASE, c * (c * c - 1.0) - h * total),
+                                (WZ, wz), (WY, wy), (WX, wx), (H1, h), (H2, h1)):
+                store(kind, t, value)
             up_pot = up_y(pot1)
             if held is not None:
-                t0, p0, u0, g0, z0, y0 = held
-                below2 = second(t0, p0, u0, up_pot, g0, z0, y0, below2)
+                below2 = second(*held, up_pot, below2)
             held = (t, pot1, up_pot, gx2, wz_old, wy_old)
             h, up_h, up_c = h_next, up_h_next, up_c_next
-        t0, p0, u0, g0, z0, y0 = held
-        second(t0, p0, u0, u0, g0, z0, y0, below2)
+            yield
+        second(*held, held[2], below2)
+        yield
+
+    def two_rows(e):
+        between = {}
+
+        def keep(kind, t, value):
+            between[kind, t] = value
+
+        def put(kind, t, value):
+            st[kind, t] = value
+
+        ahead = advance(e, lambda kind, t: st[kind, t], keep)
+        behind = advance(e + 1, lambda kind, t: between.pop((kind, t)), put)
+        next(ahead)
+        for _ in range(YT):
+            next(ahead)
+            next(behind)
+        next(behind)
 
     open_lo, open_hi = flag_ref[0], flag_ref[1]
     st[...] = jnp.zeros_like(st)
-    hr[...] = jnp.ones_like(hr)
+    st[H1:] = jnp.ones((2, YT, Z, LANES), F32)
     c_s[0] = jnp.zeros((YT, Z, LANES), F32)
     for at, ref in ((1, xlo_ref), (X + 3, xhi_ref)):
         c_s[at:at + 2] = ref[0]
@@ -333,10 +359,7 @@
             for copy in copies_in((j - 1) // pairs):
                 copy.wait()
 
-        for parity in range(2):
-            e = 2 * j + 1 + parity
-            open_x = jnp.where(e <= 3, open_lo, jnp.where(e >= X + 3, open_hi, 1.0))
-            advance(e, parity, open_x, jnp.where(e >= 5, 1.0, 0.0))
+        two_rows(2 * j + 1)
 
         @pl.when(jnp.logical_and(turn, j > pairs))
         def _():
@@ -391,8 +414,7 @@
             pltpu.VMEM((X + 5, YT, Z, LANES), jnp.int32),
             pltpu.VMEM(((X + 5) * ROW, LANES), F32),
             pltpu.VMEM((X + 5, YT, Z, LANES), F32),
-            pltpu.VMEM((7, YT, Z, LANES), F32),
-            pltpu.VMEM((2, YT, Z, LANES), F32),
+            pltpu.VMEM((9, YT, Z, LANES), F32),
             pltpu.SemaphoreType.DMA((2, NCHUNK)),
             pltpu.SemaphoreType.DMA((NCHUNK,)),
             pltpu.SemaphoreType.DMA((NCHUNK,)),
@@ -452,7 +474,7 @@
         for k in range(2):
             @pl.when(side == k)
             def _():
-                for copy in arrivals(k):
+                for copy in arrivals(k)[:4]:
                     copy.wait()
         open_z = flag_ref[2 + side]
         bias = 1.0 - open_z
@@ -468,6 +490,11 @@
             return 0
 
         lax.fori_loop(0, EXT // 6, first, 0)
+        for k in range(2):
+            @pl.when(side == k)
+            def _():
+                for copy in arrivals(k)[4:]:
+                    copy.wait()
 
         def second(i, _):
             at = pl.ds(i * GROUP, GROUP)
@@ -563,7 +590,7 @@
     )(flags, powers, *lines, xlo, xhi, corner_lo, corner_hi, edgepot.reshape(2, X, YT, LANES), mom, act)
 
 
-def lines_kernel(u_hbm, df_hbm, thigh_ref, tlow_ref, edge_ref, out_hbm, u_s, df_s, p_s, w_s, v_s, df_sem, in_sem, out_sem):
+def lines_kernel(u_hbm, df_hbm, table_ref, edge_ref, out_hbm, u_s, df_s, p_s, w_s, v_s, df_sem, in_sem, out_sem):
     groups = X // MROWS
     grow = MROWS * ROW
 
@@ -602,7 +629,6 @@
             at = pl.ds(i * grow + z, MROWS * YT, stride=Z)
             added = df_s[n, pl.ds(i * MROWS, MROWS)].reshape(MROWS * YT, LANES)
             u_s[at, :] = u_s[at, :] + added
-        table = (thigh_ref[...], tlow_ref[...])
         for b in range(YT // 2):
             pair = [
                 jnp.concatenate([
@@ -610,7 +636,7 @@
                 ], axis=0)
                 for k in range(2)
             ]
-            solved = dot3(split(jnp.concatenate(pair, axis=1)), table)
+            solved = dot6(jnp.concatenate(pair, axis=1), table_ref)
             for k in range(2):
                 w_s[:, 2 * b + k] = solved[:, k * LANES:(k + 1) * LANES].reshape(MROWS, Z, LANES)
 
@@ -637,7 +663,7 @@
     block = (X, YT, Z, LANES)
     return pl.pallas_call(
         lines_kernel,
-        in_specs=[hbm, hbm] + [vm] * 3,
+        in_specs=[hbm, hbm] + [vm] * 2,
         out_specs=hbm,
         out_shape=jax.ShapeDtypeStruct(block, F32),
         scratch_shapes=[
@@ -735,7 +761,7 @@
 FIN = 8
 
 
-def final_kernel(pow_ref, got_ref, thigh_ref, tlow_ref, edge_ref, v_hbm, out_hbm, v_s, lr_s, in_sem, out_sem):
+def final_kernel(pow_ref, got_ref, table_ref, edge_ref, v_hbm, out_hbm, v_s, lr_s, in_sem, out_sem):
     def moves(i):
         at = pl.ds(i * FIN * ROW, FIN * ROW)
         return (pltpu.make_async_copy(v_hbm.at[at], v_s.at[at], in_sem.at[i]),
@@ -754,7 +780,7 @@
                 jnp.where(half, even, pltpu.roll(odd, 4, 0)),
                 jnp.where(half, pltpu.roll(even, 4, 0), odd),
             ], axis=0))
-        solved = dot3(split(jnp.concatenate(pair, axis=1)), (thigh_ref[...], tlow_ref[...]))
+        solved = dot6(jnp.concatenate(pair, axis=1), table_ref)
         for side in range(2):
             for k in range(2):
                 lr_s[side, 2 * b + k] = solved[8 * side:8 * side + 8, k * LANES:(k + 1) * LANES]
@@ -794,7 +820,7 @@
     hbm = pl.BlockSpec(memory_space=pltpu.HBM)
     return pl.pallas_call(
         final_kernel,
-        in_specs=[pl.BlockSpec(memory_space=pltpu.SMEM)] + [vm] * 4 + [hbm],
+        in_specs=[pl.BlockSpec(memory_space=pltpu.SMEM)] + [vm] * 3 + [hbm],
         out_specs=hbm,
         out_shape=jax.ShapeDtypeStruct((ROWS, LANES), F32),
         scratch_shapes=[

time: 96.5 us -> 98.1 us (1.017)
  Pallas kernels: 47.2 us -> 48.6 us
    pallas_call x1, Pallas kernels: 6.29 us -> 7.89 us  [solve_lines(): pl.pallas_call(lines_kernel, in_specs=[hbm, hbm] + [vm] * 2, out_specs=hb...]
    unnamed x14 -> x12, local copies, waits for them, and re-layouts: 2.27 us -> 2.26 us
  transfers between devices with their start and end apart: 8 -> 8, of which waited for: 4 -> 4; matrix products, arithmetic and copies ran while one was open for 1% -> 1% of each run, Pallas kernels for 28% -> 29%
where the time goes in v4:
time: 98.1 us; the launch traced here: 97.7 us
  Pallas kernels  48.6 us (50%)
  starting transfers between devices  34.4 us (35%)
  waiting for transfers between devices  10.7 us (11%)
  local copies, waits for them, and re-layouts  2.3 us (2%)
    ppermute x6, starting transfers between devices, shift(): return lax.ppermute(value, axis, pairs)  17.3 us
    pallas_call x1, Pallas kernels, solve_block(): pl.pallas_call(block_kernel, in_specs=[sm, sm, any_spec, any_spec, vm, vm...  16.4 us
    all_to_all x1, starting transfers between devices, per_device(): got = lax.all_to_all(send, 'xy', split_axis=0, concat_axis=0, tiled=True)  9.7 us
    pallas_call x1, Pallas kernels, add_seams(): pl.pallas_call(seam_kernel, in_specs=[sm, sm] + [hbm] * 5 + [vm] * 4 + [h...  8.75 us
    pallas_call x1, Pallas kernels, solve_lines(): pl.pallas_call(lines_kernel, in_specs=[hbm, hbm] + [vm] * 2, out_specs=hb...  7.89 us
    all_to_all x1, starting transfers between devices, per_device(): lax.all_to_all(carried, 'xy', split_axis=0, concat_axis=0, tiled=True)  7.38 us
    ppermute x6, waiting for transfers between devices, shift(): return lax.ppermute(value, axis, pairs)  6.73 us
    pallas_call x1, Pallas kernels, make_faces(): pl.pallas_call(faces_kernel, in_specs=[hbm, hbm], out_specs=[hbm, hbm, hb...  5.62 us
  transfers between devices with their start and end apart: 8, of which 4 were waited for; matrix products, arithmetic and copies ran while one was open for 1% of the time, Pallas kernels for 29%

profile of v4, /device:TPU:25, one launch (start us, length us, event | category | flops | bytes accessed | tf_op | source)
XLA Modules:
  0.0 97.7 jit_solution(6907261322096736634)
XLA Ops:
  0.6 5.6 %faces.1 = (f32[3,1024,128]{2,1,0:T(8,128)S(1)}, f32[3,1024,128]{2,1,0:T(8,128)}, f32[2,1024,128]{2,1,0:T(8,128)S(1)}, f32[2,256,128]{2,1,0:T(8,128)S(1)}, f32[2,256,128]{2,1,0:T(8,128)}) custom-call(f32[8192,128]{1,0:T(8,128)} %bitcast.73, s32[8192,128]{1,0:T(8,128)} %bitcast.75), custom_call_target="tpu_custom_call" | custom-call | flops 1000000 | bytes 13631488 | tf_op jit(solution)/shard_map/faces/pallas_call | solution.py:147
  6.3 0.0 copy-start.2
  6.3 3.6 %collective-permute-start.1 = (f32[3,1024,128]{2,1,0:T(8,128)S(1)}, f32[3,1024,128]{2,1,0:T(8,128)}, u32[]{:S(2)}, u32[]{:S(2)}) collective-permute-start(f32[3,1024,128]{2,1,0:T(8,128)S(1)} %get-tuple-element.18), channel_id=1, source_target_pairs={{1,0},{2,1},{3,2},{5,4},{6,5},{7,6},{9,8},{10,9},{11,10},{13,12},{... | collective-permute-start | bytes 4718600 | tf_op jit(solution)/shard_map/ppermute | solution.py:843
  9.8 1.3 %collective-permute-start = (f32[3,1024,128]{2,1,0:T(8,128)}, f32[3,1024,128]{2,1,0:T(8,128)}, u32[]{:S(2)}, u32[]{:S(2)}) collective-permute-start(f32[3,1024,128]{2,1,0:T(8,128)} %get-tuple-element.19), channel_id=1, source_target_pairs={{0,1},{1,2},{2,3},{4,5},{5,6},{6,7},{8,9},{9,10},{10,11},{12,13},{... | collective-permute-start | bytes 4718600 | tf_op jit(solution)/shard_map/ppermute | solution.py:843
  11.1 4.4 %collective-permute-start.2 = (f32[2,256,128]{2,1,0:T(8,128)}, f32[2,256,128]{2,1,0:T(8,128)S(1)}, u32[]{:S(2)}, u32[]{:S(2)}) collective-permute-start(f32[2,256,128]{2,1,0:T(8,128)} %get-tuple-element.21), channel_id=1, source_target_pairs={{0,4},{4,8},{8,12},{12,16},{16,20},{20,24},{24,28},{28,32},{32,36}... | collective-permute-start | bytes 786440 | tf_op jit(solution)/shard_map/ppermute | solution.py:843
  15.5 1.9 %collective-permute-start.3 = (f32[2,256,128]{2,1,0:T(8,128)S(1)}, f32[2,256,128]{2,1,0:T(8,128)S(1)}, u32[]{:S(2)}, u32[]{:S(2)}) collective-permute-start(f32[2,256,128]{2,1,0:T(8,128)S(1)} %get-tuple-element.22), channel_id=1, source_target_pairs={{4,0},{8,4},{12,8},{16,12},{20,16},{24,20},{28,24},{32,28},{36,32}... | collective-permute-start | bytes 786440 | tf_op jit(solution)/shard_map/ppermute | solution.py:843
  17.5 0.7 multiply_bitcast_fusion.act_ref
  18.2 0.1 add_convert_fusion.flag_ref
  18.3 0.9 collective-permute-done.2
  19.2 4.5 %collective-permute-done.3 = f32[2,256,128]{2,1,0:T(8,128)S(1)} collective-permute-done((f32[2,256,128]{2,1,0:T(8,128)S(1)}, f32[2,256,128]{2,1,0:T(8,128)S(1)}, u32[]{:S(2)}, u32[]{:S(2)}) %collective-permute-start.3) | collective-permute-done | bytes 262176 | tf_op jit(solution)/shard_map/ppermute | solution.py:843
  23.6 1.3 %collective-permute-start.4 = (f32[4,16,128]{2,1,0:T(8,128)S(1)}, f32[4,16,128]{2,1,0:T(8,128)S(1)}, u32[]{:S(2)}, u32[]{:S(2)}) collective-permute-start(f32[4,16,128]{2,1,0:T(8,128)S(1)} %pad_maximum_fusion), channel_id=1, source_target_pairs={{0,1},{1,2},{2,3},{4,5},{5,6},{6,7},{8,9},{9,10},{10,11},{12,13},{... | collective-permute-start | bytes 98312 | tf_op jit(solution)/shard_map/ppermute | solution.py:843
  25.0 4.9 %collective-permute-start.5 = (f32[4,16,128]{2,1,0:T(8,128)S(1)}, f32[4,16,128]{2,1,0:T(8,128)S(1)}, u32[]{:S(2)}, u32[]{:S(2)}) collective-permute-start(f32[4,16,128]{2,1,0:T(8,128)S(1)} %pad_maximum_fusion.1), channel_id=1, source_target_pairs={{1,0},{2,1},{3,2},{5,4},{6,5},{7,6},{9,8},{10,9},{11,10},{13,12},{... | collective-permute-start | bytes 98312 | tf_op jit(solution)/shard_map/ppermute | solution.py:843
  29.9 0.0 copy-start.4
  29.9 16.4 %block.1 = (f32[8192,128]{1,0:T(8,128)}, f32[64,16,8,128]{3,2,1,0:T(8,128)}, f32[2,16,8,128]{3,2,1,0:T(8,128)S(1)}, f32[2,1024,128]{2,1,0:T(8,128)S(1)}) custom-call(f32[4]{0:T(128)S(1)} %add_convert_fusion.flag_ref, f32[16]{0:T(128)S(1)} %multiply_bitcast_fusion.act_ref, f32[64,16,8,128]{3,2,1,0:T(8,128)} %bitcast.74, s32[64,16,8,128]{3,2,1,0:T(8,128)} %bitcast.76, ...), custom_call_target="tpu_custom_call" | custom-call | flops 4000000000 | bytes 62914560 | tf_op jit(solution)/shard_map/block/pallas_call | solution.py:402
  46.3 0.0 copy-done.2
  46.3 1.4 %collective-permute-done.4.corner_lo_ref = f32[4,16,128]{2,1,0:T(8,128)S(1)} collective-permute-done((f32[4,16,128]{2,1,0:T(8,128)S(1)}, f32[4,16,128]{2,1,0:T(8,128)S(1)}, u32[]{:S(2)}, u32[]{:S(2)}) %collective-permute-start.4) | collective-permute-done | bytes 32800 | tf_op jit(solution)/shard_map/ppermute | solution.py:843
  47.7 0.0 collective-permute-done.5.corner_hi_ref
  47.7 0.0 collective-permute-done.1
  47.7 0.0 collective-permute-done
  47.7 0.0 copy-done.4
  47.7 0.0 copy-start.1
  47.7 0.0 copy-start.3
  47.7 8.7 %seams.1 = (f32[4,64,16,128]{3,2,1,0:T(8,128)}, f32[2,64,16,128]{3,2,1,0:T(8,128)S(1)}, f32[32,8,128]{2,1,0:T(8,128)}) custom-call(f32[4]{0:T(128)S(1)} %add_convert_fusion.flag_ref, f32[2,64]{1,0:T(2,128)S(1)} %copy-done.4, f32[3,64,16,128]{3,2,1,0:T(8,128)} %bitcast.61, f32[3,64,16,128]{3,2,1,0:T(8,128)} %bitcast.79, f32[2,64,16,128]{3,2,1,0:T(8,128)S(1)} %bitcast.62, ...), custom_call_target="tpu_custom_call" | custom-call | flops 10000000 | bytes 12582912 | tf_op jit(solution)/shard_map/seams/pallas_call | solution.py:568
  56.5 9.7 %all-to-all-start = ((f32[32,8,128]{2,1,0:T(8,128)}), f32[32,8,128]{2,1,0:T(8,128)S(1)}, u32[]{:S(2)}, u32[]{:S(2)}) async-start(f32[32,8,128]{2,1,0:T(8,128)} %get-tuple-element.25), calls=%async_computation | async-start | bytes 262144 | tf_op jit(solution)/shard_map/all_to_all | solution.py:882
  66.2 0.0 copy-done.1
  66.2 0.0 copy-done.3
  66.2 0.0 copy-start
  66.2 1.6 %copy-done = f32[4,64,16,128]{3,2,1,0:T(8,128)S(1)} copy-done((f32[4,64,16,128]{3,2,1,0:T(8,128)S(1)}, f32[4,64,16,128]{3,2,1,0:T(8,128)}, u32[]{:S(2)}) %copy-start) | copy-done | bytes 2097176
  67.8 7.9 %lines.1 = f32[64,16,8,128]{3,2,1,0:T(8,128)} custom-call(f32[8192,128]{1,0:T(8,128)} %bitcast.72, f32[4,64,16,128]{3,2,1,0:T(8,128)S(1)} %copy-done, bf16[3,256,256]{2,1,0:T(8,128)(2,1)S(1)} %copy-done.1, f32[8,128]{1,0:T(8,128)S(1)} %copy-done.3), custom_call_target="tpu_custom_call" | custom-call | flops 2000000000 | bytes 10485760 | tf_op jit(solution)/shard_map/lines/pallas_call | solution.py:664
  75.7 0.0 all-to-all-done.in_ref
  75.7 0.0 copy-start.5
  75.7 0.6 copy-done.5
  76.4 1.7 %carries.1 = f32[32,8,128]{2,1,0:T(8,128)} custom-call(f32[32,8,128]{2,1,0:T(8,128)} %copy-done.5), custom_call_target="tpu_custom_call" | custom-call | flops 1000000 | bytes 262144 | tf_op jit(solution)/shard_map/carries/pallas_call | solution.py:751
  78.0 7.4 %all-to-all-start.1 = ((f32[32,8,128]{2,1,0:T(8,128)}), f32[32,8,128]{2,1,0:T(8,128)S(1)}, u32[]{:S(2)}, u32[]{:S(2)}) async-start(f32[32,8,128]{2,1,0:T(8,128)} %carries.1), calls=%async_computation.1 | async-start | bytes 262144 | tf_op jit(solution)/shard_map/all_to_all | solution.py:886
  85.4 3.7 %mend.1 = f32[8192,128]{1,0:T(8,128)} custom-call(f32[8192,128]{1,0:T(8,128)} %get-tuple-element.30.pot_hbm, f32[2,1024,128]{2,1,0:T(8,128)S(1)} %bitcast.63), custom_call_target="tpu_custom_call" | custom-call | flops 10000000 | bytes 10485760 | tf_op jit(solution)/shard_map/mend/pallas_call | solution.py:713
  89.2 4.0 %all-to-all-done.1.got_ref = f32[32,8,128]{2,1,0:T(8,128)S(1)} async-done(((f32[32,8,128]{2,1,0:T(8,128)}), f32[32,8,128]{2,1,0:T(8,128)S(1)}, u32[]{:S(2)}, u32[]{:S(2)}) %all-to-all-start.1) | async-done | bytes 131104 | tf_op jit(solution)/shard_map/all_to_all | solution.py:886
  93.1 4.5 %finish.1 = f32[8192,128]{1,0:T(8,128)} custom-call(f32[2,64]{1,0:T(2,128)S(1)} %copy-done.4, f32[32,8,128]{2,1,0:T(8,128)S(1)} %all-to-all-done.1.got_ref, bf16[3,256,256]{2,1,0:T(8,128)(2,1)S(1)} %copy-done.1, f32[8,128]{1,0:T(8,128)S(1)} %copy-done.3, f32[8192,128]{1,0:T(8,128)} %bitcast.71), custom_call_target="tpu_custom_call" | custom-call | flops 10000000 | bytes 10485760 | tf_op jit(solution)/shard_map/finish/pallas_call | solution.py:821
  (4 shorter events, 0.1 us)
Async XLA Ops:
  6.3 40.0 %copy-start.2 = (f32[3,1024,128]{2,1,0:T(8,128)}, f32[3,1024,128]{2,1,0:T(8,128)S(1)}, u32[]{:S(2)}) copy-start(f32[3,1024,128]{2,1,0:T(8,128)S(1)} %get-tuple-element.18) | copy-start | bytes 4718596
  6.3 41.4 %collective-permute-start.1 = (f32[3,1024,128]{2,1,0:T(8,128)S(1)}, f32[3,1024,128]{2,1,0:T(8,128)}, u32[]{:S(2)}, u32[]{:S(2)}) collective-permute-start(f32[3,1024,128]{2,1,0:T(8,128)S(1)} %get-tuple-element.18), channel_id=1, source_target_pairs={{1,0},{2,1},{3,2},{5,4},{6,5},{7,6},{9,8},{10,9},{11,10},{13,12},{... | collective-permute-start | bytes 4718600 | tf_op jit(solution)/shard_map/ppermute | solution.py:843
  9.8 37.9 %collective-permute-start = (f32[3,1024,128]{2,1,0:T(8,128)}, f32[3,1024,128]{2,1,0:T(8,128)}, u32[]{:S(2)}, u32[]{:S(2)}) collective-permute-start(f32[3,1024,128]{2,1,0:T(8,128)} %get-tuple-element.19), channel_id=1, source_target_pairs={{0,1},{1,2},{2,3},{4,5},{5,6},{6,7},{8,9},{9,10},{10,11},{12,13},{... | collective-permute-start | bytes 4718600 | tf_op jit(solution)/shard_map/ppermute | solution.py:843
  11.1 8.0 %collective-permute-start.2 = (f32[2,256,128]{2,1,0:T(8,128)}, f32[2,256,128]{2,1,0:T(8,128)S(1)}, u32[]{:S(2)}, u32[]{:S(2)}) collective-permute-start(f32[2,256,128]{2,1,0:T(8,128)} %get-tuple-element.21), channel_id=1, source_target_pairs={{0,4},{4,8},{8,12},{12,16},{16,20},{20,24},{24,28},{28,32},{32,36}... | collective-permute-start | bytes 786440 | tf_op jit(solution)/shard_map/ppermute | solution.py:843
  15.5 8.1 %collective-permute-start.3 = (f32[2,256,128]{2,1,0:T(8,128)S(1)}, f32[2,256,128]{2,1,0:T(8,128)S(1)}, u32[]{:S(2)}, u32[]{:S(2)}) collective-permute-start(f32[2,256,128]{2,1,0:T(8,128)S(1)} %get-tuple-element.22), channel_id=1, source_target_pairs={{4,0},{8,4},{12,8},{16,12},{20,16},{24,20},{28,24},{32,28},{36,32}... | collective-permute-start | bytes 786440 | tf_op jit(solution)/shard_map/ppermute | solution.py:843
  23.6 24.0 %collective-permute-start.4 = (f32[4,16,128]{2,1,0:T(8,128)S(1)}, f32[4,16,128]{2,1,0:T(8,128)S(1)}, u32[]{:S(2)}, u32[]{:S(2)}) collective-permute-start(f32[4,16,128]{2,1,0:T(8,128)S(1)} %pad_maximum_fusion), channel_id=1, source_target_pairs={{0,1},{1,2},{2,3},{4,5},{5,6},{6,7},{8,9},{9,10},{10,11},{12,13},{... | collective-permute-start | bytes 98312 | tf_op jit(solution)/shard_map/ppermute | solution.py:843
  25.0 22.7 %collective-permute-start.5 = (f32[4,16,128]{2,1,0:T(8,128)S(1)}, f32[4,16,128]{2,1,0:T(8,128)S(1)}, u32[]{:S(2)}, u32[]{:S(2)}) collective-permute-start(f32[4,16,128]{2,1,0:T(8,128)S(1)} %pad_maximum_fusion.1), channel_id=1, source_target_pairs={{1,0},{2,1},{3,2},{5,4},{6,5},{7,6},{9,8},{10,9},{11,10},{13,12},{... | collective-permute-start | bytes 98312 | tf_op jit(solution)/shard_map/ppermute | solution.py:843
  29.9 17.8 %copy-start.4 = (f32[2,64]{1,0:T(2,128)S(1)}, f32[2,64]{1,0:T(2,128)}, u32[]{:S(2)}) copy-start(f32[2,64]{1,0:T(2,128)} %constant.47.clone.pow_ref) | copy-start | bytes 1540
  47.7 18.5 %copy-start.1 = (bf16[3,256,256]{2,1,0:T(8,128)(2,1)S(1)}, bf16[3,256,256]{2,1,0:T(8,128)(2,1)}, u32[]{:S(2)}) copy-start(bf16[3,256,256]{2,1,0:T(8,128)(2,1)} %constant.45.clone.table_ref) | copy-start | bytes 1179652
  47.7 18.5 %copy-start.3 = (f32[8,128]{1,0:T(8,128)S(1)}, f32[8,128]{1,0:T(8,128)}, u32[]{:S(2)}) copy-start(f32[8,128]{1,0:T(8,128)} %constant.46.clone.edge_ref) | copy-start | bytes 12292
  56.5 19.2 %all-to-all-start = ((f32[32,8,128]{2,1,0:T(8,128)}), f32[32,8,128]{2,1,0:T(8,128)S(1)}, u32[]{:S(2)}, u32[]{:S(2)}) async-start(f32[32,8,128]{2,1,0:T(8,128)} %get-tuple-element.25), calls=%async_computation | async-start | bytes 262144 | tf_op jit(solution)/shard_map/all_to_all | solution.py:882
  66.2 1.6 %copy-start = (f32[4,64,16,128]{3,2,1,0:T(8,128)S(1)}, f32[4,64,16,128]{3,2,1,0:T(8,128)}, u32[]{:S(2)}) copy-start(f32[4,64,16,128]{3,2,1,0:T(8,128)} %get-tuple-element.27.df_hbm) | copy-start | bytes 6291460
  75.7 0.7 copy-start.5
  78.0 15.1 %all-to-all-start.1 = ((f32[32,8,128]{2,1,0:T(8,128)}), f32[32,8,128]{2,1,0:T(8,128)S(1)}, u32[]{:S(2)}, u32[]{:S(2)}) async-start(f32[32,8,128]{2,1,0:T(8,128)} %carries.1), calls=%async_computation.1 | async-start | bytes 262144 | tf_op jit(solution)/shard_map/all_to_all | solution.py:886

commit v5 on v4

--- a/solution.py
+++ b/solution.py
@@ -880,11 +880,11 @@
         flags, powers, zlo, zhi, inner, got_zlo, got_zhi, got_xlo, got_xhi, corner_lo, corner_hi, edgepot, mom, act,
     )
     got = lax.all_to_all(send, "xy", split_axis=0, concat_axis=0, tiled=True)
+    potential = mend_potential(pot, dpot)
+    got, potential = lax.optimization_barrier((got, potential))
+    carried, u = lax.optimization_barrier((scan_carries(got), u))
+    back = lax.all_to_all(carried, "xy", split_axis=0, concat_axis=0, tiled=True)
     v = solve_lines(u, df, tables)
-    got, v = lax.optimization_barrier((got, v))
-    carried, pot = lax.optimization_barrier((scan_carries(got), pot))
-    back = lax.all_to_all(carried, "xy", split_axis=0, concat_axis=0, tiled=True)
-    potential = mend_potential(pot, dpot)
     increment = finish(powers, back, tables, v.reshape(ROWS, LANES))
     return from_tiles(potential), from_tiles(increment)
 

time: 98.1 us -> 95.1 us (0.969)
  starting transfers between devices: 34.4 us -> 31.8 us
  waiting for transfers between devices: 10.7 us -> 9.33 us
    all_to_all x1, waiting for transfers between devices: 3.96 us -> 0.01 us  [per_device(): lax.all_to_all(carried, 'xy', split_axis=0, concat_axis=0, tiled=True)]
    all_to_all x1, waiting for transfers between devices: 0.01 us -> 2.61 us  [per_device(): got = lax.all_to_all(send, 'xy', split_axis=0, concat_axis=0, tiled=True)]
    all_to_all x1, starting transfers between devices: 7.38 us -> 4.79 us  [per_device(): lax.all_to_all(carried, 'xy', split_axis=0, concat_axis=0, tiled=True)]
    unnamed x12 -> x16, local copies, waits for them, and re-layouts: 2.26 us -> 2.86 us
  transfers between devices with their start and end apart: 8 -> 8, of which waited for: 4 -> 4; matrix products, arithmetic and copies ran while one was open for 1% -> 1% of each run, Pallas kernels for 29% -> 30%
where the time goes in v5:
time: 95.1 us; the launch traced here: 94.4 us
  Pallas kernels  48.8 us (51%)
  starting transfers between devices  31.8 us (33%)
  waiting for transfers between devices  9.33 us (10%)
  local copies, waits for them, and re-layouts  2.9 us (3%)
    ppermute x6, starting transfers between devices, shift(): return lax.ppermute(value, axis, pairs)  17.3 us
    pallas_call x1, Pallas kernels, solve_block(): pl.pallas_call(block_kernel, in_specs=[sm, sm, any_spec, any_spec, vm, vm...  16.4 us
    all_to_all x1, starting transfers between devices, per_device(): got = lax.all_to_all(send, 'xy', split_axis=0, concat_axis=0, tiled=True)  9.69 us
    pallas_call x1, Pallas kernels, add_seams(): pl.pallas_call(seam_kernel, in_specs=[sm, sm] + [hbm] * 5 + [vm] * 4 + [h...  8.76 us
    pallas_call x1, Pallas kernels, solve_lines(): pl.pallas_call(lines_kernel, in_specs=[hbm, hbm] + [vm] * 2, out_specs=hb...  7.95 us
    ppermute x6, waiting for transfers between devices, shift(): return lax.ppermute(value, axis, pairs)  6.72 us
    pallas_call x1, Pallas kernels, make_faces(): pl.pallas_call(faces_kernel, in_specs=[hbm, hbm], out_specs=[hbm, hbm, hb...  5.61 us
    all_to_all x1, starting transfers between devices, per_device(): lax.all_to_all(carried, 'xy', split_axis=0, concat_axis=0, tiled=True)  4.79 us
  transfers between devices with their start and end apart: 8, of which 4 were waited for; matrix products, arithmetic and copies ran while one was open for 1% of the time, Pallas kernels for 30%

profile of v5, /device:TPU:25, one launch (start us, length us, event | category | flops | bytes accessed | tf_op | source)
XLA Modules:
  0.0 94.4 jit_solution(7514944687844203365)
XLA Ops:
  0.6 5.6 %faces.1 = (f32[3,1024,128]{2,1,0:T(8,128)S(1)}, f32[3,1024,128]{2,1,0:T(8,128)}, f32[2,1024,128]{2,1,0:T(8,128)S(1)}, f32[2,256,128]{2,1,0:T(8,128)S(1)}, f32[2,256,128]{2,1,0:T(8,128)}) custom-call(f32[8192,128]{1,0:T(8,128)} %bitcast.73, s32[8192,128]{1,0:T(8,128)} %bitcast.75), custom_call_target="tpu_custom_call" | custom-call | flops 1000000 | bytes 13631488 | tf_op jit(solution)/shard_map/faces/pallas_call | solution.py:147
  6.2 0.0 copy-start.2
  6.3 3.5 %collective-permute-start.1 = (f32[3,1024,128]{2,1,0:T(8,128)S(1)}, f32[3,1024,128]{2,1,0:T(8,128)}, u32[]{:S(2)}, u32[]{:S(2)}) collective-permute-start(f32[3,1024,128]{2,1,0:T(8,128)S(1)} %get-tuple-element.18), channel_id=1, source_target_pairs={{1,0},{2,1},{3,2},{5,4},{6,5},{7,6},{9,8},{10,9},{11,10},{13,12},{... | collective-permute-start | bytes 4718600 | tf_op jit(solution)/shard_map/ppermute | solution.py:843
  9.8 1.3 %collective-permute-start = (f32[3,1024,128]{2,1,0:T(8,128)}, f32[3,1024,128]{2,1,0:T(8,128)}, u32[]{:S(2)}, u32[]{:S(2)}) collective-permute-start(f32[3,1024,128]{2,1,0:T(8,128)} %get-tuple-element.19), channel_id=1, source_target_pairs={{0,1},{1,2},{2,3},{4,5},{5,6},{6,7},{8,9},{9,10},{10,11},{12,13},{... | collective-permute-start | bytes 4718600 | tf_op jit(solution)/shard_map/ppermute | solution.py:843
  11.1 4.4 %collective-permute-start.2 = (f32[2,256,128]{2,1,0:T(8,128)}, f32[2,256,128]{2,1,0:T(8,128)S(1)}, u32[]{:S(2)}, u32[]{:S(2)}) collective-permute-start(f32[2,256,128]{2,1,0:T(8,128)} %get-tuple-element.21), channel_id=1, source_target_pairs={{0,4},{4,8},{8,12},{12,16},{16,20},{20,24},{24,28},{28,32},{32,36}... | collective-permute-start | bytes 786440 | tf_op jit(solution)/shard_map/ppermute | solution.py:843
  15.5 1.9 %collective-permute-start.3 = (f32[2,256,128]{2,1,0:T(8,128)S(1)}, f32[2,256,128]{2,1,0:T(8,128)S(1)}, u32[]{:S(2)}, u32[]{:S(2)}) collective-permute-start(f32[2,256,128]{2,1,0:T(8,128)S(1)} %get-tuple-element.22), channel_id=1, source_target_pairs={{4,0},{8,4},{12,8},{16,12},{20,16},{24,20},{28,24},{32,28},{36,32}... | collective-permute-start | bytes 786440 | tf_op jit(solution)/shard_map/ppermute | solution.py:843
  17.4 0.7 multiply_bitcast_fusion.act_ref
  18.1 0.1 add_convert_fusion.flag_ref
  18.2 0.9 collective-permute-done.2
  19.1 4.5 %collective-permute-done.3 = f32[2,256,128]{2,1,0:T(8,128)S(1)} collective-permute-done((f32[2,256,128]{2,1,0:T(8,128)S(1)}, f32[2,256,128]{2,1,0:T(8,128)S(1)}, u32[]{:S(2)}, u32[]{:S(2)}) %collective-permute-start.3) | collective-permute-done | bytes 262176 | tf_op jit(solution)/shard_map/ppermute | solution.py:843
  23.6 1.3 %collective-permute-start.4 = (f32[4,16,128]{2,1,0:T(8,128)S(1)}, f32[4,16,128]{2,1,0:T(8,128)S(1)}, u32[]{:S(2)}, u32[]{:S(2)}) collective-permute-start(f32[4,16,128]{2,1,0:T(8,128)S(1)} %pad_maximum_fusion), channel_id=1, source_target_pairs={{0,1},{1,2},{2,3},{4,5},{5,6},{6,7},{8,9},{9,10},{10,11},{12,13},{... | collective-permute-start | bytes 98312 | tf_op jit(solution)/shard_map/ppermute | solution.py:843
  24.9 4.9 %collective-permute-start.5 = (f32[4,16,128]{2,1,0:T(8,128)S(1)}, f32[4,16,128]{2,1,0:T(8,128)S(1)}, u32[]{:S(2)}, u32[]{:S(2)}) collective-permute-start(f32[4,16,128]{2,1,0:T(8,128)S(1)} %pad_maximum_fusion.1), channel_id=1, source_target_pairs={{1,0},{2,1},{3,2},{5,4},{6,5},{7,6},{9,8},{10,9},{11,10},{13,12},{... | collective-permute-start | bytes 98312 | tf_op jit(solution)/shard_map/ppermute | solution.py:843
  29.8 0.0 copy-start.6
  29.8 16.4 %block.1 = (f32[8192,128]{1,0:T(8,128)}, f32[64,16,8,128]{3,2,1,0:T(8,128)}, f32[2,16,8,128]{3,2,1,0:T(8,128)S(1)}, f32[2,1024,128]{2,1,0:T(8,128)S(1)}) custom-call(f32[4]{0:T(128)S(1)} %add_convert_fusion.flag_ref, f32[16]{0:T(128)S(1)} %multiply_bitcast_fusion.act_ref, f32[64,16,8,128]{3,2,1,0:T(8,128)} %bitcast.74, s32[64,16,8,128]{3,2,1,0:T(8,128)} %bitcast.76, ...), custom_call_target="tpu_custom_call" | custom-call | flops 4000000000 | bytes 62914560 | tf_op jit(solution)/shard_map/block/pallas_call | solution.py:402
  46.2 0.0 copy-done.2
  46.2 1.4 %collective-permute-done.4.corner_lo_ref = f32[4,16,128]{2,1,0:T(8,128)S(1)} collective-permute-done((f32[4,16,128]{2,1,0:T(8,128)S(1)}, f32[4,16,128]{2,1,0:T(8,128)S(1)}, u32[]{:S(2)}, u32[]{:S(2)}) %collective-permute-start.4) | collective-permute-done | bytes 32800 | tf_op jit(solution)/shard_map/ppermute | solution.py:843
  47.6 0.0 collective-permute-done.5.corner_hi_ref
  47.6 0.0 collective-permute-done.1
  47.6 0.0 collective-permute-done
  47.6 0.0 copy-done.6
  47.6 8.8 %seams.1 = (f32[4,64,16,128]{3,2,1,0:T(8,128)}, f32[2,64,16,128]{3,2,1,0:T(8,128)S(1)}, f32[32,8,128]{2,1,0:T(8,128)}) custom-call(f32[4]{0:T(128)S(1)} %add_convert_fusion.flag_ref, f32[2,64]{1,0:T(2,128)S(1)} %copy-done.6, f32[3,64,16,128]{3,2,1,0:T(8,128)} %bitcast.61, f32[3,64,16,128]{3,2,1,0:T(8,128)} %bitcast.79, f32[2,64,16,128]{3,2,1,0:T(8,128)S(1)} %bitcast.62, ...), custom_call_target="tpu_custom_call" | custom-call | flops 10000000 | bytes 12582912 | tf_op jit(solution)/shard_map/seams/pallas_call | solution.py:568
  56.4 0.0 copy-start.3
  56.4 1.0 %copy-done.3 = f32[2,64,16,128]{3,2,1,0:T(8,128)} copy-done((f32[2,64,16,128]{3,2,1,0:T(8,128)}, f32[2,64,16,128]{3,2,1,0:T(8,128)S(1)}, u32[]{:S(2)}) %copy-start.3) | copy-done | bytes 1048600
  57.4 9.7 %all-to-all-start = ((f32[32,8,128]{2,1,0:T(8,128)}), f32[32,8,128]{2,1,0:T(8,128)S(1)}, u32[]{:S(2)}, u32[]{:S(2)}) async-start(f32[32,8,128]{2,1,0:T(8,128)} %get-tuple-element.25), calls=%async_computation | async-start | bytes 262144 | tf_op jit(solution)/shard_map/all_to_all | solution.py:882
  67.1 0.0 copy-start.4
  67.1 1.2 %copy-done.4 = f32[2,64,16,128]{3,2,1,0:T(8,128)S(1)} copy-done((f32[2,64,16,128]{3,2,1,0:T(8,128)S(1)}, f32[2,64,16,128]{3,2,1,0:T(8,128)}, u32[]{:S(2)}) %copy-start.4) | copy-done | bytes 1048600
  68.3 0.0 copy-start
  68.3 0.0 copy-start.1
  68.3 0.0 copy-start.5
  68.3 3.9 %mend.1 = f32[8192,128]{1,0:T(8,128)} custom-call(f32[8192,128]{1,0:T(8,128)} %get-tuple-element.26.pot_hbm, f32[2,1024,128]{2,1,0:T(8,128)S(1)} %bitcast.64), custom_call_target="tpu_custom_call" | custom-call | flops 10000000 | bytes 10485760 | tf_op jit(solution)/shard_map/mend/pallas_call | solution.py:713
  72.2 2.6 %all-to-all-done.in_ref = f32[32,8,128]{2,1,0:T(8,128)S(1)} async-done(((f32[32,8,128]{2,1,0:T(8,128)}), f32[32,8,128]{2,1,0:T(8,128)S(1)}, u32[]{:S(2)}, u32[]{:S(2)}) %all-to-all-start) | async-done | bytes 131104 | tf_op jit(solution)/shard_map/all_to_all | solution.py:882
  74.8 0.0 copy-start.7
  74.8 0.7 copy-done.7
  75.4 1.6 %carries.1 = f32[32,8,128]{2,1,0:T(8,128)} custom-call(f32[32,8,128]{2,1,0:T(8,128)} %copy-done.7), custom_call_target="tpu_custom_call" | custom-call | flops 1000000 | bytes 262144 | tf_op jit(solution)/shard_map/carries/pallas_call | solution.py:751
  77.1 4.8 %all-to-all-start.1 = ((f32[32,8,128]{2,1,0:T(8,128)}), f32[32,8,128]{2,1,0:T(8,128)S(1)}, u32[]{:S(2)}, u32[]{:S(2)}) async-start(f32[32,8,128]{2,1,0:T(8,128)} %carries.1), calls=%async_computation.1 | async-start | bytes 262144 | tf_op jit(solution)/shard_map/all_to_all | solution.py:886
  81.9 0.0 copy-done
  81.9 0.0 copy-done.1
  81.9 0.0 copy-done.5
  81.9 8.0 %lines.1 = f32[64,16,8,128]{3,2,1,0:T(8,128)} custom-call(f32[8192,128]{1,0:T(8,128)} %bitcast.72, f32[4,64,16,128]{3,2,1,0:T(8,128)S(1)} %copy-done, bf16[3,256,256]{2,1,0:T(8,128)(2,1)S(1)} %copy-done.1, f32[8,128]{1,0:T(8,128)S(1)} %copy-done.5), custom_call_target="tpu_custom_call" | custom-call | flops 2000000000 | bytes 10485760 | tf_op jit(solution)/shard_map/lines/pallas_call | solution.py:664
  89.9 0.0 all-to-all-done.1.got_ref
  89.9 4.6 %finish.1 = f32[8192,128]{1,0:T(8,128)} custom-call(f32[2,64]{1,0:T(2,128)S(1)} %copy-done.6, f32[32,8,128]{2,1,0:T(8,128)S(1)} %all-to-all-done.1.got_ref, bf16[3,256,256]{2,1,0:T(8,128)(2,1)S(1)} %copy-done.1, f32[8,128]{1,0:T(8,128)S(1)} %copy-done.5, f32[8192,128]{1,0:T(8,128)} %bitcast.71), custom_call_target="tpu_custom_call" | custom-call | flops 10000000 | bytes 10485760 | tf_op jit(solution)/shard_map/finish/pallas_call | solution.py:821
  (4 shorter events, 0.1 us)
Async XLA Ops:
  6.2 40.0 %copy-start.2 = (f32[3,1024,128]{2,1,0:T(8,128)}, f32[3,1024,128]{2,1,0:T(8,128)S(1)}, u32[]{:S(2)}) copy-start(f32[3,1024,128]{2,1,0:T(8,128)S(1)} %get-tuple-element.18) | copy-start | bytes 4718596
  6.3 41.4 %collective-permute-start.1 = (f32[3,1024,128]{2,1,0:T(8,128)S(1)}, f32[3,1024,128]{2,1,0:T(8,128)}, u32[]{:S(2)}, u32[]{:S(2)}) collective-permute-start(f32[3,1024,128]{2,1,0:T(8,128)S(1)} %get-tuple-element.18), channel_id=1, source_target_pairs={{1,0},{2,1},{3,2},{5,4},{6,5},{7,6},{9,8},{10,9},{11,10},{13,12},{... | collective-permute-start | bytes 4718600 | tf_op jit(solution)/shard_map/ppermute | solution.py:843
  9.8 37.9 %collective-permute-start = (f32[3,1024,128]{2,1,0:T(8,128)}, f32[3,1024,128]{2,1,0:T(8,128)}, u32[]{:S(2)}, u32[]{:S(2)}) collective-permute-start(f32[3,1024,128]{2,1,0:T(8,128)} %get-tuple-element.19), channel_id=1, source_target_pairs={{0,1},{1,2},{2,3},{4,5},{5,6},{6,7},{8,9},{9,10},{10,11},{12,13},{... | collective-permute-start | bytes 4718600 | tf_op jit(solution)/shard_map/ppermute | solution.py:843
  11.1 8.0 %collective-permute-start.2 = (f32[2,256,128]{2,1,0:T(8,128)}, f32[2,256,128]{2,1,0:T(8,128)S(1)}, u32[]{:S(2)}, u32[]{:S(2)}) collective-permute-start(f32[2,256,128]{2,1,0:T(8,128)} %get-tuple-element.21), channel_id=1, source_target_pairs={{0,4},{4,8},{8,12},{12,16},{16,20},{20,24},{24,28},{28,32},{32,36}... | collective-permute-start | bytes 786440 | tf_op jit(solution)/shard_map/ppermute | solution.py:843
  15.5 8.1 %collective-permute-start.3 = (f32[2,256,128]{2,1,0:T(8,128)S(1)}, f32[2,256,128]{2,1,0:T(8,128)S(1)}, u32[]{:S(2)}, u32[]{:S(2)}) collective-permute-start(f32[2,256,128]{2,1,0:T(8,128)S(1)} %get-tuple-element.22), channel_id=1, source_target_pairs={{4,0},{8,4},{12,8},{16,12},{20,16},{24,20},{28,24},{32,28},{36,32}... | collective-permute-start | bytes 786440 | tf_op jit(solution)/shard_map/ppermute | solution.py:843
  23.6 24.0 %collective-permute-start.4 = (f32[4,16,128]{2,1,0:T(8,128)S(1)}, f32[4,16,128]{2,1,0:T(8,128)S(1)}, u32[]{:S(2)}, u32[]{:S(2)}) collective-permute-start(f32[4,16,128]{2,1,0:T(8,128)S(1)} %pad_maximum_fusion), channel_id=1, source_target_pairs={{0,1},{1,2},{2,3},{4,5},{5,6},{6,7},{8,9},{9,10},{10,11},{12,13},{... | collective-permute-start | bytes 98312 | tf_op jit(solution)/shard_map/ppermute | solution.py:843
  24.9 22.7 %collective-permute-start.5 = (f32[4,16,128]{2,1,0:T(8,128)S(1)}, f32[4,16,128]{2,1,0:T(8,128)S(1)}, u32[]{:S(2)}, u32[]{:S(2)}) collective-permute-start(f32[4,16,128]{2,1,0:T(8,128)S(1)} %pad_maximum_fusion.1), channel_id=1, source_target_pairs={{1,0},{2,1},{3,2},{5,4},{6,5},{7,6},{9,8},{10,9},{11,10},{13,12},{... | collective-permute-start | bytes 98312 | tf_op jit(solution)/shard_map/ppermute | solution.py:843
  29.8 17.8 %copy-start.6 = (f32[2,64]{1,0:T(2,128)S(1)}, f32[2,64]{1,0:T(2,128)}, u32[]{:S(2)}) copy-start(f32[2,64]{1,0:T(2,128)} %constant.47.clone.pow_ref) | copy-start | bytes 1540
  56.4 1.0 %copy-start.3 = (f32[2,64,16,128]{3,2,1,0:T(8,128)}, f32[2,64,16,128]{3,2,1,0:T(8,128)S(1)}, u32[]{:S(2)}) copy-start(f32[2,64,16,128]{3,2,1,0:T(8,128)S(1)} %get-tuple-element.27) | copy-start | bytes 3145732
  57.4 17.4 %all-to-all-start = ((f32[32,8,128]{2,1,0:T(8,128)}), f32[32,8,128]{2,1,0:T(8,128)S(1)}, u32[]{:S(2)}, u32[]{:S(2)}) async-start(f32[32,8,128]{2,1,0:T(8,128)} %get-tuple-element.25), calls=%async_computation | async-start | bytes 262144 | tf_op jit(solution)/shard_map/all_to_all | solution.py:882
  67.1 1.2 %copy-start.4 = (f32[2,64,16,128]{3,2,1,0:T(8,128)S(1)}, f32[2,64,16,128]{3,2,1,0:T(8,128)}, u32[]{:S(2)}) copy-start(f32[2,64,16,128]{3,2,1,0:T(8,128)} %copy-done.3) | copy-start | bytes 3145732
  68.3 13.6 %copy-start = (f32[4,64,16,128]{3,2,1,0:T(8,128)S(1)}, f32[4,64,16,128]{3,2,1,0:T(8,128)}, u32[]{:S(2)}) copy-start(f32[4,64,16,128]{3,2,1,0:T(8,128)} %get-tuple-element.33.df_hbm) | copy-start | bytes 6291460
  68.3 13.6 %copy-start.1 = (bf16[3,256,256]{2,1,0:T(8,128)(2,1)S(1)}, bf16[3,256,256]{2,1,0:T(8,128)(2,1)}, u32[]{:S(2)}) copy-start(bf16[3,256,256]{2,1,0:T(8,128)(2,1)} %constant.45.clone.table_ref) | copy-start | bytes 1179652
  68.3 13.6 %copy-start.5 = (f32[8,128]{1,0:T(8,128)S(1)}, f32[8,128]{1,0:T(8,128)}, u32[]{:S(2)}) copy-start(f32[8,128]{1,0:T(8,128)} %constant.46.clone.edge_ref) | copy-start | bytes 12292
  74.8 0.7 copy-start.7
  77.1 12.8 %all-to-all-start.1 = ((f32[32,8,128]{2,1,0:T(8,128)}), f32[32,8,128]{2,1,0:T(8,128)S(1)}, u32[]{:S(2)}, u32[]{:S(2)}) async-start(f32[32,8,128]{2,1,0:T(8,128)} %carries.1), calls=%async_computation.1 | async-start | bytes 262144 | tf_op jit(solution)/shard_map/all_to_all | solution.py:886
